TPU v7x, 256 devices: a whole 4x4x8 slice. The times are simulated.
256 devices in a mesh: adapter: 8 (over z), tensor: 32 (over y, x, core).
Axes of the slice: x: 4, y: 4, z: 8, core: 2. Of those that a mesh axis runs over, the one named last changes fastest.
Arguments:
- hidden_rows: bfloat16 [6144, 8192], P('adapter', 'tensor'), may hold values from -6 to 6
- query_weight: bfloat16 [8192, 8192], P(None, 'tensor'), may hold values from -0.0625 to 0.0625
- down_panels: bfloat16 [192, 64, 8192], P('adapter', None, 'tensor'), may hold values from -0.0625 to 0.0625
- up_panels: bfloat16 [192, 64, 8192], P('adapter', None, 'tensor'), may hold values from -0.75 to 0.75
- store_index: int32 [192], replicated, may hold values from 0 to 191, each once
- requests: int32 [8, 8], replicated, may hold values from 0 to 191, as said below
- row_slot: int32 [6144], P('adapter'), may hold values from 0 to 7
Outputs:
- query_out: bfloat16 [6144, 8192], P('adapter', 'tensor')
Inputs may be any that keep to these rules, and one draw needn't show every extreme that they name: `requests`: the 8 ids of each group are distinct adapter ids. `store_index`: each adapter id has its own storage slot.
All inputs are finite; a program needn't handle non-finite values.
Results may differ from a plain program's by a relative error of at most 0.003.
Values may be sent and summed in bfloat16 or wider, within the bound.
No kernel may reach another device: no remote copies, remote signals or barrier semaphores. Data moves between devices by JAX's collectives and lax.ppermute only.
A program may use at most 128 MiB of HBM per device.

v0:
```python
import jax
import jax.numpy as jnp
from jax import lax
from jax.sharding import PartitionSpec as P

adapter_scale = 0.5


def per_device(hidden_rows, query_weight, down_panels, up_panels, store_index, requests, row_slot):
    rows_here = hidden_rows.shape[0]
    columns = query_weight.shape[1]
    rank = down_panels.shape[1]
    wanted_count = requests.shape[1]
    row_group = lax.axis_index("adapter")
    base_query = jnp.dot(
        lax.all_gather(hidden_rows, "tensor", axis=1, tiled=True),
        query_weight,
        preferred_element_type=jnp.float32,
    )
    my_requests = lax.dynamic_index_in_dim(requests, row_group, 0, keepdims=False)
    wanted = jnp.take(store_index, my_requests)
    pieces = (
        lax.all_gather(down_panels, "adapter", axis=0, tiled=True),
        lax.all_gather(up_panels, "adapter", axis=0, tiled=True),
    )
    count = pieces[0].shape[0]
    picker = (wanted[:, None] == jnp.arange(count, dtype=jnp.int32)[None, :]).astype(jnp.bfloat16)
    down_add = jnp.einsum("js,srd->jrd", picker, pieces[0], preferred_element_type=jnp.float32)
    up_add = jnp.einsum("js,srd->jrd", picker, pieces[1], preferred_element_type=jnp.float32)
    down_flat = down_add.astype(jnp.bfloat16).reshape(wanted_count * rank, columns)
    flat_up_weight = up_add.astype(jnp.bfloat16).reshape(wanted_count * rank, columns)
    partial_shrink = lax.dot_general(
        hidden_rows, down_flat, (((1,), (1,)), ((), ())), preferred_element_type=jnp.float32
    )
    selection_mask = (
        row_slot[:, None] == jnp.arange(wanted_count, dtype=jnp.int32)[None, :]
    ).astype(jnp.float32)
    own_part = jnp.sum(
        partial_shrink.reshape(rows_here, wanted_count, rank) * selection_mask[:, :, None], axis=1
    )
    local_total = lax.psum(own_part, "tensor")
    scaled_delta = (selection_mask[:, :, None] * local_total[:, None, :] * adapter_scale).reshape(
        rows_here, wanted_count * rank
    )
    scaled_delta = scaled_delta.astype(jnp.bfloat16)
    adapter_delta = jnp.dot(scaled_delta, flat_up_weight, preferred_element_type=jnp.float32)
    return (base_query + adapter_delta).astype(jnp.bfloat16)


def solution(mesh):
    return jax.shard_map(
        per_device,
        mesh=mesh,
        in_specs=(
            P("adapter", "tensor"),
            P(None, "tensor"),
            P("adapter", None, "tensor"),
            P("adapter", None, "tensor"),
            P(),
            P(),
            P("adapter"),
        ),
        out_specs=P("adapter", "tensor"),
        check_vma=False,
    )
```

profile of v0, /device:TPU:1, one launch (start us, length us, event | category | flops | bytes accessed | tf_op | source)
XLA Modules:
  0.0 359.7 jit_solution(4985076121827693434)
XLA Ops:
  6.5 0.0 copy-start
  6.5 0.0 all-gather.6.cloned.1.call-start
  6.5 2.5 copy.11
  9.1 0.0 all-gather.6.cloned.1.call-update
  9.1 0.0 all-gather.8.cloned.1.call-start
  9.1 0.7 all-gather.8.cloned.1.call-update
  9.8 0.0 copy-start.1
  9.9 0.0 all-gather.4.cloned.1.call-start
  9.9 0.7 all-gather.4.cloned.1.call-update
  10.6 0.0 all-reduce.2.cloned.1.call-start
  10.6 0.7 fusion.17
  11.4 0.0 copy-done
  11.4 0.6 gather_fusion
  12.0 0.7 and_select_fusion
  12.7 0.7 fusion.11
  13.4 74.1 %all-gather.6.cloned.1.call-done = bf16[192,64,256]{2,0,1:T(8,128)(2,1)} async-done(((bf16[24,64,256]{2,0,1:T(8,128)(2,1)}), bf16[192,64,256]{2,0,1:T(8,128)(2,1)}) %all-gather.6.cloned.1.call-update) | async-done | bytes 6291472 | tf_op jit(solution)/shard_map/all_gather | solution.py:23
  87.5 3.7 %convolution_convert_fusion = bf16[8,64,256]{2,0,1:T(8,128)(2,1)S(1)} fusion(bf16[192,64,256]{2,0,1:T(8,128)(2,1)} %all-gather.6.cloned.1.call-done, s32[8]{0:T(128)S(1)} %and_select_fusion), kind=kOutput, calls=%fused_computation.9 | convolution fusion | flops 50464256 | bytes 6553632 | tf_op jit(solution)/shard_map/js,srd->jrd/dot_general | solution.py:28
  91.2 0.1 copy.12
  91.3 0.0 copy-done.1
  91.3 0.4 fusion.20
  91.7 0.8 multiply_reduce_fusion
  92.5 0.0 all-reduce.2.cloned.1.call-update
  92.5 69.9 %all-gather.8.cloned.1.call-done = bf16[192,64,256]{2,1,0:T(8,128)(2,1)} async-done(((bf16[24,64,256]{2,1,0:T(8,128)(2,1)}), bf16[192,64,256]{2,1,0:T(8,128)(2,1)}) %all-gather.8.cloned.1.call-update) | async-done | bytes 6291472 | tf_op jit(solution)/shard_map/all_gather | solution.py:24
  162.4 6.2 %fusion.4 = bf16[8,64,256]{2,0,1:T(8,128)(2,1)S(1)} fusion(bf16[192,64,256]{2,1,0:T(8,128)(2,1)} %all-gather.8.cloned.1.call-done, s32[8]{0:T(128)S(1)} %and_select_fusion), kind=kOutput, calls=%fused_computation.8 | convolution fusion | flops 50464256 | bytes 6553632 | tf_op jit(solution)/shard_map/js,srd->jrd/dot_general | solution.py:29
  168.6 70.5 %all-gather.4.cloned.1.call-done = bf16[768,8192]{1,0:T(8,128)(2,1)} async-done(((bf16[768,256]{1,0:T(8,128)(2,1)}), bf16[768,8192]{1,0:T(8,128)(2,1)}) %all-gather.4.cloned.1.call-update) | async-done | bytes 12582928 | tf_op jit(solution)/shard_map/all_gather | solution.py:16
  239.1 7.6 %fusion.19 = f32[768,256]{1,0:T(8,128)S(1)} fusion(bf16[768,8192]{1,0:T(8,128)(2,1)} %all-gather.4.cloned.1.call-done, bf16[8192,256]{1,0:T(8,128)(2,1)} %param.8), kind=kOutput, calls=%fused_computation.27 | convolution fusion | flops 3221225472 | bytes 17563648 | tf_op jit(solution)/shard_map/dot_general | solution.py:15
  246.8 104.3 %all-reduce.2.cloned.1.call-done = f32[768,64]{0,1:T(8,128)} async-done(((f32[768,64]{0,1:T(8,128)}), f32[768,64]{0,1:T(8,128)}) %all-reduce.2.cloned.1.call-update) | async-done | bytes 196624 | tf_op jit(solution)/shard_map/psum | solution.py:41
  351.0 2.1 fusion.3
  (1 shorter events, 0.0 us)
Async XLA Ops:
  6.5 4.8 %copy-start = (s32[192]{0:T(256)S(1)}, s32[192]{0:T(256)}, u32[]{:S(2)}) copy-start(s32[192]{0:T(256)} %param.11) | copy-start | bytes 2308
  6.5 81.0 %all-gather.6.cloned.1.call-start = ((), (), s32[]{:S(2)}) async-start(), calls=%async_computation.1 | async-start | bytes 7077888 | tf_op jit(solution)/shard_map/all_gather | solution.py:23
  9.1 153.3 %all-gather.8.cloned.1.call-start = ((), (), s32[]{:S(2)}) async-start(), calls=%async_computation.3 | async-start | bytes 7077888 | tf_op jit(solution)/shard_map/all_gather | solution.py:24
  9.8 81.5 %copy-start.1 = (bf16[768,256]{1,0:T(8,128)(2,1)S(1)}, bf16[768,256]{1,0:T(8,128)(2,1)}, u32[]{:S(2)}) copy-start(bf16[768,256]{1,0:T(8,128)(2,1)} %param.7) | copy-start | bytes 1179652
  9.9 229.3 %all-gather.4.cloned.1.call-start = ((), (), s32[]{:S(2)}) async-start(), calls=%async_computation | async-start | bytes 12976128 | tf_op jit(solution)/shard_map/all_gather | solution.py:16
  10.6 340.4 %all-reduce.2.cloned.1.call-start = ((), (), s32[]{:S(2)}) async-start(), calls=%async_computation.2 | async-start | bytes 393216 | tf_op jit(solution)/shard_map/psum | solution.py:41
Sparse Core Ops, SparseCore 0:
  9.2 78.2 all-gather.5
  89.3 73.1 all-gather.7
  164.9 74.1 all-gather.3
  242.2 108.7 all-reduce.1
where the time goes:
time: 360 us
  waiting for transfers between devices  320 us (89%)
  matrix products  20 us (6%)
  between operations  13.2 us (4%)
    psum x1, waiting for transfers between devices, per_device(): local_total = lax.psum(own_part, 'tensor')  104 us
    all_gather x1, waiting for transfers between devices, per_device(): lax.all_gather(down_panels, 'adapter', axis=0, tiled=True)  74.1 us
    all_gather x1, waiting for transfers between devices, per_device(): lax.all_gather(hidden_rows, 'tensor', axis=1, tiled=True)  70.5 us
    all_gather x1, waiting for transfers between devices, per_device(): lax.all_gather(up_panels, 'adapter', axis=0, tiled=True)  69.9 us
    dot_general x1, matrix products, per_device(): jnp.dot(lax.all_gather(hidden_rows, 'tensor', axis=1, tiled=True), query_...  7.62 us
  transfers between devices with their start and end apart: 4, of which 4 were waited for; matrix products, arithmetic and copies ran while one was open for 6% of the time, Pallas kernels for 0%

commit v1 on v0

v1 whole, which is shorter than its diff:
```python
import jax
import jax.numpy as jnp
from jax import lax
from jax.experimental import pallas as pl
from jax.experimental.pallas import tpu as pltpu
from jax.sharding import PartitionSpec as P

adapter_scale = 0.5
f32, bf16, i32 = jnp.float32, jnp.bfloat16, jnp.int32
NZ, NY, NX, NC = 8, 4, 4, 2
WANTED = 8
INDEX = NZ * WANTED
SMEM = pl.BlockSpec(memory_space=pltpu.SMEM)
VMEM = pl.BlockSpec(memory_space=pltpu.VMEM)
HBM = pl.BlockSpec(memory_space=pltpu.HBM)
ANY = pl.BlockSpec(memory_space=pl.ANY)
LIMIT = pltpu.CompilerParams(vmem_limit_bytes=48 * 1024 * 1024)


def kernel_call(kernel, out_shape, *operands, scratch=(), specs=None, out=VMEM):
    return pl.pallas_call(
        kernel,
        out_shape=out_shape,
        in_specs=[spec if spec else SMEM if v.dtype == i32 and v.size <= 256 else VMEM for v, spec in zip(operands, specs or [None] * len(operands))],
        out_specs=jax.tree.map(lambda _: out, out_shape),
        scratch_shapes=list(scratch),
        compiler_params=LIMIT,
    )(*operands)


def send(value, to):
    pairs = []
    for z in range(NZ):
        for y in range(NY):
            for x in range(NX):
                for c in range(NC):
                    tz, ty, tx, tc = to(z, y, x, c)
                    here = ((z * NY + y) * NX + x) * NC + c
                    there = ((tz % NZ * NY + ty % NY) * NX + tx % NX) * NC + tc
                    pairs.append((here, there))
    return lax.ppermute(value, ("adapter", "tensor"), pairs)


def to_sibling(value):
    return send(value, lambda z, y, x, c: (z, y, x, 1 - c))


def along_z(value, cross=0):
    return send(value, lambda z, y, x, c: (z + 1 - 2 * c, y, x, c ^ cross))


def along_x(value, step):
    return send(value, lambda z, y, x, c: (z, y, x + step, c))


def along_y(value, step):
    return send(value, lambda z, y, x, c: (z, y + step, x, c))


def along_first(value, step):
    return send(value, lambda z, y, x, c: (z, y + step * c, x + step * (1 - c), c))


def along_second(value, step):
    return send(value, lambda z, y, x, c: (z, y + step * (1 - c), x + step * c, c))


def spread_kernel(table_ref, down_ref, up_ref, out_ref):
    stored = down_ref.shape[0]

    def slot(i, carry):
        local = table_ref[INDEX + table_ref[i]] - lax.axis_index("adapter") * stored
        at, here = jnp.clip(local, 0, stored - 1), (local >= 0) & (local < stored)
        for kind, store in enumerate((down_ref, up_ref)):
            panel = store[at]
            out_ref[i, kind] = jnp.where(here, panel, jnp.zeros_like(panel))
        return carry

    lax.fori_loop(0, out_ref.shape[0], slot, 0, unroll=4)


def shrink_kernel(panels_ref, hidden_ref, slot_ref, keep_ref, give_ref):
    wanted, _, rank, _ = panels_ref.shape
    rows = hidden_ref.shape[0]
    core = lax.rem(lax.axis_index("tensor"), 2)

    def one(j, total):
        part = lax.dot_general(
            panels_ref[j, 0], hidden_ref[...], (((1,), (1,)), ((), ())), preferred_element_type=f32
        )
        return jnp.where(slot_ref[...] == j, part, total)

    total = lax.fori_loop(0, wanted, one, jnp.zeros((rank, rows), f32))
    left, right = total[:, : rows // 2], total[:, rows // 2 :]
    keep_ref[...] = jnp.where(core == 0, left, right)
    give_ref[...] = jnp.where(core == 0, right, left)


def base_kernel(block_ref, *refs):
    *stacks, mine_ref, sib_ref, out_ref, weights, sems = refs
    count = weights.shape[0]
    columns = mine_ref.shape[2]

    def fetch(i, side):
        source = (mine_ref, sib_ref)[side].at[block_ref[i]]
        place = weights.at[i, :, side * columns : (side + 1) * columns]
        return pltpu.make_async_copy(source, place, sems.at[i, side])

    for i in range(count):
        for side in range(2):
            fetch(i, side).start()
    if len(stacks[0].shape) == 3 and stacks[0].shape[2] == columns:
        out_ref[...] = stacks[0][...]
        stacks = stacks[1:]
    else:
        out_ref[...] = jnp.zeros_like(out_ref)
    at = 0
    for stack in stacks:
        first = at

        def piece(i, carry):
            for side in range(2):
                fetch(first + i, side).wait()
            both = jnp.dot(stack[i], weights[first + i], preferred_element_type=f32)
            out_ref[0] += both[:, :columns]
            out_ref[1] += both[:, columns:]
            return carry

        lax.fori_loop(0, stack.shape[0], piece, 0)
        at += stack.shape[0]


def expand_kernel(panels_ref, scaled_ref, other_ref, slot_ref, here_ref, there_ref, out_ref):
    core = lax.rem(lax.axis_index("tensor"), 2)
    wanted, _, rank, columns = panels_ref.shape
    half = scaled_ref.shape[1]
    panel = jnp.concatenate([panels_ref[j, 1] for j in range(wanted)], axis=0)
    for part in range(2):
        mine = core == part
        scaled = jnp.where(mine, scaled_ref[...], other_ref[...])
        base = jnp.where(mine, here_ref[...], there_ref[...])
        slot = slot_ref[:, part * half : (part + 1) * half]
        delta = jnp.concatenate(
            [jnp.where(slot == j, scaled, jnp.zeros_like(scaled)) for j in range(wanted)], axis=0
        )
        total = base + lax.dot_general(delta, panel, (((0,), (0,)), ((), ())), preferred_element_type=f32)
        out_ref[part * half : (part + 1) * half, :] = total.astype(out_ref.dtype)


def own_kernel(hidden_ref, got_ref, out_ref):
    core = lax.rem(lax.axis_index("tensor"), 2)
    rows, feats = got_ref.shape
    mine = hidden_ref[pl.ds(pl.multiple_of(core * rows, rows), rows), :]
    got = got_ref[...]
    out_ref[:, :feats] = jnp.where(core == 0, mine, got)
    out_ref[:, feats:] = jnp.where(core == 0, got, mine)


def after(value, *earlier):
    return lax.optimization_barrier((value, *earlier))[0]


def per_device(hidden_rows, query_weight, down_panels, up_panels, store_index, requests, row_slot):
    rows, feats = hidden_rows.shape
    stored, rank, columns = down_panels.shape
    groups, wanted = requests.shape
    t = lax.axis_index("tensor")
    y, x, c = t // 8, (t // 2) % 4, t % 2
    slot_row = row_slot.reshape(1, rows)
    table = jnp.concatenate((requests.reshape(-1), store_index))

    with jax.named_scope("hidden_swap"):
        give = jnp.where(c == 0, hidden_rows[rows // 2 :], hidden_rows[: rows // 2])
        got = to_sibling(give)

    with jax.named_scope("panel_fetch"):
        spread = kernel_call(
            spread_kernel, jax.ShapeDtypeStruct((groups * wanted, 2, rank, columns), bf16),
            after(table, give), down_panels, up_panels,
        )
        panels = lax.psum_scatter(spread, "adapter", scatter_dimension=0, tiled=True)

    with jax.named_scope("hidden_first"):
        own_piece = kernel_call(
            own_kernel, jax.ShapeDtypeStruct((rows // 2, 2 * feats), bf16), hidden_rows, after(got, spread)
        )
        below = along_first(own_piece, 1)
        above = along_first(own_piece, -1)

    with jax.named_scope("weight_swap"):
        weight_sib = to_sibling(after(query_weight, own_piece))

    def blocks(firsts, second):
        out = []
        for first in firsts:
            sy = y + jnp.where(c == 0, second, first)
            sx = x + jnp.where(c == 0, first, second)
            out.append((sy % 4) * 4 + sx % 4)
        return out

    weight_shape = (16, 2 * feats, columns)
    weights = (query_weight.reshape(weight_shape), weight_sib.reshape(weight_shape))

    def add_base(total, *parts):
        order = sum([blocks(firsts, second) for _, firsts, second in parts], [])
        stacks = [stack for stack, _, _ in parts]
        if total is not None:
            stacks = [total] + stacks
        operands = [jnp.stack(order).astype(i32), *stacks, *weights]
        return kernel_call(
            base_kernel,
            jax.ShapeDtypeStruct((2, rows // 2, columns), f32),
            *operands,
            specs=[SMEM] + [VMEM] * len(stacks) + [ANY, ANY],
            scratch=[
                pltpu.VMEM((len(order), 2 * feats, 2 * columns), bf16),
                pltpu.SemaphoreType.DMA((len(order), 2)),
            ],
        )

    near_at, rest_at = (0, -1), (1, 2)
    with jax.named_scope("hidden_second"):
        near = jnp.stack((own_piece, below))
        beyond = along_first(below, 1)
        near_below, near_above = along_second(near, 1), along_second(near, -1)
        rest = jnp.stack((above, after(beyond, weight_sib)))
        rest_below, rest_above = along_second(rest, 1), along_second(rest, -1)
        near_below = after(near_below, rest)
        near_beyond = along_second(near_below, 1)
        near_above = after(near_above, near_below)
        rest_above = after(rest_above, near_above)
        rest_beyond = along_second(rest_above, -1)
    with jax.named_scope("shrink"):
        part = jax.ShapeDtypeStruct((rank, rows // 2), f32)
        keep, give = kernel_call(
            shrink_kernel, (part, part), after(panels, near_beyond, rest_beyond), hidden_rows, slot_row
        )
    with jax.named_scope("shrink_sum"):
        part = keep + to_sibling(give)
        pieces = along_x(part, 1), along_x(part, -1), along_x(part, 2)
    with jax.named_scope("base"):
        base = add_base(
            None, (after(near, part), near_at, 0), (rest, rest_at, 0), (near_below, near_at, -1), (near_above, near_at, 1)
        )
    with jax.named_scope("shrink_sum"):
        pieces = after(pieces, base)
        part = part + pieces[0] + pieces[1] + pieces[2]
        pieces = along_y(part, 1), along_y(part, -1), along_y(part, 2)
    with jax.named_scope("base"):
        base = add_base(
            after(base, part), (rest_below, rest_at, -1), (rest_above, rest_at, 1), (near_beyond, near_at, 2),
            (rest_beyond, rest_at, 2),
        )
    with jax.named_scope("shrink_sum"):
        pieces = after(pieces, base)
        part = part + pieces[0] + pieces[1] + pieces[2]
        scaled = (part * adapter_scale).astype(bf16)
        scaled_other = to_sibling(scaled)
    with jax.named_scope("base"):
        base_here = base[0]
        base_there = to_sibling(after(base[1], scaled))

    with jax.named_scope("expand"):
        return kernel_call(
            expand_kernel, jax.ShapeDtypeStruct((rows, columns), bf16),
            panels, scaled, scaled_other, slot_row, base_here, base_there,
        )


def solution(mesh):
    return jax.shard_map(
        per_device,
        mesh=mesh,
        in_specs=(
            P("adapter", "tensor"),
            P(None, "tensor"),
            P("adapter", None, "tensor"),
            P("adapter", None, "tensor"),
            P(),
            P(),
            P("adapter"),
        ),
        out_specs=P("adapter", "tensor"),
        check_vma=False,
    )
```

time: 360 us -> 112 us (0.31)
  waiting for transfers between devices: 320 us -> 45.4 us
  starting transfers between devices: 0.12 us -> 24.8 us
  matrix products: 20 us -> 0 us
  Pallas kernels: 0 us -> 14.8 us
  local copies, waits for them, and re-layouts: 3.24 us -> 11.2 us
    all_gather x3 -> x0, waiting for transfers between devices: 215 us -> none  [the longest x1 74.1 us: per_device(): lax.all_gather(down_panels, 'adapter', axis=0, tiled=True)]
    psum x1 -> x0, waiting for transfers between devices: 104 us -> none  [per_device(): local_total = lax.psum(own_part, 'tensor')]
    ppermute x0 -> x20, waiting for transfers between devices: none -> 38.5 us  [send(): return lax.ppermute(value, ('adapter', 'tensor'), pairs)]
    ppermute x0 -> x20, starting transfers between devices: none -> 24.8 us  [send(): return lax.ppermute(value, ('adapter', 'tensor'), pairs)]
    dot_general x5 -> x0, matrix products: 20 us -> none  [the longest x1 7.62 us: per_device(): jnp.dot(lax.all_gather(hidden_rows, 'tensor', axis=1, tiled=True), query_...]
    pallas_call x0 -> x6, Pallas kernels: none -> 14.8 us  [kernel_call(): pl.pallas_call(kernel, out_shape=out_shape, in_specs=[spec if spec else S...]
    unnamed x5 -> x28, local copies, waits for them, and re-layouts: 2.54 us -> 10.2 us
    reduce_scatter x0 -> x1, waiting for transfers between devices: none -> 6.95 us  [per_device(): lax.psum_scatter(spread, 'adapter', scatter_dimension=0, tiled=True)]
  transfers between devices with their start and end apart: 4 -> 21, of which waited for: 4 -> 10; matrix products, arithmetic and copies ran while one was open for 6% -> 0% of each run, Pallas kernels for 0% -> 11%
where the time goes in v1:
time: 112 us
  waiting for transfers between devices  45.4 us (41%)
  starting transfers between devices  24.8 us (22%)
  Pallas kernels  14.8 us (13%)
  between operations  13.6 us (12%)
  local copies, waits for them, and re-layouts  11.2 us (10%)
  other arithmetic  2.01 us (2%)
    ppermute x20, waiting for transfers between devices, send(): return lax.ppermute(value, ('adapter', 'tensor'), pairs)  38.5 us
    ppermute x20, starting transfers between devices, send(): return lax.ppermute(value, ('adapter', 'tensor'), pairs)  24.8 us
    pallas_call x6, Pallas kernels, kernel_call(): pl.pallas_call(kernel, out_shape=out_shape, in_specs=[spec if spec else S...  14.8 us
    unnamed x28, local copies, waits for them, and re-layouts  10.2 us
    reduce_scatter x1, waiting for transfers between devices, per_device(): lax.psum_scatter(spread, 'adapter', scatter_dimension=0, tiled=True)  6.95 us
  transfers between devices with their start and end apart: 21, of which 10 were waited for; matrix products, arithmetic and copies ran while one was open for 0% of the time, Pallas kernels for 11%

profile of v1, /device:TPU:1, one launch (start us, length us, event | category | flops | bytes accessed | tf_op | source)
XLA Modules:
  0.0 111.8 jit_solution(2396287234192986415)
XLA Ops:
  8.1 1.0 slice_select_fusion
  9.1 1.1 %copy-done.4 = bf16[24,64,256]{2,1,0:T(8,128)(2,1)S(1)} copy-done((bf16[24,64,256]{2,1,0:T(8,128)(2,1)S(1)}, bf16[24,64,256]{2,1,0:T(8,128)(2,1)}, u32[]{:S(2)}) %copy-start.4) | copy-done | bytes 786456
  10.2 1.1 %copy-done.5 = bf16[24,64,256]{2,1,0:T(8,128)(2,1)S(1)} copy-done((bf16[24,64,256]{2,1,0:T(8,128)(2,1)S(1)}, bf16[24,64,256]{2,1,0:T(8,128)(2,1)}, u32[]{:S(2)}) %copy-start.5) | copy-done | bytes 786456
  11.4 1.4 %panel_fetch.1 = bf16[64,2,64,256]{3,2,1,0:T(8,128)(2,1)S(1)} custom-call(s32[256]{0:T(256)S(1)} %pad_add_fusion.table_ref, bf16[24,64,256]{2,1,0:T(8,128)(2,1)S(1)} %copy-done.4, bf16[24,64,256]{2,1,0:T(8,128)(2,1)S(1)} %copy-done.5), custom_call_target="tpu_custom_call" | custom-call | tf_op jit(solution)/shard_map/panel_fetch/pallas_call | solution.py:21
  12.8 2.0 %copy-done = bf16[64,2,64,256]{3,2,1,0:T(8,128)(2,1)} copy-done((bf16[64,2,64,256]{3,2,1,0:T(8,128)(2,1)}, bf16[64,2,64,256]{3,2,1,0:T(8,128)(2,1)S(1)}, u32[]{:S(2)}) %copy-start) | copy-done | bytes 4194328
  14.8 3.3 %collective-permute-start = (bf16[384,256]{1,0:T(8,128)(2,1)S(1)}, bf16[384,256]{1,0:T(8,128)(2,1)S(1)}, u32[]{:S(2)}, u32[]{:S(2)}) collective-permute-start(bf16[384,256]{1,0:T(8,128)(2,1)S(1)} %slice_select_fusion), channel_id=1, source_target_pairs={{0,1},{1,0},{2,3},{3,2},{4,5},{5,4},{6,7},{7,6},{8,9},{9,8},{10,11... | collective-permute-start | bytes 589832 | tf_op jit(solution)/shard_map/hidden_swap/ppermute | solution.py:41
  18.1 1.1 collective-permute-done.got_ref
  19.7 8.1 %collective-permute-done.1 = bf16[384,512]{1,0:T(8,128)(2,1)S(1)} collective-permute-done((bf16[384,512]{1,0:T(8,128)(2,1)S(1)}, bf16[384,512]{1,0:T(8,128)(2,1)S(1)}, u32[]{:S(2)}, u32[]{:S(2)}) %collective-permute-start.1) | collective-permute-done | bytes 393248 | tf_op jit(solution)/shard_map/hidden_first/ppermute | solution.py:41
  27.8 2.7 %collective-permute-start.3 = (bf16[384,512]{1,0:T(8,128)(2,1)S(1)}, bf16[384,512]{1,0:T(8,128)(2,1)S(1)}, u32[]{:S(2)}, u32[]{:S(2)}) collective-permute-start(bf16[384,512]{1,0:T(8,128)(2,1)S(1)} %hidden_first.1), channel_id=1, source_target_pairs={{0,6},{1,25},{2,0},{3,27},{4,2},{5,29},{6,4},{7,31},{8,14},{9,1},{... | collective-permute-start | bytes 1179656 | tf_op jit(solution)/shard_map/hidden_first/ppermute | solution.py:41
  30.7 2.7 %collective-permute-start.8 = (bf16[2,384,512]{2,1,0:T(8,128)(2,1)S(1)}, bf16[2,384,512]{2,1,0:T(8,128)(2,1)S(1)}, u32[]{:S(2)}, u32[]{:S(2)}) collective-permute-start(bf16[2,384,512]{2,1,0:T(8,128)(2,1)S(1)} %pad_maximum_fusion.refs_0_), channel_id=1, source_target_pairs={{0,24},{1,7},{2,26},{3,1},{4,28},{5,3},{6,30},{7,5},{8,0},{9,15},{... | collective-permute-start | bytes 2359304 | tf_op jit(solution)/shard_map/hidden_second/ppermute | solution.py:41
  33.4 2.7 %collective-permute-done.4 = bf16[384,512]{1,0:T(8,128)(2,1)S(1)} collective-permute-done((bf16[384,512]{1,0:T(8,128)(2,1)S(1)}, bf16[384,512]{1,0:T(8,128)(2,1)S(1)}, u32[]{:S(2)}, u32[]{:S(2)}) %collective-permute-start.4) | collective-permute-done | bytes 393248 | tf_op jit(solution)/shard_map/hidden_second/ppermute | solution.py:41
  36.7 9.2 %collective-permute-done.2.refs_2_ = bf16[2,384,512]{2,1,0:T(8,128)(2,1)S(1)} collective-permute-done((bf16[2,384,512]{2,1,0:T(8,128)(2,1)S(1)}, bf16[2,384,512]{2,1,0:T(8,128)(2,1)S(1)}, u32[]{:S(2)}, u32[]{:S(2)}) %collective-permute-start.2) | collective-permute-done | bytes 786464 | tf_op jit(solution)/shard_map/hidden_second/ppermute | solution.py:41
  47.7 6.1 %collective-permute-done.7.refs_2_ = bf16[2,384,512]{2,1,0:T(8,128)(2,1)S(1)} collective-permute-done((bf16[2,384,512]{2,1,0:T(8,128)(2,1)S(1)}, bf16[2,384,512]{2,1,0:T(8,128)(2,1)S(1)}, u32[]{:S(2)}, u32[]{:S(2)}) %collective-permute-start.7) | collective-permute-done | bytes 786464 | tf_op jit(solution)/shard_map/hidden_second/ppermute | solution.py:41
  53.8 3.5 %collective-permute-start.9 = (bf16[2,384,512]{2,1,0:T(8,128)(2,1)S(1)}, bf16[2,384,512]{2,1,0:T(8,128)(2,1)S(1)}, u32[]{:S(2)}, u32[]{:S(2)}) collective-permute-start(bf16[2,384,512]{2,1,0:T(8,128)(2,1)S(1)} %collective-permute-done.7.refs_2_), channel_id=1, source_target_pairs={{0,24},{1,7},{2,26},{3,1},{4,28},{5,3},{6,30},{7,5},{8,0},{9,15},{... | collective-permute-start | bytes 2359304 | tf_op jit(solution)/shard_map/hidden_second/ppermute | solution.py:41
  57.4 1.1 collective-permute-done.6.refs_3_
  58.4 7.9 %collective-permute-done.9.refs_4_ = bf16[2,384,512]{2,1,0:T(8,128)(2,1)S(1)} collective-permute-done((bf16[2,384,512]{2,1,0:T(8,128)(2,1)S(1)}, bf16[2,384,512]{2,1,0:T(8,128)(2,1)S(1)}, u32[]{:S(2)}, u32[]{:S(2)}) %collective-permute-start.9) | collective-permute-done | bytes 786464 | tf_op jit(solution)/shard_map/hidden_second/ppermute | solution.py:41
  67.1 7.0 %reduce-scatter.2.cloned.1.call-done.panels_ref = bf16[8,2,64,256]{3,2,1,0:T(8,128)(2,1)} async-done(((bf16[64,2,64,256]{3,2,1,0:T(8,128)(2,1)}), bf16[8,2,64,256]{3,2,1,0:T(8,128)(2,1)}) %reduce-scatter.2.cloned.1.call-update) | async-done | bytes 524304 | tf_op jit(solution)/shard_map/panel_fetch/reduce_scatter | solution.py:181
  74.1 1.0 copy-done.2
  75.1 2.2 %shrink.1 = (f32[64,384]{1,0:T(8,128)S(1)}, f32[64,384]{1,0:T(8,128)S(1)}) custom-call(bf16[8,2,64,256]{3,2,1,0:T(8,128)(2,1)S(1)} %copy-done.2, bf16[768,256]{1,0:T(8,128)(2,1)S(1)} %copy-done.1, s32[1,768]{1,0:T(1,128)S(1)} %reshape.13.slot_ref), custom_call_target="tpu_custom_call" | custom-call | tf_op jit(solution)/shard_map/shrink/pallas_call | solution.py:21
  79.0 1.3 %collective-permute-start.11 = (f32[64,384]{1,0:T(8,128)S(1)}, f32[64,384]{1,0:T(8,128)S(1)}, u32[]{:S(2)}, u32[]{:S(2)}) collective-permute-start(f32[64,384]{1,0:T(8,128)S(1)} %add.269), channel_id=1, source_target_pairs={{0,2},{1,3},{2,4},{3,5},{4,6},{5,7},{6,0},{7,1},{8,10},{9,11},{10,... | collective-permute-start | bytes 294920 | tf_op jit(solution)/shard_map/shrink_sum/ppermute | solution.py:41
  80.3 1.5 %collective-permute-start.12 = (f32[64,384]{1,0:T(8,128)S(1)}, f32[64,384]{1,0:T(8,128)S(1)}, u32[]{:S(2)}, u32[]{:S(2)}) collective-permute-start(f32[64,384]{1,0:T(8,128)S(1)} %add.269), channel_id=1, source_target_pairs={{0,6},{1,7},{2,0},{3,1},{4,2},{5,3},{6,4},{7,5},{8,14},{9,15},{10,... | collective-permute-start | bytes 294920 | tf_op jit(solution)/shard_map/shrink_sum/ppermute | solution.py:41
  81.8 1.5 %collective-permute-start.13 = (f32[64,384]{1,0:T(8,128)S(1)}, f32[64,384]{1,0:T(8,128)S(1)}, u32[]{:S(2)}, u32[]{:S(2)}) collective-permute-start(f32[64,384]{1,0:T(8,128)S(1)} %add.269), channel_id=1, source_target_pairs={{0,4},{1,5},{2,6},{3,7},{4,0},{5,1},{6,2},{7,3},{8,12},{9,13},{10,... | collective-permute-start | bytes 294920 | tf_op jit(solution)/shard_map/shrink_sum/ppermute | solution.py:41
  83.4 1.1 %copy-done.7 = bf16[2,384,512]{2,1,0:T(8,128)(2,1)S(1)} copy-done((bf16[2,384,512]{2,1,0:T(8,128)(2,1)S(1)}, bf16[2,384,512]{2,1,0:T(8,128)(2,1)}, u32[]{:S(2)}) %copy-start.7) | copy-done | bytes 786456
  84.6 1.1 %copy-done.11 = bf16[2,384,512]{2,1,0:T(8,128)(2,1)S(1)} copy-done((bf16[2,384,512]{2,1,0:T(8,128)(2,1)S(1)}, bf16[2,384,512]{2,1,0:T(8,128)(2,1)}, u32[]{:S(2)}) %copy-start.11) | copy-done | bytes 786456
  85.7 4.7 %base.2.refs_0_ = f32[2,384,256]{2,1,0:T(8,128)S(1)} custom-call(s32[8]{0:T(128)S(1)} %stack.86.block_ref, bf16[2,384,512]{2,1,0:T(8,128)(2,1)S(1)} %pad_maximum_fusion.refs_0_, bf16[2,384,512]{2,1,0:T(8,128)(2,1)S(1)} %pad_maximum_fusion.1.refs_1_, bf16[2,384,512]{2,1,0:T(8,128)(2,1)S(1)} %copy-done.7, bf16[2,384,512]{2,1,0:T(8,128)(2,1)S(1)} %copy-done.11, ...), custom_call_target="tpu_custom_call" | custom-call | tf_op jit(solution)/shard_map/base/pallas_call | solution.py:21
  90.5 1.3 %collective-permute-start.14 = (f32[64,384]{1,0:T(8,128)S(1)}, f32[64,384]{1,0:T(8,128)S(1)}, u32[]{:S(2)}, u32[]{:S(2)}) collective-permute-start(f32[64,384]{1,0:T(8,128)S(1)} %add_add_fusion), channel_id=1, source_target_pairs={{0,8},{1,9},{2,10},{3,11},{4,12},{5,13},{6,14},{7,15},{8,16},{9,17... | collective-permute-start | bytes 294920 | tf_op jit(solution)/shard_map/shrink_sum/ppermute | solution.py:41
  91.8 1.5 %collective-permute-start.15 = (f32[64,384]{1,0:T(8,128)S(1)}, f32[64,384]{1,0:T(8,128)S(1)}, u32[]{:S(2)}, u32[]{:S(2)}) collective-permute-start(f32[64,384]{1,0:T(8,128)S(1)} %add_add_fusion), channel_id=1, source_target_pairs={{0,24},{1,25},{2,26},{3,27},{4,28},{5,29},{6,30},{7,31},{8,0},{9,1... | collective-permute-start | bytes 294920 | tf_op jit(solution)/shard_map/shrink_sum/ppermute | solution.py:41
  93.3 1.5 %collective-permute-start.16 = (f32[64,384]{1,0:T(8,128)S(1)}, f32[64,384]{1,0:T(8,128)S(1)}, u32[]{:S(2)}, u32[]{:S(2)}) collective-permute-start(f32[64,384]{1,0:T(8,128)S(1)} %add_add_fusion), channel_id=1, source_target_pairs={{0,16},{1,17},{2,18},{3,19},{4,20},{5,21},{6,22},{7,23},{8,24},{9,... | collective-permute-start | bytes 294920 | tf_op jit(solution)/shard_map/shrink_sum/ppermute | solution.py:41
  94.8 5.3 %base.3 = f32[2,384,256]{2,1,0:T(8,128)S(1)} custom-call(s32[8]{0:T(128)S(1)} %stack.95.block_ref, f32[2,384,256]{2,1,0:T(8,128)S(1)} %base.2.refs_0_, bf16[2,384,512]{2,1,0:T(8,128)(2,1)} %collective-permute-done.17.refs_1_, bf16[2,384,512]{2,1,0:T(8,128)(2,1)S(1)} %collective-permute-done.7.refs_2_, ...), custom_call_target="tpu_custom_call" | custom-call | tf_op jit(solution)/shard_map/base/pallas_call | solution.py:21
  100.2 2.1 %collective-permute-start.19 = (f32[384,256]{1,0:T(8,128)S(1)}, f32[384,256]{1,0:T(8,128)S(1)}, u32[]{:S(2)}, u32[]{:S(2)}) collective-permute-start(f32[384,256]{1,0:T(8,128)S(1)} %get-tuple-element.42), channel_id=1, source_target_pairs={{0,1},{1,0},{2,3},{3,2},{4,5},{5,4},{6,7},{7,6},{8,9},{9,8},{10,11... | collective-permute-start | bytes 1179656 | tf_op jit(solution)/shard_map/base/ppermute | solution.py:41
  102.5 1.3 %collective-permute-done.18.other_ref = bf16[64,384]{1,0:T(8,128)(2,1)S(1)} collective-permute-done((bf16[64,384]{1,0:T(8,128)(2,1)S(1)}, bf16[64,384]{1,0:T(8,128)(2,1)S(1)}, u32[]{:S(2)}, u32[]{:S(2)}) %collective-permute-start.18) | collective-permute-done | bytes 49184 | tf_op jit(solution)/shard_map/shrink_sum/ppermute | solution.py:41
  103.8 1.2 %expand.1 = bf16[768,256]{1,0:T(8,128)(2,1)} custom-call(bf16[8,2,64,256]{3,2,1,0:T(8,128)(2,1)S(1)} %copy-done.3, bf16[64,384]{1,0:T(8,128)(2,1)S(1)} %multiply_convert_fusion.scaled_ref, bf16[64,384]{1,0:T(8,128)(2,1)S(1)} %collective-permute-done.18.other_ref, s32[1,768]{1,0:T(1,128)S(1)} %reshape.13.slot_ref, f32[384,256]{1,0:T(8,128)S(1)} %get-tuple-element.44.here_ref, ...), custom_call_target="tpu_custom_call" | custom-call | tf_op jit(solution)/shard_map/expand/pallas_call | solution.py:21
  (57 shorter events, 7.6 us)
Async XLA Ops:
  6.5 67.6 %reduce-scatter.2.cloned.1.call-start = ((), (), s32[]{:S(2)}) async-start(), calls=%async_computation.1 | async-start | bytes 4718592 | tf_op jit(solution)/shard_map/panel_fetch/reduce_scatter | solution.py:181
  9.1 1.1 %copy-start.4 = (bf16[24,64,256]{2,1,0:T(8,128)(2,1)S(1)}, bf16[24,64,256]{2,1,0:T(8,128)(2,1)}, u32[]{:S(2)}) copy-start(bf16[24,64,256]{2,1,0:T(8,128)(2,1)} %down_ref.1) | copy-start | bytes 2359300
  10.2 1.1 %copy-start.5 = (bf16[24,64,256]{2,1,0:T(8,128)(2,1)S(1)}, bf16[24,64,256]{2,1,0:T(8,128)(2,1)}, u32[]{:S(2)}) copy-start(bf16[24,64,256]{2,1,0:T(8,128)(2,1)} %up_ref.1) | copy-start | bytes 2359300
  11.4 7.8 %copy-start.1 = (bf16[768,256]{1,0:T(8,128)(2,1)S(1)}, bf16[768,256]{1,0:T(8,128)(2,1)}, u32[]{:S(2)}) copy-start(bf16[768,256]{1,0:T(8,128)(2,1)} %hidden_ref.3) | copy-start | bytes 1179652
  12.7 2.0 %copy-start = (bf16[64,2,64,256]{3,2,1,0:T(8,128)(2,1)}, bf16[64,2,64,256]{3,2,1,0:T(8,128)(2,1)S(1)}, u32[]{:S(2)}) copy-start(bf16[64,2,64,256]{3,2,1,0:T(8,128)(2,1)S(1)} %panel_fetch.1) | copy-start | bytes 12582916
  14.8 42.6 %copy-start.13 = (s32[768]{0:T(1024)S(1)}, s32[768]{0:T(1024)}, u32[]{:S(2)}) copy-start(s32[768]{0:T(1024)} %param.13) | copy-start | bytes 9220
  14.8 4.4 %collective-permute-start = (bf16[384,256]{1,0:T(8,128)(2,1)S(1)}, bf16[384,256]{1,0:T(8,128)(2,1)S(1)}, u32[]{:S(2)}, u32[]{:S(2)}) collective-permute-start(bf16[384,256]{1,0:T(8,128)(2,1)S(1)} %slice_select_fusion), channel_id=1, source_target_pairs={{0,1},{1,0},{2,3},{3,2},{4,5},{5,4},{6,7},{7,6},{8,9},{9,8},{10,11... | collective-permute-start | bytes 589832 | tf_op jit(solution)/shard_map/hidden_swap/ppermute | solution.py:41
  19.2 16.8 %collective-permute-start.5 = (bf16[8192,256]{1,0:T(8,128)(2,1)}, bf16[8192,256]{1,0:T(8,128)(2,1)S(1)}, u32[]{:S(2)}, u32[]{:S(2)}) collective-permute-start(bf16[8192,256]{1,0:T(8,128)(2,1)} %param.8), channel_id=1, source_target_pairs={{0,1},{1,0},{2,3},{3,2},{4,5},{5,4},{6,7},{7,6},{8,9},{9,8},{10,11... | collective-permute-start | bytes 12582920 | tf_op jit(solution)/shard_map/weight_swap/ppermute | solution.py:41
  19.7 8.1 %collective-permute-start.1 = (bf16[384,512]{1,0:T(8,128)(2,1)S(1)}, bf16[384,512]{1,0:T(8,128)(2,1)S(1)}, u32[]{:S(2)}, u32[]{:S(2)}) collective-permute-start(bf16[384,512]{1,0:T(8,128)(2,1)S(1)} %hidden_first.1), channel_id=1, source_target_pairs={{0,2},{1,9},{2,4},{3,11},{4,6},{5,13},{6,0},{7,15},{8,10},{9,17},{... | collective-permute-start | bytes 1179656 | tf_op jit(solution)/shard_map/hidden_first/ppermute | solution.py:41
  27.8 8.2 %collective-permute-start.4 = (bf16[384,512]{1,0:T(8,128)(2,1)S(1)}, bf16[384,512]{1,0:T(8,128)(2,1)S(1)}, u32[]{:S(2)}, u32[]{:S(2)}) collective-permute-start(bf16[384,512]{1,0:T(8,128)(2,1)S(1)} %collective-permute-done.1), channel_id=1, source_target_pairs={{0,2},{1,9},{2,4},{3,11},{4,6},{5,13},{6,0},{7,15},{8,10},{9,17},{... | collective-permute-start | bytes 1179656 | tf_op jit(solution)/shard_map/hidden_second/ppermute | solution.py:41
  27.8 8.2 %collective-permute-start.3 = (bf16[384,512]{1,0:T(8,128)(2,1)S(1)}, bf16[384,512]{1,0:T(8,128)(2,1)S(1)}, u32[]{:S(2)}, u32[]{:S(2)}) collective-permute-start(bf16[384,512]{1,0:T(8,128)(2,1)S(1)} %hidden_first.1), channel_id=1, source_target_pairs={{0,6},{1,25},{2,0},{3,27},{4,2},{5,29},{6,4},{7,31},{8,14},{9,1},{... | collective-permute-start | bytes 1179656 | tf_op jit(solution)/shard_map/hidden_first/ppermute | solution.py:41
  30.6 15.4 %collective-permute-start.2 = (bf16[2,384,512]{2,1,0:T(8,128)(2,1)S(1)}, bf16[2,384,512]{2,1,0:T(8,128)(2,1)S(1)}, u32[]{:S(2)}, u32[]{:S(2)}) collective-permute-start(bf16[2,384,512]{2,1,0:T(8,128)(2,1)S(1)} %pad_maximum_fusion.refs_0_), channel_id=1, source_target_pairs={{0,8},{1,3},{2,10},{3,5},{4,12},{5,7},{6,14},{7,1},{8,16},{9,11},{... | collective-permute-start | bytes 2359304 | tf_op jit(solution)/shard_map/hidden_second/ppermute | solution.py:41
  30.7 16.1 %collective-permute-start.8 = (bf16[2,384,512]{2,1,0:T(8,128)(2,1)S(1)}, bf16[2,384,512]{2,1,0:T(8,128)(2,1)S(1)}, u32[]{:S(2)}, u32[]{:S(2)}) collective-permute-start(bf16[2,384,512]{2,1,0:T(8,128)(2,1)S(1)} %pad_maximum_fusion.refs_0_), channel_id=1, source_target_pairs={{0,24},{1,7},{2,26},{3,1},{4,28},{5,3},{6,30},{7,5},{8,0},{9,15},{... | collective-permute-start | bytes 2359304 | tf_op jit(solution)/shard_map/hidden_second/ppermute | solution.py:41
  36.1 22.3 %copy-start.12 = (bf16[8192,256]{1,0:T(8,128)(2,1)}, bf16[8192,256]{1,0:T(8,128)(2,1)S(1)}, u32[]{:S(2)}) copy-start(bf16[8192,256]{1,0:T(8,128)(2,1)S(1)} %collective-permute-done.5) | copy-start | bytes 12582916
  36.2 17.7 %collective-permute-start.7 = (bf16[2,384,512]{2,1,0:T(8,128)(2,1)S(1)}, bf16[2,384,512]{2,1,0:T(8,128)(2,1)S(1)}, u32[]{:S(2)}, u32[]{:S(2)}) collective-permute-start(bf16[2,384,512]{2,1,0:T(8,128)(2,1)S(1)} %pad_maximum_fusion.1.refs_1_), channel_id=1, source_target_pairs={{0,24},{1,7},{2,26},{3,1},{4,28},{5,3},{6,30},{7,5},{8,0},{9,15},{... | collective-permute-start | bytes 2359304 | tf_op jit(solution)/shard_map/hidden_second/ppermute | solution.py:41
  46.0 12.5 %collective-permute-start.6 = (bf16[2,384,512]{2,1,0:T(8,128)(2,1)S(1)}, bf16[2,384,512]{2,1,0:T(8,128)(2,1)S(1)}, u32[]{:S(2)}, u32[]{:S(2)}) collective-permute-start(bf16[2,384,512]{2,1,0:T(8,128)(2,1)S(1)} %collective-permute-done.2.refs_2_), channel_id=1, source_target_pairs={{0,8},{1,3},{2,10},{3,5},{4,12},{5,7},{6,14},{7,1},{8,16},{9,11},{... | collective-permute-start | bytes 2359304 | tf_op jit(solution)/shard_map/hidden_second/ppermute | solution.py:41
  53.8 12.5 %collective-permute-start.9 = (bf16[2,384,512]{2,1,0:T(8,128)(2,1)S(1)}, bf16[2,384,512]{2,1,0:T(8,128)(2,1)S(1)}, u32[]{:S(2)}, u32[]{:S(2)}) collective-permute-start(bf16[2,384,512]{2,1,0:T(8,128)(2,1)S(1)} %collective-permute-done.7.refs_2_), channel_id=1, source_target_pairs={{0,24},{1,7},{2,26},{3,1},{4,28},{5,3},{6,30},{7,5},{8,0},{9,15},{... | collective-permute-start | bytes 2359304 | tf_op jit(solution)/shard_map/hidden_second/ppermute | solution.py:41
  57.3 37.5 %collective-permute-start.17 = (bf16[2,384,512]{2,1,0:T(8,128)(2,1)S(1)}, bf16[2,384,512]{2,1,0:T(8,128)(2,1)}, u32[]{:S(2)}, u32[]{:S(2)}) collective-permute-start(bf16[2,384,512]{2,1,0:T(8,128)(2,1)S(1)} %pad_maximum_fusion.1.refs_1_), channel_id=1, source_target_pairs={{0,8},{1,3},{2,10},{3,5},{4,12},{5,7},{6,14},{7,1},{8,16},{9,11},{... | collective-permute-start | bytes 2359304 | tf_op jit(solution)/shard_map/hidden_second/ppermute | solution.py:41
  74.1 1.0 copy-start.2
  77.3 1.7 %collective-permute-start.10 = (f32[64,384]{1,0:T(8,128)S(1)}, f32[64,384]{1,0:T(8,128)S(1)}, u32[]{:S(2)}, u32[]{:S(2)}) collective-permute-start(f32[64,384]{1,0:T(8,128)S(1)} %get-tuple-element.33), channel_id=1, source_target_pairs={{0,1},{1,0},{2,3},{3,2},{4,5},{5,4},{6,7},{7,6},{8,9},{9,8},{10,11... | collective-permute-start | bytes 294920 | tf_op jit(solution)/shard_map/shrink_sum/ppermute | solution.py:41
  79.0 11.4 %collective-permute-start.11 = (f32[64,384]{1,0:T(8,128)S(1)}, f32[64,384]{1,0:T(8,128)S(1)}, u32[]{:S(2)}, u32[]{:S(2)}) collective-permute-start(f32[64,384]{1,0:T(8,128)S(1)} %add.269), channel_id=1, source_target_pairs={{0,2},{1,3},{2,4},{3,5},{4,6},{5,7},{6,0},{7,1},{8,10},{9,11},{10,... | collective-permute-start | bytes 294920 | tf_op jit(solution)/shard_map/shrink_sum/ppermute | solution.py:41
  80.3 10.2 %collective-permute-start.12 = (f32[64,384]{1,0:T(8,128)S(1)}, f32[64,384]{1,0:T(8,128)S(1)}, u32[]{:S(2)}, u32[]{:S(2)}) collective-permute-start(f32[64,384]{1,0:T(8,128)S(1)} %add.269), channel_id=1, source_target_pairs={{0,6},{1,7},{2,0},{3,1},{4,2},{5,3},{6,4},{7,5},{8,14},{9,15},{10,... | collective-permute-start | bytes 294920 | tf_op jit(solution)/shard_map/shrink_sum/ppermute | solution.py:41
  81.8 8.7 %collective-permute-start.13 = (f32[64,384]{1,0:T(8,128)S(1)}, f32[64,384]{1,0:T(8,128)S(1)}, u32[]{:S(2)}, u32[]{:S(2)}) collective-permute-start(f32[64,384]{1,0:T(8,128)S(1)} %add.269), channel_id=1, source_target_pairs={{0,4},{1,5},{2,6},{3,7},{4,0},{5,1},{6,2},{7,3},{8,12},{9,13},{10,... | collective-permute-start | bytes 294920 | tf_op jit(solution)/shard_map/shrink_sum/ppermute | solution.py:41
  83.4 1.1 %copy-start.7 = (bf16[2,384,512]{2,1,0:T(8,128)(2,1)S(1)}, bf16[2,384,512]{2,1,0:T(8,128)(2,1)}, u32[]{:S(2)}) copy-start(bf16[2,384,512]{2,1,0:T(8,128)(2,1)} %copy-done.6) | copy-start | bytes 2359300
  84.6 1.1 %copy-start.11 = (bf16[2,384,512]{2,1,0:T(8,128)(2,1)S(1)}, bf16[2,384,512]{2,1,0:T(8,128)(2,1)}, u32[]{:S(2)}) copy-start(bf16[2,384,512]{2,1,0:T(8,128)(2,1)} %copy-done.10) | copy-start | bytes 2359300
  85.7 9.1 %copy-start.9 = (bf16[2,384,512]{2,1,0:T(8,128)(2,1)S(1)}, bf16[2,384,512]{2,1,0:T(8,128)(2,1)}, u32[]{:S(2)}) copy-start(bf16[2,384,512]{2,1,0:T(8,128)(2,1)} %copy-done.8) | copy-start | bytes 2359300
  90.5 13.3 %copy-start.3 = (bf16[8,2,64,256]{3,2,1,0:T(8,128)(2,1)S(1)}, bf16[8,2,64,256]{3,2,1,0:T(8,128)(2,1)}, u32[]{:S(2)}) copy-start(bf16[8,2,64,256]{3,2,1,0:T(8,128)(2,1)} %reduce-scatter.2.cloned.1.call-done.panels_ref) | copy-start | bytes 1572868
  90.5 9.7 %collective-permute-start.14 = (f32[64,384]{1,0:T(8,128)S(1)}, f32[64,384]{1,0:T(8,128)S(1)}, u32[]{:S(2)}, u32[]{:S(2)}) collective-permute-start(f32[64,384]{1,0:T(8,128)S(1)} %add_add_fusion), channel_id=1, source_target_pairs={{0,8},{1,9},{2,10},{3,11},{4,12},{5,13},{6,14},{7,15},{8,16},{9,17... | collective-permute-start | bytes 294920 | tf_op jit(solution)/shard_map/shrink_sum/ppermute | solution.py:41
  91.8 8.4 %collective-permute-start.15 = (f32[64,384]{1,0:T(8,128)S(1)}, f32[64,384]{1,0:T(8,128)S(1)}, u32[]{:S(2)}, u32[]{:S(2)}) collective-permute-start(f32[64,384]{1,0:T(8,128)S(1)} %add_add_fusion), channel_id=1, source_target_pairs={{0,24},{1,25},{2,26},{3,27},{4,28},{5,29},{6,30},{7,31},{8,0},{9,1... | collective-permute-start | bytes 294920 | tf_op jit(solution)/shard_map/shrink_sum/ppermute | solution.py:41
  93.3 6.9 %collective-permute-start.16 = (f32[64,384]{1,0:T(8,128)S(1)}, f32[64,384]{1,0:T(8,128)S(1)}, u32[]{:S(2)}, u32[]{:S(2)}) collective-permute-start(f32[64,384]{1,0:T(8,128)S(1)} %add_add_fusion), channel_id=1, source_target_pairs={{0,16},{1,17},{2,18},{3,19},{4,20},{5,21},{6,22},{7,23},{8,24},{9,... | collective-permute-start | bytes 294920 | tf_op jit(solution)/shard_map/shrink_sum/ppermute | solution.py:41
  100.2 3.5 %collective-permute-start.19 = (f32[384,256]{1,0:T(8,128)S(1)}, f32[384,256]{1,0:T(8,128)S(1)}, u32[]{:S(2)}, u32[]{:S(2)}) collective-permute-start(f32[384,256]{1,0:T(8,128)S(1)} %get-tuple-element.42), channel_id=1, source_target_pairs={{0,1},{1,0},{2,3},{3,2},{4,5},{5,4},{6,7},{7,6},{8,9},{9,8},{10,11... | collective-permute-start | bytes 1179656 | tf_op jit(solution)/shard_map/base/ppermute | solution.py:41
  102.4 1.4 %collective-permute-start.18 = (bf16[64,384]{1,0:T(8,128)(2,1)S(1)}, bf16[64,384]{1,0:T(8,128)(2,1)S(1)}, u32[]{:S(2)}, u32[]{:S(2)}) collective-permute-start(bf16[64,384]{1,0:T(8,128)(2,1)S(1)} %multiply_convert_fusion.scaled_ref), channel_id=1, source_target_pairs={{0,1},{1,0},{2,3},{3,2},{4,5},{5,4},{6,7},{7,6},{8,9},{9,8},{10,11... | collective-permute-start | bytes 147464 | tf_op jit(solution)/shard_map/shrink_sum/ppermute | solution.py:41
  (3 other events, 2.6 us)
Sparse Core Ops, SparseCore 0:
  14.9 59.1 reduce-scatter.1

commit v2 on v1

v2 whole, which is shorter than its diff:
```python
import functools

import jax
import jax.numpy as jnp
from jax import lax
from jax.experimental import pallas as pl
from jax.experimental.pallas import tpu as pltpu
from jax.sharding import PartitionSpec as P

adapter_scale = 0.5
f32, bf16, i32 = jnp.float32, jnp.bfloat16, jnp.int32
NZ, NY, NX, NC = 8, 4, 4, 2
WANTED = 8
INDEX = NZ * WANTED
SMEM = pl.BlockSpec(memory_space=pltpu.SMEM)
VMEM = pl.BlockSpec(memory_space=pltpu.VMEM)
HBM = pl.BlockSpec(memory_space=pltpu.HBM)
ANY = pl.BlockSpec(memory_space=pl.ANY)


def kernel_call(kernel, out_shape, *operands, scratch=(), specs=None, limit=16 << 20, pin=True):
    specs = specs or [SMEM if v.dtype == i32 and v.size <= 256 else VMEM for v in operands]
    if pin:
        operands = [
            pltpu.with_memory_space_constraint(v, pltpu.VMEM) if spec is VMEM and v.size > 1024 else v
            for v, spec in zip(operands, specs)
        ]
        out_shape = jax.tree.map(lambda leaf: pltpu.VMEM(leaf.shape, leaf.dtype), out_shape)
    return pl.pallas_call(
        kernel,
        out_shape=out_shape,
        in_specs=specs,
        out_specs=jax.tree.map(lambda _: VMEM, out_shape),
        scratch_shapes=list(scratch),
        compiler_params=pltpu.CompilerParams(vmem_limit_bytes=limit),
    )(*operands)


def load_kernel(*refs):
    *sources, sems = refs
    sources, targets = sources[: len(sources) // 2], sources[len(sources) // 2 :]
    loads = [pltpu.make_async_copy(a, b, sems.at[i]) for i, (a, b) in enumerate(zip(sources, targets))]
    for load in loads:
        load.start()
    for load in loads:
        load.wait()


def send(value, to):
    pairs = []
    for z in range(NZ):
        for y in range(NY):
            for x in range(NX):
                for c in range(NC):
                    tz, ty, tx, tc = to(z, y, x, c)
                    here = ((z * NY + y) * NX + x) * NC + c
                    there = ((tz % NZ * NY + ty % NY) * NX + tx % NX) * NC + tc
                    pairs.append((here, there))
    return lax.ppermute(value, ("adapter", "tensor"), pairs)


def to_sibling(value):
    return send(value, lambda z, y, x, c: (z, y, x, 1 - c))


def along_z(value, cross=0):
    return send(value, lambda z, y, x, c: (z + 1 - 2 * c, y, x, c ^ cross))


def along_x(value, step):
    return send(value, lambda z, y, x, c: (z, y, x + step, c))


def along_y(value, step):
    return send(value, lambda z, y, x, c: (z, y + step, x, c))


def along_first(value, step):
    return send(value, lambda z, y, x, c: (z, y + step * c, x + step * (1 - c), c))


def along_second(value, step):
    return send(value, lambda z, y, x, c: (z, y + step * (1 - c), x + step * c, c))


def slot_of(table_ref, group, at):
    return table_ref[INDEX + table_ref[group * WANTED + at]]


def panel_of(table_ref, group, at, stored):
    local = slot_of(table_ref, group, at) - lax.axis_index("adapter") * stored
    return jnp.clip(local, 0, stored - 1), (local >= 0) & (local < stored)


def ahead(distance):
    sign = 1 - 2 * lax.rem(lax.axis_index("tensor"), 2)
    return lax.rem(lax.axis_index("adapter") + sign * distance + NZ, NZ)


def fill_kernel(blocks, stores_at, table_ref, *refs):
    inputs, stores, outs = refs[: stores_at[0]], refs[stores_at[0] : stores_at[1]], refs[stores_at[1] :]
    core = lax.rem(lax.axis_index("tensor"), 2)
    for kind, side, distance, width, source, (target, place) in blocks:
        store = stores[2 * kind + side]
        group = ahead(distance)
        first = core * width if width < WANTED else 0

        def slot(j, carry, store=store, group=group, first=first, source=source, out=outs[target], place=place):
            at, here = panel_of(table_ref, group, first + j, store.shape[0])
            panel = store[at]
            if source is None:
                old = jnp.zeros_like(panel)
            else:
                array, begin, held = source
                there = j - core * held if held < WANTED else j
                old = inputs[array][begin + jnp.clip(there, 0, held - 1)]
                if held < WANTED:
                    old = jnp.where((there >= 0) & (there < held), old, jnp.zeros_like(old))
            out[place + j] = jnp.where(here, panel, old)
            return carry

        lax.fori_loop(0, width, slot, 0, unroll=4)


def joined(table_ref, j, same_ref, cross_ref, store_ref):
    stored = store_ref.shape[0]
    core = lax.rem(lax.axis_index("tensor"), 2)
    group = lax.axis_index("adapter")
    storage = slot_of(table_ref, group, j)
    behind = lax.rem(group - storage // stored + NZ, NZ)
    below = (behind < NZ // 2) | ((behind == NZ // 2) & (j < WANTED // 2))
    own = store_ref[jnp.clip(storage - group * stored, 0, stored - 1)]
    return jnp.where(behind == 0, own, jnp.where(below == (core == 0), same_ref[j], cross_ref[j]))


def join_kernel(table_ref, same_ref, cross_ref, store_ref, out_ref):
    def one(j, carry):
        out_ref[j] = joined(table_ref, j, same_ref, cross_ref, store_ref)
        return carry

    lax.fori_loop(0, out_ref.shape[0], one, 0)


def shrink_kernel(table_ref, same_ref, cross_ref, store_ref, turned_ref, slot_ref, keep_ref, give_ref, panels, parts):
    wanted, rank, feats = panels.shape
    half = turned_ref.shape[1] // 2
    core = lax.rem(lax.axis_index("tensor"), 2)

    def one(j, carry):
        panels[j] = joined(table_ref, j, same_ref, cross_ref, store_ref)
        return carry

    lax.fori_loop(0, wanted, one, 0)
    flat = panels[...].reshape(wanted * rank, feats)
    parts[...] = jnp.dot(flat, turned_ref[...], preferred_element_type=f32)
    for side in range(2):
        columns = slice(side * half, (side + 1) * half)
        slot = slot_ref[:, columns]
        total = jnp.zeros((rank, half), f32)
        for j in range(wanted):
            total = jnp.where(slot == j, parts[j * rank : (j + 1) * rank, columns], total)

        @pl.when(core == side)
        def _():
            keep_ref[...] = total

        @pl.when(core != side)
        def _():
            give_ref[...] = total


def base_kernel(block_ref, *refs):
    *stacks, mine_ref, sib_ref, out_ref, lefts, weights, sems = refs
    columns = mine_ref.shape[2]
    total = stacks.pop(0) if len(stacks[0].shape) == 3 and stacks[0].shape[2] == columns else None
    pieces = [stack.at[i] for stack in stacks for i in range(stack.shape[0])]

    def fetch(i, side):
        source = (mine_ref, sib_ref)[side].at[block_ref[i]]
        place = weights.at[i, :, side * columns : (side + 1) * columns]
        return pltpu.make_async_copy(source, place, sems.at[i, side])

    def fetch_left(i):
        return pltpu.make_async_copy(pieces[i] if isinstance(i, int) else pieces[0], lefts.at[i], sems.at[i, 2])

    for i in range(len(pieces)):
        fetch_left(i).start()
        for side in range(2):
            fetch(i, side).start()
    out_ref[...] = jnp.zeros_like(out_ref) if total is None else total[...]

    def piece(i, carry):
        fetch_left(i).wait()
        for side in range(2):
            fetch(i, side).wait()
        both = jnp.dot(lefts[i], weights[i], preferred_element_type=f32)
        out_ref[0] += both[:, :columns]
        out_ref[1] += both[:, columns:]
        return carry

    lax.fori_loop(0, len(pieces), piece, 0)


def expand_kernel(panels_ref, scaled_ref, other_ref, slot_ref, here_ref, there_ref, out_ref):
    core = lax.rem(lax.axis_index("tensor"), 2)
    wanted, rank, columns = panels_ref.shape
    half = scaled_ref.shape[1]
    panel = panels_ref[...].reshape(wanted * rank, columns)
    for part in range(2):
        mine = core == part
        scaled = jnp.where(mine, scaled_ref[...], other_ref[...])
        base = jnp.where(mine, here_ref[...], there_ref[...])
        slot = slot_ref[:, part * half : (part + 1) * half]
        delta = jnp.concatenate(
            [jnp.where(slot == j, scaled, jnp.zeros_like(scaled)) for j in range(wanted)], axis=0
        )
        total = base + lax.dot_general(delta, panel, (((0,), (0,)), ((), ())), preferred_element_type=f32)
        out_ref[part * half : (part + 1) * half, :] = total.astype(out_ref.dtype)


def own_kernel(hidden_ref, got_ref, out_ref, turned_ref):
    core = lax.rem(lax.axis_index("tensor"), 2)
    rows, feats = hidden_ref.shape
    half = pl.ds(pl.multiple_of(core * (rows // 2), rows // 2), rows // 2)
    mine, got = hidden_ref[half, :], got_ref[half, :]
    out_ref[:, :feats] = jnp.where(core == 0, mine, got)
    out_ref[:, feats:] = jnp.where(core == 0, got, mine)
    turned_ref[...] = hidden_ref[...].T


def after(value, *earlier):
    return lax.optimization_barrier((value, *earlier))[0]


def per_device(hidden_rows, query_weight, down_panels, up_panels, store_index, requests, row_slot):
    rows, feats = hidden_rows.shape
    stored, rank, columns = down_panels.shape
    groups, wanted = requests.shape
    t = lax.axis_index("tensor")
    y, x, c = t // 8, (t // 2) % 4, t % 2
    slot_row = row_slot.reshape(1, rows)
    table = jnp.concatenate((requests.reshape(-1), store_index))

    down_sib = to_sibling(down_panels)
    got = to_sibling(hidden_rows)
    sources = (down_panels, up_panels, hidden_rows)
    down_panels, up_panels_here, hidden_rows = kernel_call(
        load_kernel, tuple(jax.ShapeDtypeStruct(v.shape, bf16) for v in sources),
        *[pltpu.with_memory_space_constraint(v, pltpu.HBM) for v in sources],
        specs=[ANY] * 3, scratch=[pltpu.SemaphoreType.DMA((3,))],
    )

    def step(parts, sizes, inputs, *earlier):
        stores = (down_panels, down_sib) + ((up_panels_here, up_sib) if any(part[0] for part in parts) else ())
        inputs = [after(value, *earlier) for value in inputs]
        ends = (len(inputs), len(inputs) + len(stores))
        return kernel_call(
            functools.partial(fill_kernel, parts, ends),
            tuple(jax.ShapeDtypeStruct((size, rank, columns), bf16) for size in sizes),
            after(table, *earlier), *inputs, *stores,
        )

    def blocks(firsts, second):
        out = []
        for first in firsts:
            sy = y + jnp.where(c == 0, second, first)
            sx = x + jnp.where(c == 0, first, second)
            out.append((sy % 4) * 4 + sx % 4)
        return out

    weight_shape = (16, 2 * feats, columns)

    def add_base(total, *parts):
        order = sum([blocks(firsts, second) for _, firsts, second in parts], [])
        stacks = [stack for stack, _, _ in parts]
        operands = ([] if total is None else [total]) + stacks
        return kernel_call(
            base_kernel,
            jax.ShapeDtypeStruct((2, rows // 2, columns), f32),
            jnp.stack(order).astype(i32), *operands,
            pltpu.with_memory_space_constraint(query_weight.reshape(weight_shape), pltpu.HBM),
            weight_sib.reshape(weight_shape),
            specs=[SMEM] + ([] if total is None else [VMEM]) + [ANY] * (len(stacks) + 2), pin=False,
            scratch=[
                pltpu.VMEM((len(order), rows // 2, 2 * feats), bf16),
                pltpu.VMEM((len(order), 2 * feats, 2 * columns), bf16),
                pltpu.SemaphoreType.DMA((len(order), 3)),
            ],
        )

    near_at, rest_at = (0, -1), (1, 2)
    few, all_of = wanted // 2, wanted
    (ring1,) = step(
        [(0, 0, 4, few, None, (0, 0)), (0, 1, 4, few, None, (0, few))], (2 * few,), [], down_sib
    )
    hop1 = along_z(ring1)
    own_piece, turned = kernel_call(
        own_kernel,
        (jax.ShapeDtypeStruct((rows // 2, 2 * feats), bf16), jax.ShapeDtypeStruct((feats, rows), bf16)),
        hidden_rows, after(got, ring1),
    )
    below, above = along_first(own_piece, 1), along_first(own_piece, -1)
    up_sib = to_sibling(after(up_panels, own_piece))
    weight_sib = to_sibling(after(query_weight, own_piece))

    (ring2,) = step(
        [
            (0, 0, 3, all_of, (0, 0, few), (0, 0)), (0, 1, 3, all_of, (0, few, few), (0, all_of)),
            (1, 0, 4, few, None, (0, 2 * all_of)), (1, 1, 4, few, None, (0, 2 * all_of + few)),
        ],
        (3 * all_of,), [hop1], own_piece, up_sib, below, above,
    )
    hop2 = along_z(ring2)
    below, above = after((below, above), ring2)
    near = jnp.stack((own_piece, below))
    near_below, near_above, beyond = along_second(near, 1), along_second(near, -1), along_first(below, 1)

    (ring3,) = step(
        [
            (0, 0, 2, all_of, (0, 0, all_of), (0, 0)), (0, 1, 2, all_of, (0, all_of, all_of), (0, all_of)),
            (1, 0, 3, all_of, (0, 2 * all_of, few), (0, 2 * all_of)),
            (1, 1, 3, all_of, (0, 2 * all_of + few, few), (0, 3 * all_of)),
        ],
        (4 * all_of,), [hop2], near, beyond,
    )
    hop3 = along_z(ring3)
    near_below, near_above, beyond = after((near_below, near_above, beyond), ring3)
    rest = jnp.stack((above, beyond))
    rest_below, rest_above, near_beyond = along_second(rest, 1), along_second(rest, -1), along_second(near_below, 1)
    base = add_base(None, (after(near, rest), near_at, 0), (near_below, near_at, -1), (near_above, near_at, 1))

    ring4, ring4_cross = step(
        [
            (0, 0, 1, all_of, (0, 0, all_of), (0, 0)), (0, 1, 1, all_of, (0, all_of, all_of), (1, 0)),
            (1, 0, 2, all_of, (0, 2 * all_of, all_of), (0, all_of)),
            (1, 1, 2, all_of, (0, 3 * all_of, all_of), (0, 2 * all_of)),
        ],
        (3 * all_of, all_of), [hop3], base,
    )
    hop4, down_cross = along_z(ring4), along_z(ring4_cross, 1)
    rest_below, rest_above = after((rest_below, rest_above), ring4)
    rest_beyond = along_second(rest_above, -1)
    base = add_base(base, (rest, rest_at, 0), (rest_below, rest_at, -1), (rest_above, rest_at, 1))

    with jax.named_scope("shrink"):
        part = jax.ShapeDtypeStruct((rank, rows // 2), f32)
        keep, give = kernel_call(
            shrink_kernel, (part, part), table, after(hop4, base), down_cross, down_panels, turned, slot_row,
            scratch=[pltpu.VMEM((wanted, rank, columns), bf16), pltpu.VMEM((wanted * rank, rows), f32)],
        )
    with jax.named_scope("shrink_sum"):
        part = keep + to_sibling(give)
        pieces = along_x(part, 1), along_x(part, -1), along_x(part, 2)
    up_to_same, up_to_cross = step(
        [
            (1, 0, 1, all_of, (0, all_of, all_of), (0, 0)), (1, 1, 1, all_of, (0, 2 * all_of, all_of), (1, 0)),
        ],
        (all_of, all_of), [hop4], part,
    )
    up_same, up_cross = along_z(up_to_same), along_z(up_to_cross, 1)
    with jax.named_scope("shrink_sum"):
        pieces = after(pieces, up_to_same)
        part = part + pieces[0] + pieces[1] + pieces[2]
        pieces = along_y(part, 1), along_y(part, -1), along_y(part, 2)
    base = add_base(after(base, part), (near_beyond, near_at, 2), (rest_beyond, rest_at, 2))
    up_here = kernel_call(
        join_kernel, jax.ShapeDtypeStruct((wanted, rank, columns), bf16), table, after(up_same, base), up_cross, up_panels_here
    )
    with jax.named_scope("shrink_sum"):
        pieces = after(pieces, up_here)
        part = part + pieces[0] + pieces[1] + pieces[2]
        scaled = (part * adapter_scale).astype(bf16)
        scaled_other = to_sibling(scaled)
    with jax.named_scope("base"):
        base_here = base[0]
        base_there = to_sibling(after(base[1], scaled))

    with jax.named_scope("expand"):
        return kernel_call(
            expand_kernel, jax.ShapeDtypeStruct((rows, columns), bf16),
            up_here, scaled, scaled_other, slot_row, base_here, base_there,
        )


def solution(mesh):
    return jax.shard_map(
        per_device,
        mesh=mesh,
        in_specs=(
            P("adapter", "tensor"),
            P(None, "tensor"),
            P("adapter", None, "tensor"),
            P("adapter", None, "tensor"),
            P(),
            P(),
            P("adapter"),
        ),
        out_specs=P("adapter", "tensor"),
        check_vma=False,
    )
```

time: 112 us -> 98.4 us (0.88)
  waiting for transfers between devices: 45.4 us -> 21.1 us
  starting transfers between devices: 24.8 us -> 40.4 us
  between operations: 13.6 us -> 0.22 us
  Pallas kernels: 14.8 us -> 24.1 us
  local copies, waits for them, and re-layouts: 11.2 us -> 9.31 us
    ppermute x20 -> x29, waiting for transfers between devices: 38.5 us -> 21.1 us  [send(): return lax.ppermute(value, ('adapter', 'tensor'), pairs)]
    ppermute x20 -> x29, starting transfers between devices: 24.8 us -> 40.4 us  [send(): return lax.ppermute(value, ('adapter', 'tensor'), pairs)]
    pallas_call x6 -> x13, Pallas kernels: 14.8 us -> 24.1 us  [kernel_call(): pl.pallas_call(kernel, out_shape=out_shape, in_specs=specs, out_specs=jax...]
    reduce_scatter x1 -> x0, waiting for transfers between devices: 6.95 us -> none  [per_device(): lax.psum_scatter(spread, 'adapter', scatter_dimension=0, tiled=True)]
    unnamed x28 -> x23, local copies, waits for them, and re-layouts: 10.2 us -> 8.32 us
  transfers between devices with their start and end apart: 21 -> 29, of which waited for: 10 -> 8; matrix products, arithmetic and copies ran while one was open for 0% -> 4% of each run, Pallas kernels for 11% -> 24%
where the time goes in v2:
time: 98.4 us; the launch traced here: 98 us
  starting transfers between devices  40.4 us (41%)
  Pallas kernels  24.1 us (24%)
  waiting for transfers between devices  21.1 us (21%)
  local copies, waits for them, and re-layouts  9.31 us (9%)
  other arithmetic  2.82 us (3%)
    ppermute x29, starting transfers between devices, send(): return lax.ppermute(value, ('adapter', 'tensor'), pairs)  40.4 us
    pallas_call x13, Pallas kernels, kernel_call(): pl.pallas_call(kernel, out_shape=out_shape, in_specs=specs, out_specs=jax...  24.1 us
    ppermute x29, waiting for transfers between devices, send(): return lax.ppermute(value, ('adapter', 'tensor'), pairs)  21.1 us
    unnamed x23, local copies, waits for them, and re-layouts  8.32 us
  transfers between devices with their start and end apart: 29, of which 8 were waited for; matrix products, arithmetic and copies ran while one was open for 4% of the time, Pallas kernels for 24%

profile of v2, /device:TPU:1, one launch (start us, length us, event | category | flops | bytes accessed | tf_op | source)
XLA Modules:
  0.0 98.0 jit_solution(8366705543537135060)
XLA Ops:
  0.0 3.2 %collective-permute-start.1 = (bf16[24,64,256]{2,1,0:T(8,128)(2,1)}, bf16[24,64,256]{2,1,0:T(8,128)(2,1)S(1)}, u32[]{:S(2)}, u32[]{:S(2)}) collective-permute-start(bf16[24,64,256]{2,1,0:T(8,128)(2,1)} %refs_0_.1), channel_id=1, source_target_pairs={{0,1},{1,0},{2,3},{3,2},{4,5},{5,4},{6,7},{7,6},{8,9},{9,8},{10,11... | collective-permute-start | bytes 2359304 | tf_op jit(solution)/shard_map/ppermute | solution.py:59
  4.0 1.6 %shard_map.73 = (bf16[24,64,256]{2,1,0:T(8,128)(2,1)S(1)}, bf16[24,64,256]{2,1,0:T(8,128)(2,1)S(1)}, bf16[768,256]{1,0:T(8,128)(2,1)S(1)}) custom-call(bf16[24,64,256]{2,1,0:T(8,128)(2,1)} %refs_0_.1, bf16[24,64,256]{2,1,0:T(8,128)(2,1)} %refs_1_.1, bf16[768,256]{1,0:T(8,128)(2,1)} %refs_2_.1), custom_call_target="tpu_custom_call" | custom-call | tf_op jit(solution)/shard_map/pallas_call | solution.py:29
  7.9 2.7 %collective-permute-start.3 = (bf16[384,512]{1,0:T(8,128)(2,1)S(1)}, bf16[384,512]{1,0:T(8,128)(2,1)S(1)}, u32[]{:S(2)}, u32[]{:S(2)}) collective-permute-start(bf16[384,512]{1,0:T(8,128)(2,1)S(1)} %get-tuple-element.50), channel_id=1, source_target_pairs={{0,6},{1,25},{2,0},{3,27},{4,2},{5,29},{6,4},{7,31},{8,14},{9,1},{... | collective-permute-start | bytes 1179656 | tf_op jit(solution)/shard_map/ppermute | solution.py:59
  10.5 3.9 %collective-permute-start.5 = (bf16[8,64,256]{2,1,0:T(8,128)(2,1)S(1)}, bf16[8,64,256]{2,1,0:T(8,128)(2,1)S(1)}, u32[]{:S(2)}, u32[]{:S(2)}) collective-permute-start(bf16[8,64,256]{2,1,0:T(8,128)(2,1)S(1)} %shard_map.74), channel_id=1, source_target_pairs={{0,32},{1,225},{2,34},{3,227},{4,36},{5,229},{6,38},{7,231},{8,40}... | collective-permute-start | bytes 786440 | tf_op jit(solution)/shard_map/ppermute | solution.py:59
  14.4 3.3 %collective-permute-done.5.refs_0_ = bf16[8,64,256]{2,1,0:T(8,128)(2,1)S(1)} collective-permute-done((bf16[8,64,256]{2,1,0:T(8,128)(2,1)S(1)}, bf16[8,64,256]{2,1,0:T(8,128)(2,1)S(1)}, u32[]{:S(2)}, u32[]{:S(2)}) %collective-permute-start.5) | collective-permute-done | bytes 262176 | tf_op jit(solution)/shard_map/ppermute | solution.py:59
  18.6 3.2 %collective-permute-start.9 = (bf16[24,64,256]{2,1,0:T(8,128)(2,1)S(1)}, bf16[24,64,256]{2,1,0:T(8,128)(2,1)S(1)}, u32[]{:S(2)}, u32[]{:S(2)}) collective-permute-start(bf16[24,64,256]{2,1,0:T(8,128)(2,1)S(1)} %shard_map.76), channel_id=1, source_target_pairs={{0,32},{1,225},{2,34},{3,227},{4,36},{5,229},{6,38},{7,231},{8,40}... | collective-permute-start | bytes 2359304 | tf_op jit(solution)/shard_map/ppermute | solution.py:59
  22.2 1.3 %collective-permute-start.6 = (bf16[2,384,512]{2,1,0:T(8,128)(2,1)S(1)}, bf16[2,384,512]{2,1,0:T(8,128)(2,1)}, u32[]{:S(2)}, u32[]{:S(2)}) collective-permute-start(bf16[2,384,512]{2,1,0:T(8,128)(2,1)S(1)} %pad_maximum_fusion.refs_0_), channel_id=1, source_target_pairs={{0,8},{1,3},{2,10},{3,5},{4,12},{5,7},{6,14},{7,1},{8,16},{9,11},{... | collective-permute-start | bytes 2359304 | tf_op jit(solution)/shard_map/ppermute | solution.py:59
  23.5 1.5 %collective-permute-start.7 = (bf16[2,384,512]{2,1,0:T(8,128)(2,1)S(1)}, bf16[2,384,512]{2,1,0:T(8,128)(2,1)S(1)}, u32[]{:S(2)}, u32[]{:S(2)}) collective-permute-start(bf16[2,384,512]{2,1,0:T(8,128)(2,1)S(1)} %pad_maximum_fusion.refs_0_), channel_id=1, source_target_pairs={{0,24},{1,7},{2,26},{3,1},{4,28},{5,3},{6,30},{7,5},{8,0},{9,15},{... | collective-permute-start | bytes 2359304 | tf_op jit(solution)/shard_map/ppermute | solution.py:59
  25.8 8.3 %collective-permute-done.8 = bf16[384,512]{1,0:T(8,128)(2,1)S(1)} collective-permute-done((bf16[384,512]{1,0:T(8,128)(2,1)S(1)}, bf16[384,512]{1,0:T(8,128)(2,1)S(1)}, u32[]{:S(2)}, u32[]{:S(2)}) %collective-permute-start.8) | collective-permute-done | bytes 393248 | tf_op jit(solution)/shard_map/ppermute | solution.py:59
  34.1 1.8 %shard_map.77 = bf16[32,64,256]{2,1,0:T(8,128)(2,1)} custom-call(s32[256]{0:T(256)S(1)} %pad_add_fusion.table_ref, bf16[24,64,256]{2,1,0:T(8,128)(2,1)S(1)} %collective-permute-done.9.refs_0_, bf16[24,64,256]{2,1,0:T(8,128)(2,1)S(1)} %get-tuple-element.48.refs_0_.refs_1_.store_ref, bf16[24,64,256]{2,1,0:T(8,128)(2,1)S(1)} %collective-permute-done.1.refs_1_.refs_2_, ...), custom_call_target="tpu_custom_call" | custom-call | tf_op jit(solution)/shard_map/pallas_call | solution.py:29
  36.0 2.0 %collective-permute-done.6.refs_1_ = bf16[2,384,512]{2,1,0:T(8,128)(2,1)} collective-permute-done((bf16[2,384,512]{2,1,0:T(8,128)(2,1)S(1)}, bf16[2,384,512]{2,1,0:T(8,128)(2,1)}, u32[]{:S(2)}, u32[]{:S(2)}) %collective-permute-start.6) | collective-permute-done | bytes 786464 | tf_op jit(solution)/shard_map/ppermute | solution.py:59
  39.9 2.7 %collective-permute-start.14 = (bf16[2,384,512]{2,1,0:T(8,128)(2,1)}, bf16[2,384,512]{2,1,0:T(8,128)(2,1)}, u32[]{:S(2)}, u32[]{:S(2)}) collective-permute-start(bf16[2,384,512]{2,1,0:T(8,128)(2,1)} %pad_maximum_fusion.1.refs_1_), channel_id=1, source_target_pairs={{0,24},{1,7},{2,26},{3,1},{4,28},{5,3},{6,30},{7,5},{8,0},{9,15},{... | collective-permute-start | bytes 2359304 | tf_op jit(solution)/shard_map/ppermute | solution.py:59
  42.7 1.1 %copy-done.5 = bf16[2,384,512]{2,1,0:T(8,128)(2,1)S(1)} copy-done((bf16[2,384,512]{2,1,0:T(8,128)(2,1)S(1)}, bf16[2,384,512]{2,1,0:T(8,128)(2,1)}, u32[]{:S(2)}) %copy-start.5) | copy-done | bytes 786456
  45.0 4.2 %shard_map.78.refs_0_ = f32[2,384,256]{2,1,0:T(8,128)S(1)} custom-call(s32[6]{0:T(128)S(1)} %stack.81.block_ref, bf16[2,384,512]{2,1,0:T(8,128)(2,1)S(1)} %copy-done.5, bf16[2,384,512]{2,1,0:T(8,128)(2,1)} %collective-permute-done.6.refs_1_, bf16[2,384,512]{2,1,0:T(8,128)(2,1)S(1)} %copy-done.7, bf16[16,512,256]{2,1,0:T(8,128)(2,1)} %bitcast.10.refs_3_.refs_4_, ...), custom_call_target="tpu_custom_call" | custom-call | tf_op jit(solution)/shard_map/pallas_call | solution.py:29
  50.2 2.5 %shard_map.79 = (bf16[24,64,256]{2,1,0:T(8,128)(2,1)}, bf16[8,64,256]{2,1,0:T(8,128)(2,1)}) custom-call(s32[256]{0:T(256)S(1)} %pad_add_fusion.table_ref, bf16[32,64,256]{2,1,0:T(8,128)(2,1)} %collective-permute-done.11.refs_0_, bf16[24,64,256]{2,1,0:T(8,128)(2,1)S(1)} %get-tuple-element.48.refs_0_.refs_1_.store_ref, ...), custom_call_target="tpu_custom_call" | custom-call | tf_op jit(solution)/shard_map/pallas_call | solution.py:29
  52.7 1.3 %collective-permute-start.12 = (bf16[24,64,256]{2,1,0:T(8,128)(2,1)}, bf16[24,64,256]{2,1,0:T(8,128)(2,1)}, u32[]{:S(2)}, u32[]{:S(2)}) collective-permute-start(bf16[24,64,256]{2,1,0:T(8,128)(2,1)} %get-tuple-element.66), channel_id=1, source_target_pairs={{0,32},{1,225},{2,34},{3,227},{4,36},{5,229},{6,38},{7,231},{8,40}... | collective-permute-start | bytes 2359304 | tf_op jit(solution)/shard_map/ppermute | solution.py:59
  54.0 1.2 %collective-permute-start.21 = (bf16[2,384,512]{2,1,0:T(8,128)(2,1)}, bf16[2,384,512]{2,1,0:T(8,128)(2,1)}, u32[]{:S(2)}, u32[]{:S(2)}) collective-permute-start(bf16[2,384,512]{2,1,0:T(8,128)(2,1)} %collective-permute-done.6.refs_1_), channel_id=1, source_target_pairs={{0,8},{1,3},{2,10},{3,5},{4,12},{5,7},{6,14},{7,1},{8,16},{9,11},{... | collective-permute-start | bytes 2359304 | tf_op jit(solution)/shard_map/ppermute | solution.py:59
  55.2 1.6 %collective-permute-start.22 = (bf16[2,384,512]{2,1,0:T(8,128)(2,1)}, bf16[2,384,512]{2,1,0:T(8,128)(2,1)}, u32[]{:S(2)}, u32[]{:S(2)}) collective-permute-start(bf16[2,384,512]{2,1,0:T(8,128)(2,1)} %collective-permute-done.14.refs_3_), channel_id=1, source_target_pairs={{0,24},{1,7},{2,26},{3,1},{4,28},{5,3},{6,30},{7,5},{8,0},{9,15},{... | collective-permute-start | bytes 2359304 | tf_op jit(solution)/shard_map/ppermute | solution.py:59
  56.8 4.0 %collective-permute-start.15 = (bf16[8,64,256]{2,1,0:T(8,128)(2,1)}, bf16[8,64,256]{2,1,0:T(8,128)(2,1)}, u32[]{:S(2)}, u32[]{:S(2)}) collective-permute-start(bf16[8,64,256]{2,1,0:T(8,128)(2,1)} %get-tuple-element.70), channel_id=1, source_target_pairs={{0,33},{1,224},{2,35},{3,226},{4,37},{5,228},{6,39},{7,230},{8,41}... | collective-permute-start | bytes 786440 | tf_op jit(solution)/shard_map/ppermute | solution.py:59
  62.0 4.1 %shard_map.80.refs_0_ = f32[2,384,256]{2,1,0:T(8,128)S(1)} custom-call(s32[6]{0:T(128)S(1)} %stack.94.block_ref, f32[2,384,256]{2,1,0:T(8,128)S(1)} %copy-done.1, bf16[2,384,512]{2,1,0:T(8,128)(2,1)} %pad_maximum_fusion.1.refs_1_, bf16[2,384,512]{2,1,0:T(8,128)(2,1)} %collective-permute-done.13.refs_2_, ...), custom_call_target="tpu_custom_call" | custom-call | tf_op jit(solution)/shard_map/pallas_call | solution.py:29
  67.0 3.4 %collective-permute-done.15.cross_ref = bf16[8,64,256]{2,1,0:T(8,128)(2,1)} collective-permute-done((bf16[8,64,256]{2,1,0:T(8,128)(2,1)}, bf16[8,64,256]{2,1,0:T(8,128)(2,1)}, u32[]{:S(2)}, u32[]{:S(2)}) %collective-permute-start.15) | collective-permute-done | bytes 262176 | tf_op jit(solution)/shard_map/ppermute | solution.py:59
  70.4 2.6 %shrink.1 = (f32[64,384]{1,0:T(8,128)S(1)}, f32[64,384]{1,0:T(8,128)}) custom-call(s32[256]{0:T(256)S(1)} %pad_add_fusion.table_ref, bf16[24,64,256]{2,1,0:T(8,128)(2,1)} %collective-permute-done.12.same_ref.refs_0_, bf16[8,64,256]{2,1,0:T(8,128)(2,1)} %collective-permute-done.15.cross_ref, ...), custom_call_target="tpu_custom_call" | custom-call | tf_op jit(solution)/shard_map/shrink/pallas_call | solution.py:29
  73.6 1.5 %collective-permute-done.16 = f32[64,384]{1,0:T(8,128)S(1)} collective-permute-done((f32[64,384]{1,0:T(8,128)}, f32[64,384]{1,0:T(8,128)S(1)}, u32[]{:S(2)}, u32[]{:S(2)}) %collective-permute-start.16) | collective-permute-done | bytes 98336 | tf_op jit(solution)/shard_map/shrink_sum/ppermute | solution.py:59
  76.3 2.4 %collective-permute-start.19 = (f32[64,384]{1,0:T(8,128)S(1)}, f32[64,384]{1,0:T(8,128)S(1)}, u32[]{:S(2)}, u32[]{:S(2)}) collective-permute-start(f32[64,384]{1,0:T(8,128)S(1)} %add.326), channel_id=1, source_target_pairs={{0,6},{1,7},{2,0},{3,1},{4,2},{5,3},{6,4},{7,5},{8,14},{9,15},{10,... | collective-permute-start | bytes 294920 | tf_op jit(solution)/shard_map/shrink_sum/ppermute | solution.py:59
  79.2 1.3 %shard_map.81 = (bf16[8,64,256]{2,1,0:T(8,128)(2,1)S(1)}, bf16[8,64,256]{2,1,0:T(8,128)(2,1)S(1)}) custom-call(s32[256]{0:T(256)S(1)} %pad_add_fusion.table_ref, bf16[24,64,256]{2,1,0:T(8,128)(2,1)} %collective-permute-done.12.same_ref.refs_0_, bf16[24,64,256]{2,1,0:T(8,128)(2,1)S(1)} %get-tuple-element.48.refs_0_.refs_1_.store_ref, ...), custom_call_target="tpu_custom_call" | custom-call | tf_op jit(solution)/shard_map/pallas_call | solution.py:29
  82.3 3.0 %collective-permute-start.23 = (bf16[8,64,256]{2,1,0:T(8,128)(2,1)S(1)}, bf16[8,64,256]{2,1,0:T(8,128)(2,1)S(1)}, u32[]{:S(2)}, u32[]{:S(2)}) collective-permute-start(bf16[8,64,256]{2,1,0:T(8,128)(2,1)S(1)} %get-tuple-element.82), channel_id=1, source_target_pairs={{0,33},{1,224},{2,35},{3,226},{4,37},{5,228},{6,39},{7,230},{8,41}... | collective-permute-start | bytes 786440 | tf_op jit(solution)/shard_map/ppermute | solution.py:59
  85.4 1.4 %collective-permute-start.24 = (f32[64,384]{1,0:T(8,128)S(1)}, f32[64,384]{1,0:T(8,128)S(1)}, u32[]{:S(2)}, u32[]{:S(2)}) collective-permute-start(f32[64,384]{1,0:T(8,128)S(1)} %add_add_fusion), channel_id=1, source_target_pairs={{0,8},{1,9},{2,10},{3,11},{4,12},{5,13},{6,14},{7,15},{8,16},{9,17... | collective-permute-start | bytes 294920 | tf_op jit(solution)/shard_map/shrink_sum/ppermute | solution.py:59
  86.8 1.5 %collective-permute-start.25 = (f32[64,384]{1,0:T(8,128)S(1)}, f32[64,384]{1,0:T(8,128)S(1)}, u32[]{:S(2)}, u32[]{:S(2)}) collective-permute-start(f32[64,384]{1,0:T(8,128)S(1)} %add_add_fusion), channel_id=1, source_target_pairs={{0,24},{1,25},{2,26},{3,27},{4,28},{5,29},{6,30},{7,31},{8,0},{9,1... | collective-permute-start | bytes 294920 | tf_op jit(solution)/shard_map/shrink_sum/ppermute | solution.py:59
  88.3 1.5 %collective-permute-start.26 = (f32[64,384]{1,0:T(8,128)S(1)}, f32[64,384]{1,0:T(8,128)S(1)}, u32[]{:S(2)}, u32[]{:S(2)}) collective-permute-start(f32[64,384]{1,0:T(8,128)S(1)} %add_add_fusion), channel_id=1, source_target_pairs={{0,16},{1,17},{2,18},{3,19},{4,20},{5,21},{6,22},{7,23},{8,24},{9,... | collective-permute-start | bytes 294920 | tf_op jit(solution)/shard_map/shrink_sum/ppermute | solution.py:59
  89.9 3.3 %shard_map.82 = f32[2,384,256]{2,1,0:T(8,128)S(1)} custom-call(s32[4]{0:T(128)S(1)} %pad_add_fusion.1.block_ref, f32[2,384,256]{2,1,0:T(8,128)S(1)} %copy-done.3, bf16[2,384,512]{2,1,0:T(8,128)(2,1)} %collective-permute-done.21.refs_1_, bf16[2,384,512]{2,1,0:T(8,128)(2,1)} %collective-permute-done.22.refs_2_, bf16[16,512,256]{2,1,0:T(8,128)(2,1)} %bitcast.10.refs_3_.refs_4_, ...), custom_call_target="tpu_custom_call" | custom-call | tf_op jit(solution)/shard_map/pallas_call | solution.py:29
  94.2 1.2 %collective-permute-start.28 = (f32[384,256]{1,0:T(8,128)S(1)}, f32[384,256]{1,0:T(8,128)S(1)}, u32[]{:S(2)}, u32[]{:S(2)}) collective-permute-start(f32[384,256]{1,0:T(8,128)S(1)} %get-tuple-element.86), channel_id=1, source_target_pairs={{0,1},{1,0},{2,3},{3,2},{4,5},{5,4},{6,7},{7,6},{8,9},{9,8},{10,11... | collective-permute-start | bytes 1179656 | tf_op jit(solution)/shard_map/base/ppermute | solution.py:59
  95.5 1.3 %collective-permute-done.27.other_ref = bf16[64,384]{1,0:T(8,128)(2,1)S(1)} collective-permute-done((bf16[64,384]{1,0:T(8,128)(2,1)S(1)}, bf16[64,384]{1,0:T(8,128)(2,1)S(1)}, u32[]{:S(2)}, u32[]{:S(2)}) %collective-permute-start.27) | collective-permute-done | bytes 49184 | tf_op jit(solution)/shard_map/shrink_sum/ppermute | solution.py:59
  (74 shorter events, 18.0 us)
Async XLA Ops:
  0.0 6.3 %collective-permute-start.1 = (bf16[24,64,256]{2,1,0:T(8,128)(2,1)}, bf16[24,64,256]{2,1,0:T(8,128)(2,1)S(1)}, u32[]{:S(2)}, u32[]{:S(2)}) collective-permute-start(bf16[24,64,256]{2,1,0:T(8,128)(2,1)} %refs_0_.1), channel_id=1, source_target_pairs={{0,1},{1,0},{2,3},{3,2},{4,5},{5,4},{6,7},{7,6},{8,9},{9,8},{10,11... | collective-permute-start | bytes 2359304 | tf_op jit(solution)/shard_map/ppermute | solution.py:59
  3.2 3.7 %collective-permute-start = (bf16[768,256]{1,0:T(8,128)(2,1)}, bf16[768,256]{1,0:T(8,128)(2,1)S(1)}, u32[]{:S(2)}, u32[]{:S(2)}) collective-permute-start(bf16[768,256]{1,0:T(8,128)(2,1)} %refs_2_.1), channel_id=1, source_target_pairs={{0,1},{1,0},{2,3},{3,2},{4,5},{5,4},{6,7},{7,6},{8,9},{9,8},{10,11... | collective-permute-start | bytes 1179656 | tf_op jit(solution)/shard_map/ppermute | solution.py:59
  4.0 3.7 %copy-start.9 = (bf16[24,64,256]{2,1,0:T(8,128)(2,1)S(1)}, bf16[24,64,256]{2,1,0:T(8,128)(2,1)}, u32[]{:S(2)}) copy-start(bf16[24,64,256]{2,1,0:T(8,128)(2,1)} %refs_1_.1) | copy-start | bytes 2359300
  7.2 35.5 %collective-permute-start.10 = (bf16[8192,256]{1,0:T(8,128)(2,1)}, bf16[8192,256]{1,0:T(8,128)(2,1)}, u32[]{:S(2)}, u32[]{:S(2)}) collective-permute-start(bf16[8192,256]{1,0:T(8,128)(2,1)} %param.8), channel_id=1, source_target_pairs={{0,1},{1,0},{2,3},{3,2},{4,5},{5,4},{6,7},{7,6},{8,9},{9,8},{10,11... | collective-permute-start | bytes 12582920 | tf_op jit(solution)/shard_map/ppermute | solution.py:59
  7.8 10.0 %collective-permute-start.4 = (bf16[24,64,256]{2,1,0:T(8,128)(2,1)S(1)}, bf16[24,64,256]{2,1,0:T(8,128)(2,1)S(1)}, u32[]{:S(2)}, u32[]{:S(2)}) collective-permute-start(bf16[24,64,256]{2,1,0:T(8,128)(2,1)S(1)} %copy-done.9), channel_id=1, source_target_pairs={{0,1},{1,0},{2,3},{3,2},{4,5},{5,4},{6,7},{7,6},{8,9},{9,8},{10,11... | collective-permute-start | bytes 2359304 | tf_op jit(solution)/shard_map/ppermute | solution.py:59
  7.9 9.9 %collective-permute-start.2 = (bf16[384,512]{1,0:T(8,128)(2,1)S(1)}, bf16[384,512]{1,0:T(8,128)(2,1)S(1)}, u32[]{:S(2)}, u32[]{:S(2)}) collective-permute-start(bf16[384,512]{1,0:T(8,128)(2,1)S(1)} %get-tuple-element.50), channel_id=1, source_target_pairs={{0,2},{1,9},{2,4},{3,11},{4,6},{5,13},{6,0},{7,15},{8,10},{9,17},{... | collective-permute-start | bytes 1179656 | tf_op jit(solution)/shard_map/ppermute | solution.py:59
  7.9 9.9 %collective-permute-start.3 = (bf16[384,512]{1,0:T(8,128)(2,1)S(1)}, bf16[384,512]{1,0:T(8,128)(2,1)S(1)}, u32[]{:S(2)}, u32[]{:S(2)}) collective-permute-start(bf16[384,512]{1,0:T(8,128)(2,1)S(1)} %get-tuple-element.50), channel_id=1, source_target_pairs={{0,6},{1,25},{2,0},{3,27},{4,2},{5,29},{6,4},{7,31},{8,14},{9,1},{... | collective-permute-start | bytes 1179656 | tf_op jit(solution)/shard_map/ppermute | solution.py:59
  10.5 7.2 %collective-permute-start.5 = (bf16[8,64,256]{2,1,0:T(8,128)(2,1)S(1)}, bf16[8,64,256]{2,1,0:T(8,128)(2,1)S(1)}, u32[]{:S(2)}, u32[]{:S(2)}) collective-permute-start(bf16[8,64,256]{2,1,0:T(8,128)(2,1)S(1)} %shard_map.74), channel_id=1, source_target_pairs={{0,32},{1,225},{2,34},{3,227},{4,36},{5,229},{6,38},{7,231},{8,40}... | collective-permute-start | bytes 786440 | tf_op jit(solution)/shard_map/ppermute | solution.py:59
  18.6 15.6 %collective-permute-start.9 = (bf16[24,64,256]{2,1,0:T(8,128)(2,1)S(1)}, bf16[24,64,256]{2,1,0:T(8,128)(2,1)S(1)}, u32[]{:S(2)}, u32[]{:S(2)}) collective-permute-start(bf16[24,64,256]{2,1,0:T(8,128)(2,1)S(1)} %shard_map.76), channel_id=1, source_target_pairs={{0,32},{1,225},{2,34},{3,227},{4,36},{5,229},{6,38},{7,231},{8,40}... | collective-permute-start | bytes 2359304 | tf_op jit(solution)/shard_map/ppermute | solution.py:59
  21.8 12.4 %collective-permute-start.8 = (bf16[384,512]{1,0:T(8,128)(2,1)S(1)}, bf16[384,512]{1,0:T(8,128)(2,1)S(1)}, u32[]{:S(2)}, u32[]{:S(2)}) collective-permute-start(bf16[384,512]{1,0:T(8,128)(2,1)S(1)} %collective-permute-done.2), channel_id=1, source_target_pairs={{0,2},{1,9},{2,4},{3,11},{4,6},{5,13},{6,0},{7,15},{8,10},{9,17},{... | collective-permute-start | bytes 1179656 | tf_op jit(solution)/shard_map/ppermute | solution.py:59
  22.2 15.9 %collective-permute-start.6 = (bf16[2,384,512]{2,1,0:T(8,128)(2,1)S(1)}, bf16[2,384,512]{2,1,0:T(8,128)(2,1)}, u32[]{:S(2)}, u32[]{:S(2)}) collective-permute-start(bf16[2,384,512]{2,1,0:T(8,128)(2,1)S(1)} %pad_maximum_fusion.refs_0_), channel_id=1, source_target_pairs={{0,8},{1,3},{2,10},{3,5},{4,12},{5,7},{6,14},{7,1},{8,16},{9,11},{... | collective-permute-start | bytes 2359304 | tf_op jit(solution)/shard_map/ppermute | solution.py:59
  23.5 14.6 %collective-permute-start.7 = (bf16[2,384,512]{2,1,0:T(8,128)(2,1)S(1)}, bf16[2,384,512]{2,1,0:T(8,128)(2,1)S(1)}, u32[]{:S(2)}, u32[]{:S(2)}) collective-permute-start(bf16[2,384,512]{2,1,0:T(8,128)(2,1)S(1)} %pad_maximum_fusion.refs_0_), channel_id=1, source_target_pairs={{0,24},{1,7},{2,26},{3,1},{4,28},{5,3},{6,30},{7,5},{8,0},{9,15},{... | collective-permute-start | bytes 2359304 | tf_op jit(solution)/shard_map/ppermute | solution.py:59
  36.0 14.3 %collective-permute-start.11 = (bf16[32,64,256]{2,1,0:T(8,128)(2,1)}, bf16[32,64,256]{2,1,0:T(8,128)(2,1)}, u32[]{:S(2)}, u32[]{:S(2)}) collective-permute-start(bf16[32,64,256]{2,1,0:T(8,128)(2,1)} %shard_map.77), channel_id=1, source_target_pairs={{0,32},{1,225},{2,34},{3,227},{4,36},{5,229},{6,38},{7,231},{8,40}... | collective-permute-start | bytes 3145736 | tf_op jit(solution)/shard_map/ppermute | solution.py:59
  39.9 15.3 %collective-permute-start.13 = (bf16[2,384,512]{2,1,0:T(8,128)(2,1)}, bf16[2,384,512]{2,1,0:T(8,128)(2,1)}, u32[]{:S(2)}, u32[]{:S(2)}) collective-permute-start(bf16[2,384,512]{2,1,0:T(8,128)(2,1)} %pad_maximum_fusion.1.refs_1_), channel_id=1, source_target_pairs={{0,8},{1,3},{2,10},{3,5},{4,12},{5,7},{6,14},{7,1},{8,16},{9,11},{... | collective-permute-start | bytes 2359304 | tf_op jit(solution)/shard_map/ppermute | solution.py:59
  39.9 15.3 %collective-permute-start.14 = (bf16[2,384,512]{2,1,0:T(8,128)(2,1)}, bf16[2,384,512]{2,1,0:T(8,128)(2,1)}, u32[]{:S(2)}, u32[]{:S(2)}) collective-permute-start(bf16[2,384,512]{2,1,0:T(8,128)(2,1)} %pad_maximum_fusion.1.refs_1_), channel_id=1, source_target_pairs={{0,24},{1,7},{2,26},{3,1},{4,28},{5,3},{6,30},{7,5},{8,0},{9,15},{... | collective-permute-start | bytes 2359304 | tf_op jit(solution)/shard_map/ppermute | solution.py:59
  50.0 10.8 %copy-start.10 = (s32[768]{0:T(1024)S(1)}, s32[768]{0:T(1024)}, u32[]{:S(2)}) copy-start(s32[768]{0:T(1024)} %param.13) | copy-start | bytes 9220
  52.7 14.3 %collective-permute-start.12 = (bf16[24,64,256]{2,1,0:T(8,128)(2,1)}, bf16[24,64,256]{2,1,0:T(8,128)(2,1)}, u32[]{:S(2)}, u32[]{:S(2)}) collective-permute-start(bf16[24,64,256]{2,1,0:T(8,128)(2,1)} %get-tuple-element.66), channel_id=1, source_target_pairs={{0,32},{1,225},{2,34},{3,227},{4,36},{5,229},{6,38},{7,231},{8,40}... | collective-permute-start | bytes 2359304 | tf_op jit(solution)/shard_map/ppermute | solution.py:59
  54.0 32.8 %collective-permute-start.21 = (bf16[2,384,512]{2,1,0:T(8,128)(2,1)}, bf16[2,384,512]{2,1,0:T(8,128)(2,1)}, u32[]{:S(2)}, u32[]{:S(2)}) collective-permute-start(bf16[2,384,512]{2,1,0:T(8,128)(2,1)} %collective-permute-done.6.refs_1_), channel_id=1, source_target_pairs={{0,8},{1,3},{2,10},{3,5},{4,12},{5,7},{6,14},{7,1},{8,16},{9,11},{... | collective-permute-start | bytes 2359304 | tf_op jit(solution)/shard_map/ppermute | solution.py:59
  55.2 33.1 %collective-permute-start.22 = (bf16[2,384,512]{2,1,0:T(8,128)(2,1)}, bf16[2,384,512]{2,1,0:T(8,128)(2,1)}, u32[]{:S(2)}, u32[]{:S(2)}) collective-permute-start(bf16[2,384,512]{2,1,0:T(8,128)(2,1)} %collective-permute-done.14.refs_3_), channel_id=1, source_target_pairs={{0,24},{1,7},{2,26},{3,1},{4,28},{5,3},{6,30},{7,5},{8,0},{9,15},{... | collective-permute-start | bytes 2359304 | tf_op jit(solution)/shard_map/ppermute | solution.py:59
  56.8 13.5 %collective-permute-start.15 = (bf16[8,64,256]{2,1,0:T(8,128)(2,1)}, bf16[8,64,256]{2,1,0:T(8,128)(2,1)}, u32[]{:S(2)}, u32[]{:S(2)}) collective-permute-start(bf16[8,64,256]{2,1,0:T(8,128)(2,1)} %get-tuple-element.70), channel_id=1, source_target_pairs={{0,33},{1,224},{2,35},{3,226},{4,37},{5,228},{6,39},{7,230},{8,41}... | collective-permute-start | bytes 786440 | tf_op jit(solution)/shard_map/ppermute | solution.py:59
  73.6 1.5 %collective-permute-start.16 = (f32[64,384]{1,0:T(8,128)}, f32[64,384]{1,0:T(8,128)S(1)}, u32[]{:S(2)}, u32[]{:S(2)}) collective-permute-start(f32[64,384]{1,0:T(8,128)} %get-tuple-element.73), channel_id=1, source_target_pairs={{0,1},{1,0},{2,3},{3,2},{4,5},{5,4},{6,7},{7,6},{8,9},{9,8},{10,11... | collective-permute-start | bytes 294920 | tf_op jit(solution)/shard_map/shrink_sum/ppermute | solution.py:59
  73.6 16.3 %copy-start.3 = (f32[2,384,256]{2,1,0:T(8,128)S(1)}, f32[2,384,256]{2,1,0:T(8,128)}, u32[]{:S(2)}) copy-start(f32[2,384,256]{2,1,0:T(8,128)} %copy-done.2) | copy-start | bytes 2359300
  76.0 5.5 %collective-permute-start.18 = (f32[64,384]{1,0:T(8,128)S(1)}, f32[64,384]{1,0:T(8,128)S(1)}, u32[]{:S(2)}, u32[]{:S(2)}) collective-permute-start(f32[64,384]{1,0:T(8,128)S(1)} %add.326), channel_id=1, source_target_pairs={{0,2},{1,3},{2,4},{3,5},{4,6},{5,7},{6,0},{7,1},{8,10},{9,11},{10,... | collective-permute-start | bytes 294920 | tf_op jit(solution)/shard_map/shrink_sum/ppermute | solution.py:59
  76.3 6.0 %collective-permute-start.19 = (f32[64,384]{1,0:T(8,128)S(1)}, f32[64,384]{1,0:T(8,128)S(1)}, u32[]{:S(2)}, u32[]{:S(2)}) collective-permute-start(f32[64,384]{1,0:T(8,128)S(1)} %add.326), channel_id=1, source_target_pairs={{0,6},{1,7},{2,0},{3,1},{4,2},{5,3},{6,4},{7,5},{8,14},{9,15},{10,... | collective-permute-start | bytes 294920 | tf_op jit(solution)/shard_map/shrink_sum/ppermute | solution.py:59
  78.7 6.6 %collective-permute-start.20 = (f32[64,384]{1,0:T(8,128)S(1)}, f32[64,384]{1,0:T(8,128)S(1)}, u32[]{:S(2)}, u32[]{:S(2)}) collective-permute-start(f32[64,384]{1,0:T(8,128)S(1)} %add.326), channel_id=1, source_target_pairs={{0,4},{1,5},{2,6},{3,7},{4,0},{5,1},{6,2},{7,3},{8,12},{9,13},{10,... | collective-permute-start | bytes 294920 | tf_op jit(solution)/shard_map/shrink_sum/ppermute | solution.py:59
  81.5 11.7 %collective-permute-start.17 = (bf16[8,64,256]{2,1,0:T(8,128)(2,1)S(1)}, bf16[8,64,256]{2,1,0:T(8,128)(2,1)S(1)}, u32[]{:S(2)}, u32[]{:S(2)}) collective-permute-start(bf16[8,64,256]{2,1,0:T(8,128)(2,1)S(1)} %get-tuple-element.76), channel_id=1, source_target_pairs={{0,32},{1,225},{2,34},{3,227},{4,36},{5,229},{6,38},{7,231},{8,40}... | collective-permute-start | bytes 786440 | tf_op jit(solution)/shard_map/ppermute | solution.py:59
  82.3 10.9 %collective-permute-start.23 = (bf16[8,64,256]{2,1,0:T(8,128)(2,1)S(1)}, bf16[8,64,256]{2,1,0:T(8,128)(2,1)S(1)}, u32[]{:S(2)}, u32[]{:S(2)}) collective-permute-start(bf16[8,64,256]{2,1,0:T(8,128)(2,1)S(1)} %get-tuple-element.82), channel_id=1, source_target_pairs={{0,33},{1,224},{2,35},{3,226},{4,37},{5,228},{6,39},{7,230},{8,41}... | collective-permute-start | bytes 786440 | tf_op jit(solution)/shard_map/ppermute | solution.py:59
  85.4 8.8 %collective-permute-start.24 = (f32[64,384]{1,0:T(8,128)S(1)}, f32[64,384]{1,0:T(8,128)S(1)}, u32[]{:S(2)}, u32[]{:S(2)}) collective-permute-start(f32[64,384]{1,0:T(8,128)S(1)} %add_add_fusion), channel_id=1, source_target_pairs={{0,8},{1,9},{2,10},{3,11},{4,12},{5,13},{6,14},{7,15},{8,16},{9,17... | collective-permute-start | bytes 294920 | tf_op jit(solution)/shard_map/shrink_sum/ppermute | solution.py:59
  86.8 7.4 %collective-permute-start.25 = (f32[64,384]{1,0:T(8,128)S(1)}, f32[64,384]{1,0:T(8,128)S(1)}, u32[]{:S(2)}, u32[]{:S(2)}) collective-permute-start(f32[64,384]{1,0:T(8,128)S(1)} %add_add_fusion), channel_id=1, source_target_pairs={{0,24},{1,25},{2,26},{3,27},{4,28},{5,29},{6,30},{7,31},{8,0},{9,1... | collective-permute-start | bytes 294920 | tf_op jit(solution)/shard_map/shrink_sum/ppermute | solution.py:59
  88.3 5.8 %collective-permute-start.26 = (f32[64,384]{1,0:T(8,128)S(1)}, f32[64,384]{1,0:T(8,128)S(1)}, u32[]{:S(2)}, u32[]{:S(2)}) collective-permute-start(f32[64,384]{1,0:T(8,128)S(1)} %add_add_fusion), channel_id=1, source_target_pairs={{0,16},{1,17},{2,18},{3,19},{4,20},{5,21},{6,22},{7,23},{8,24},{9,... | collective-permute-start | bytes 294920 | tf_op jit(solution)/shard_map/shrink_sum/ppermute | solution.py:59
  94.2 2.6 %collective-permute-start.28 = (f32[384,256]{1,0:T(8,128)S(1)}, f32[384,256]{1,0:T(8,128)S(1)}, u32[]{:S(2)}, u32[]{:S(2)}) collective-permute-start(f32[384,256]{1,0:T(8,128)S(1)} %get-tuple-element.86), channel_id=1, source_target_pairs={{0,1},{1,0},{2,3},{3,2},{4,5},{5,4},{6,7},{7,6},{8,9},{9,8},{10,11... | collective-permute-start | bytes 1179656 | tf_op jit(solution)/shard_map/base/ppermute | solution.py:59
  95.4 1.4 %collective-permute-start.27 = (bf16[64,384]{1,0:T(8,128)(2,1)S(1)}, bf16[64,384]{1,0:T(8,128)(2,1)S(1)}, u32[]{:S(2)}, u32[]{:S(2)}) collective-permute-start(bf16[64,384]{1,0:T(8,128)(2,1)S(1)} %multiply_convert_fusion.scaled_ref), channel_id=1, source_target_pairs={{0,1},{1,0},{2,3},{3,2},{4,5},{5,4},{6,7},{7,6},{8,9},{9,8},{10,11... | collective-permute-start | bytes 147464 | tf_op jit(solution)/shard_map/shrink_sum/ppermute | solution.py:59
  (8 other events, 7.6 us)

commit v3 on v2

--- a/solution.py
+++ b/solution.py
@@ -141,32 +141,31 @@
     lax.fori_loop(0, out_ref.shape[0], one, 0)
 
 
-def shrink_kernel(table_ref, same_ref, cross_ref, store_ref, turned_ref, slot_ref, keep_ref, give_ref, panels, parts):
-    wanted, rank, feats = panels.shape
-    half = turned_ref.shape[1] // 2
+def shrink_kernel(table_ref, here_ref, other_ref, mine_ref, sib_ref, turned_ref, slot_ref, out_ref, panels, parts):
+    rank, half = out_ref.shape
+    stored = mine_ref.shape[0]
     core = lax.rem(lax.axis_index("tensor"), 2)
+    group = lax.axis_index("adapter")
+    feats = mine_ref.shape[2]
 
     def one(j, carry):
-        panels[j] = joined(table_ref, j, same_ref, cross_ref, store_ref)
+        storage = slot_of(table_ref, group, j)
+        behind = lax.rem(group - storage // stored + NZ, NZ)
+        below = (behind < NZ // 2) | ((behind == NZ // 2) & (j < WANTED // 2))
+        at = jnp.clip(storage - group * stored, 0, stored - 1)
+        for side, store in enumerate((mine_ref, sib_ref)):
+            came = jnp.where(below == (core == 0), here_ref[side * WANTED + j], other_ref[(1 - side) * WANTED + j])
+            panels[j, :, side * feats : (side + 1) * feats] = jnp.where(behind == 0, store[at], came)
         return carry
 
-    lax.fori_loop(0, wanted, one, 0)
-    flat = panels[...].reshape(wanted * rank, feats)
+    lax.fori_loop(0, WANTED, one, 0, unroll=2)
+    flat = panels[...].reshape(WANTED * rank, 2 * feats)
     parts[...] = jnp.dot(flat, turned_ref[...], preferred_element_type=f32)
-    for side in range(2):
-        columns = slice(side * half, (side + 1) * half)
-        slot = slot_ref[:, columns]
-        total = jnp.zeros((rank, half), f32)
-        for j in range(wanted):
-            total = jnp.where(slot == j, parts[j * rank : (j + 1) * rank, columns], total)
-
-        @pl.when(core == side)
-        def _():
-            keep_ref[...] = total
-
-        @pl.when(core != side)
-        def _():
-            give_ref[...] = total
+    slot = slot_ref[:, pl.ds(pl.multiple_of(core * half, 128), half)]
+    total = jnp.zeros((rank, half), f32)
+    for j in range(WANTED):
+        total = jnp.where(slot == j, parts[j * rank : (j + 1) * rank, :], total)
+    out_ref[...] = total
 
 
 def base_kernel(block_ref, *refs):
@@ -225,7 +224,8 @@
     mine, got = hidden_ref[half, :], got_ref[half, :]
     out_ref[:, :feats] = jnp.where(core == 0, mine, got)
     out_ref[:, feats:] = jnp.where(core == 0, got, mine)
-    turned_ref[...] = hidden_ref[...].T
+    turned_ref[:feats, :] = mine.T
+    turned_ref[feats:, :] = got.T
 
 
 def after(value, *earlier):
@@ -296,7 +296,7 @@
     hop1 = along_z(ring1)
     own_piece, turned = kernel_call(
         own_kernel,
-        (jax.ShapeDtypeStruct((rows // 2, 2 * feats), bf16), jax.ShapeDtypeStruct((feats, rows), bf16)),
+        (jax.ShapeDtypeStruct((rows // 2, 2 * feats), bf16), jax.ShapeDtypeStruct((2 * feats, rows // 2), bf16)),
         hidden_rows, after(got, ring1),
     )
     below, above = along_first(own_piece, 1), along_first(own_piece, -1)
@@ -329,33 +329,35 @@
     rest_below, rest_above, near_beyond = along_second(rest, 1), along_second(rest, -1), along_second(near_below, 1)
     base = add_base(None, (after(near, rest), near_at, 0), (near_below, near_at, -1), (near_above, near_at, 1))
 
-    ring4, ring4_cross = step(
+    ring4, ring4_up = step(
         [
-            (0, 0, 1, all_of, (0, 0, all_of), (0, 0)), (0, 1, 1, all_of, (0, all_of, all_of), (1, 0)),
-            (1, 0, 2, all_of, (0, 2 * all_of, all_of), (0, all_of)),
-            (1, 1, 2, all_of, (0, 3 * all_of, all_of), (0, 2 * all_of)),
+            (0, 0, 1, all_of, (0, 0, all_of), (0, 0)), (0, 1, 1, all_of, (0, all_of, all_of), (0, all_of)),
+            (1, 0, 2, all_of, (0, 2 * all_of, all_of), (1, 0)), (1, 1, 2, all_of, (0, 3 * all_of, all_of), (1, all_of)),
         ],
-        (3 * all_of, all_of), [hop3], base,
-    )
-    hop4, down_cross = along_z(ring4), along_z(ring4_cross, 1)
+        (2 * all_of, 2 * all_of), [hop3], base,
+    )
+    hop4, hop4_up = along_z(ring4), along_z(ring4_up)
     rest_below, rest_above = after((rest_below, rest_above), ring4)
     rest_beyond = along_second(rest_above, -1)
-    base = add_base(base, (rest, rest_at, 0), (rest_below, rest_at, -1), (rest_above, rest_at, 1))
+    base = add_base(
+        base, (rest, rest_at, 0), (rest_below, rest_at, -1), (rest_above, rest_at, 1),
+    )
 
     with jax.named_scope("shrink"):
-        part = jax.ShapeDtypeStruct((rank, rows // 2), f32)
-        keep, give = kernel_call(
-            shrink_kernel, (part, part), table, after(hop4, base), down_cross, down_panels, turned, slot_row,
-            scratch=[pltpu.VMEM((wanted, rank, columns), bf16), pltpu.VMEM((wanted * rank, rows), f32)],
+        hop4 = after(hop4, base)
+        part = kernel_call(
+            shrink_kernel, jax.ShapeDtypeStruct((rank, rows // 2), f32),
+            table, hop4, to_sibling(hop4), down_panels, down_sib, turned, slot_row,
+            scratch=[pltpu.VMEM((wanted, rank, 2 * feats), bf16), pltpu.VMEM((wanted * rank, rows // 2), f32)],
         )
     with jax.named_scope("shrink_sum"):
-        part = keep + to_sibling(give)
+        part = after(part, near_beyond, rest_beyond)
         pieces = along_x(part, 1), along_x(part, -1), along_x(part, 2)
     up_to_same, up_to_cross = step(
         [
-            (1, 0, 1, all_of, (0, all_of, all_of), (0, 0)), (1, 1, 1, all_of, (0, 2 * all_of, all_of), (1, 0)),
+            (1, 0, 1, all_of, (0, 0, all_of), (0, 0)), (1, 1, 1, all_of, (0, all_of, all_of), (1, 0)),
         ],
-        (all_of, all_of), [hop4], part,
+        (all_of, all_of), [hop4_up], part,
     )
     up_same, up_cross = along_z(up_to_same), along_z(up_to_cross, 1)
     with jax.named_scope("shrink_sum"):

time: 98.4 us -> 96.8 us (0.984)
  waiting for transfers between devices: 21.1 us -> 22.2 us
    ppermute x29, waiting for transfers between devices: 21.1 us -> 22.2 us  [send(): return lax.ppermute(value, ('adapter', 'tensor'), pairs)]
    unnamed x23 -> x21, local copies, waits for them, and re-layouts: 8.32 us -> 7.79 us
  transfers between devices with their start and end apart: 29 -> 29, of which waited for: 8 -> 8; matrix products, arithmetic and copies ran while one was open for 4% -> 3% of each run, Pallas kernels for 24% -> 24%
where the time goes in v3:
time: 96.8 us; the launch traced here: 96.4 us
  starting transfers between devices  39.7 us (41%)
  Pallas kernels  23.4 us (24%)
  waiting for transfers between devices  22.2 us (23%)
  local copies, waits for them, and re-layouts  8.78 us (9%)
  other arithmetic  1.98 us (2%)
    ppermute x29, starting transfers between devices, send(): return lax.ppermute(value, ('adapter', 'tensor'), pairs)  39.7 us
    pallas_call x13, Pallas kernels, kernel_call(): pl.pallas_call(kernel, out_shape=out_shape, in_specs=specs, out_specs=jax...  23.4 us
    ppermute x29, waiting for transfers between devices, send(): return lax.ppermute(value, ('adapter', 'tensor'), pairs)  22.2 us
    unnamed x21, local copies, waits for them, and re-layouts  7.79 us
  transfers between devices with their start and end apart: 29, of which 8 were waited for; matrix products, arithmetic and copies ran while one was open for 3% of the time, Pallas kernels for 24%

profile of v3, /device:TPU:1, one launch (start us, length us, event | category | flops | bytes accessed | tf_op | source)
XLA Modules:
  0.0 96.4 jit_solution(17027343282783467978)
XLA Ops:
  0.0 3.2 %collective-permute-start.1 = (bf16[24,64,256]{2,1,0:T(8,128)(2,1)}, bf16[24,64,256]{2,1,0:T(8,128)(2,1)S(1)}, u32[]{:S(2)}, u32[]{:S(2)}) collective-permute-start(bf16[24,64,256]{2,1,0:T(8,128)(2,1)} %refs_0_.1), channel_id=1, source_target_pairs={{0,1},{1,0},{2,3},{3,2},{4,5},{5,4},{6,7},{7,6},{8,9},{9,8},{10,11... | collective-permute-start | bytes 2359304 | tf_op jit(solution)/shard_map/ppermute | solution.py:59
  4.0 1.6 %shard_map.73 = (bf16[24,64,256]{2,1,0:T(8,128)(2,1)S(1)}, bf16[24,64,256]{2,1,0:T(8,128)(2,1)S(1)}, bf16[768,256]{1,0:T(8,128)(2,1)S(1)}) custom-call(bf16[24,64,256]{2,1,0:T(8,128)(2,1)} %refs_0_.1, bf16[24,64,256]{2,1,0:T(8,128)(2,1)} %refs_1_.1, bf16[768,256]{1,0:T(8,128)(2,1)} %refs_2_.1), custom_call_target="tpu_custom_call" | custom-call | tf_op jit(solution)/shard_map/pallas_call | solution.py:29
  7.9 2.7 %collective-permute-start.3 = (bf16[384,512]{1,0:T(8,128)(2,1)S(1)}, bf16[384,512]{1,0:T(8,128)(2,1)S(1)}, u32[]{:S(2)}, u32[]{:S(2)}) collective-permute-start(bf16[384,512]{1,0:T(8,128)(2,1)S(1)} %get-tuple-element.49), channel_id=1, source_target_pairs={{0,6},{1,25},{2,0},{3,27},{4,2},{5,29},{6,4},{7,31},{8,14},{9,1},{... | collective-permute-start | bytes 1179656 | tf_op jit(solution)/shard_map/ppermute | solution.py:59
  10.6 3.9 %collective-permute-start.5 = (bf16[8,64,256]{2,1,0:T(8,128)(2,1)S(1)}, bf16[8,64,256]{2,1,0:T(8,128)(2,1)S(1)}, u32[]{:S(2)}, u32[]{:S(2)}) collective-permute-start(bf16[8,64,256]{2,1,0:T(8,128)(2,1)S(1)} %shard_map.74), channel_id=1, source_target_pairs={{0,32},{1,225},{2,34},{3,227},{4,36},{5,229},{6,38},{7,231},{8,40}... | collective-permute-start | bytes 786440 | tf_op jit(solution)/shard_map/ppermute | solution.py:59
  14.5 3.3 %collective-permute-done.5.refs_0_ = bf16[8,64,256]{2,1,0:T(8,128)(2,1)S(1)} collective-permute-done((bf16[8,64,256]{2,1,0:T(8,128)(2,1)S(1)}, bf16[8,64,256]{2,1,0:T(8,128)(2,1)S(1)}, u32[]{:S(2)}, u32[]{:S(2)}) %collective-permute-start.5) | collective-permute-done | bytes 262176 | tf_op jit(solution)/shard_map/ppermute | solution.py:59
  18.6 3.2 %collective-permute-start.9 = (bf16[24,64,256]{2,1,0:T(8,128)(2,1)S(1)}, bf16[24,64,256]{2,1,0:T(8,128)(2,1)S(1)}, u32[]{:S(2)}, u32[]{:S(2)}) collective-permute-start(bf16[24,64,256]{2,1,0:T(8,128)(2,1)S(1)} %shard_map.76), channel_id=1, source_target_pairs={{0,32},{1,225},{2,34},{3,227},{4,36},{5,229},{6,38},{7,231},{8,40}... | collective-permute-start | bytes 2359304 | tf_op jit(solution)/shard_map/ppermute | solution.py:59
  21.8 1.3 %collective-permute-start.6 = (bf16[2,384,512]{2,1,0:T(8,128)(2,1)S(1)}, bf16[2,384,512]{2,1,0:T(8,128)(2,1)}, u32[]{:S(2)}, u32[]{:S(2)}) collective-permute-start(bf16[2,384,512]{2,1,0:T(8,128)(2,1)S(1)} %pad_maximum_fusion.refs_0_), channel_id=1, source_target_pairs={{0,8},{1,3},{2,10},{3,5},{4,12},{5,7},{6,14},{7,1},{8,16},{9,11},{... | collective-permute-start | bytes 2359304 | tf_op jit(solution)/shard_map/ppermute | solution.py:59
  23.1 1.7 %collective-permute-start.7 = (bf16[2,384,512]{2,1,0:T(8,128)(2,1)S(1)}, bf16[2,384,512]{2,1,0:T(8,128)(2,1)S(1)}, u32[]{:S(2)}, u32[]{:S(2)}) collective-permute-start(bf16[2,384,512]{2,1,0:T(8,128)(2,1)S(1)} %pad_maximum_fusion.refs_0_), channel_id=1, source_target_pairs={{0,24},{1,7},{2,26},{3,1},{4,28},{5,3},{6,30},{7,5},{8,0},{9,15},{... | collective-permute-start | bytes 2359304 | tf_op jit(solution)/shard_map/ppermute | solution.py:59
  25.8 12.3 %collective-permute-done.8 = bf16[384,512]{1,0:T(8,128)(2,1)S(1)} collective-permute-done((bf16[384,512]{1,0:T(8,128)(2,1)S(1)}, bf16[384,512]{1,0:T(8,128)(2,1)S(1)}, u32[]{:S(2)}, u32[]{:S(2)}) %collective-permute-start.8) | collective-permute-done | bytes 393248 | tf_op jit(solution)/shard_map/ppermute | solution.py:59
  38.1 1.9 %shard_map.77 = bf16[32,64,256]{2,1,0:T(8,128)(2,1)} custom-call(s32[256]{0:T(256)S(1)} %pad_add_fusion.table_ref, bf16[24,64,256]{2,1,0:T(8,128)(2,1)S(1)} %collective-permute-done.9.refs_0_, bf16[24,64,256]{2,1,0:T(8,128)(2,1)S(1)} %get-tuple-element.47.refs_0_.refs_1_.mine_ref, bf16[24,64,256]{2,1,0:T(8,128)(2,1)S(1)} %collective-permute-done.1.refs_1_.refs_2_.sib_ref, ...), custom_call_target="tpu_custom_call" | custom-call | tf_op jit(solution)/shard_map/pallas_call | solution.py:29
  41.0 1.0 %pad_maximum_fusion.1.refs_1_ = bf16[2,384,512]{2,1,0:T(8,128)(2,1)} fusion(bf16[1,384,512]{2,1,0:T(8,128)(2,1)S(1)} %bitcast.29, bf16[1,384,512]{2,1,0:T(8,128)(2,1)S(1)} %bitcast.27), kind=kLoop, calls=%fused_computation.1 | loop fusion | flops 393216 | bytes 1572864 | tf_op jit(solution)/shard_map/stack | solution.py:328
  42.0 2.7 %collective-permute-start.14 = (bf16[2,384,512]{2,1,0:T(8,128)(2,1)}, bf16[2,384,512]{2,1,0:T(8,128)(2,1)}, u32[]{:S(2)}, u32[]{:S(2)}) collective-permute-start(bf16[2,384,512]{2,1,0:T(8,128)(2,1)} %pad_maximum_fusion.1.refs_1_), channel_id=1, source_target_pairs={{0,24},{1,7},{2,26},{3,1},{4,28},{5,3},{6,30},{7,5},{8,0},{9,15},{... | collective-permute-start | bytes 2359304 | tf_op jit(solution)/shard_map/ppermute | solution.py:59
  44.7 1.1 %copy-done.5 = bf16[2,384,512]{2,1,0:T(8,128)(2,1)S(1)} copy-done((bf16[2,384,512]{2,1,0:T(8,128)(2,1)S(1)}, bf16[2,384,512]{2,1,0:T(8,128)(2,1)}, u32[]{:S(2)}) %copy-start.5) | copy-done | bytes 786456
  45.9 1.1 %copy-done.7 = bf16[2,384,512]{2,1,0:T(8,128)(2,1)S(1)} copy-done((bf16[2,384,512]{2,1,0:T(8,128)(2,1)S(1)}, bf16[2,384,512]{2,1,0:T(8,128)(2,1)}, u32[]{:S(2)}) %copy-start.7) | copy-done | bytes 786456
  47.0 4.2 %shard_map.78.refs_0_ = f32[2,384,256]{2,1,0:T(8,128)S(1)} custom-call(s32[6]{0:T(128)S(1)} %stack.81.block_ref, bf16[2,384,512]{2,1,0:T(8,128)(2,1)S(1)} %copy-done.5, bf16[2,384,512]{2,1,0:T(8,128)(2,1)} %collective-permute-done.6.refs_1_, bf16[2,384,512]{2,1,0:T(8,128)(2,1)S(1)} %copy-done.7, bf16[16,512,256]{2,1,0:T(8,128)(2,1)} %bitcast.10.refs_3_.refs_4_, ...), custom_call_target="tpu_custom_call" | custom-call | tf_op jit(solution)/shard_map/pallas_call | solution.py:29
  52.1 2.2 %collective-permute-done.11.refs_0_ = bf16[32,64,256]{2,1,0:T(8,128)(2,1)} collective-permute-done((bf16[32,64,256]{2,1,0:T(8,128)(2,1)}, bf16[32,64,256]{2,1,0:T(8,128)(2,1)}, u32[]{:S(2)}, u32[]{:S(2)}) %collective-permute-start.11) | collective-permute-done | bytes 1048608 | tf_op jit(solution)/shard_map/ppermute | solution.py:59
  54.2 2.5 %shard_map.79 = (bf16[16,64,256]{2,1,0:T(8,128)(2,1)}, bf16[16,64,256]{2,1,0:T(8,128)(2,1)}) custom-call(s32[256]{0:T(256)S(1)} %pad_add_fusion.table_ref, bf16[32,64,256]{2,1,0:T(8,128)(2,1)} %collective-permute-done.11.refs_0_, bf16[24,64,256]{2,1,0:T(8,128)(2,1)S(1)} %get-tuple-element.47.refs_0_.refs_1_.mine_ref, ...), custom_call_target="tpu_custom_call" | custom-call | tf_op jit(solution)/shard_map/pallas_call | solution.py:29
  56.7 1.3 %collective-permute-start.12 = (bf16[16,64,256]{2,1,0:T(8,128)(2,1)}, bf16[16,64,256]{2,1,0:T(8,128)(2,1)}, u32[]{:S(2)}, u32[]{:S(2)}) collective-permute-start(bf16[16,64,256]{2,1,0:T(8,128)(2,1)} %get-tuple-element.65), channel_id=1, source_target_pairs={{0,32},{1,225},{2,34},{3,227},{4,36},{5,229},{6,38},{7,231},{8,40}... | collective-permute-start | bytes 1572872 | tf_op jit(solution)/shard_map/ppermute | solution.py:59
  58.0 2.7 %collective-permute-start.17 = (bf16[2,384,512]{2,1,0:T(8,128)(2,1)}, bf16[2,384,512]{2,1,0:T(8,128)(2,1)}, u32[]{:S(2)}, u32[]{:S(2)}) collective-permute-start(bf16[2,384,512]{2,1,0:T(8,128)(2,1)} %collective-permute-done.14.refs_3_), channel_id=1, source_target_pairs={{0,24},{1,7},{2,26},{3,1},{4,28},{5,3},{6,30},{7,5},{8,0},{9,15},{... | collective-permute-start | bytes 2359304 | tf_op jit(solution)/shard_map/ppermute | solution.py:59
  60.8 1.1 %copy-done.1 = f32[2,384,256]{2,1,0:T(8,128)S(1)} copy-done((f32[2,384,256]{2,1,0:T(8,128)S(1)}, f32[2,384,256]{2,1,0:T(8,128)}, u32[]{:S(2)}) %copy-start.1) | copy-done | bytes 786456
  61.9 4.1 %shard_map.80.refs_0_ = f32[2,384,256]{2,1,0:T(8,128)S(1)} custom-call(s32[6]{0:T(128)S(1)} %stack.94.block_ref, f32[2,384,256]{2,1,0:T(8,128)S(1)} %copy-done.1, bf16[2,384,512]{2,1,0:T(8,128)(2,1)} %pad_maximum_fusion.1.refs_1_, bf16[2,384,512]{2,1,0:T(8,128)(2,1)} %collective-permute-done.13.refs_2_, ...), custom_call_target="tpu_custom_call" | custom-call | tf_op jit(solution)/shard_map/pallas_call | solution.py:29
  67.0 2.8 %collective-permute-start.15 = (bf16[16,64,256]{2,1,0:T(8,128)(2,1)}, bf16[16,64,256]{2,1,0:T(8,128)(2,1)}, u32[]{:S(2)}, u32[]{:S(2)}) collective-permute-start(bf16[16,64,256]{2,1,0:T(8,128)(2,1)} %collective-permute-done.12.here_ref), channel_id=1, source_target_pairs={{0,1},{1,0},{2,3},{3,2},{4,5},{5,4},{6,7},{7,6},{8,9},{9,8},{10,11... | collective-permute-start | bytes 1572872 | tf_op jit(solution)/shard_map/shrink/ppermute | solution.py:59
  69.8 1.8 %collective-permute-start.18 = (bf16[16,64,256]{2,1,0:T(8,128)(2,1)}, bf16[16,64,256]{2,1,0:T(8,128)(2,1)}, u32[]{:S(2)}, u32[]{:S(2)}) collective-permute-start(bf16[16,64,256]{2,1,0:T(8,128)(2,1)} %get-tuple-element.72), channel_id=1, source_target_pairs={{0,32},{1,225},{2,34},{3,227},{4,36},{5,229},{6,38},{7,231},{8,40}... | collective-permute-start | bytes 1572872 | tf_op jit(solution)/shard_map/ppermute | solution.py:59
  71.7 1.9 %shrink.1 = f32[64,384]{1,0:T(8,128)S(1)} custom-call(s32[256]{0:T(256)S(1)} %pad_add_fusion.table_ref, bf16[16,64,256]{2,1,0:T(8,128)(2,1)} %collective-permute-done.12.here_ref, bf16[16,64,256]{2,1,0:T(8,128)(2,1)} %collective-permute-done.15.other_ref, bf16[24,64,256]{2,1,0:T(8,128)(2,1)S(1)} %get-tuple-element.47.refs_0_.refs_1_.mine_ref, ...), custom_call_target="tpu_custom_call" | custom-call | tf_op jit(solution)/shard_map/shrink/pallas_call | solution.py:29
  73.7 2.7 %collective-permute-start.21 = (f32[64,384]{1,0:T(8,128)S(1)}, f32[64,384]{1,0:T(8,128)S(1)}, u32[]{:S(2)}, u32[]{:S(2)}) collective-permute-start(f32[64,384]{1,0:T(8,128)S(1)} %shrink.1), channel_id=1, source_target_pairs={{0,6},{1,7},{2,0},{3,1},{4,2},{5,3},{6,4},{7,5},{8,14},{9,15},{10,... | collective-permute-start | bytes 294920 | tf_op jit(solution)/shard_map/shrink_sum/ppermute | solution.py:59
  76.5 2.0 %collective-permute-done.18.refs_0_ = bf16[16,64,256]{2,1,0:T(8,128)(2,1)} collective-permute-done((bf16[16,64,256]{2,1,0:T(8,128)(2,1)}, bf16[16,64,256]{2,1,0:T(8,128)(2,1)}, u32[]{:S(2)}, u32[]{:S(2)}) %collective-permute-start.18) | collective-permute-done | bytes 524320 | tf_op jit(solution)/shard_map/ppermute | solution.py:59
  78.5 1.2 %shard_map.81 = (bf16[8,64,256]{2,1,0:T(8,128)(2,1)S(1)}, bf16[8,64,256]{2,1,0:T(8,128)(2,1)S(1)}) custom-call(s32[256]{0:T(256)S(1)} %pad_add_fusion.table_ref, bf16[16,64,256]{2,1,0:T(8,128)(2,1)} %collective-permute-done.18.refs_0_, bf16[24,64,256]{2,1,0:T(8,128)(2,1)S(1)} %get-tuple-element.47.refs_0_.refs_1_.mine_ref, ...), custom_call_target="tpu_custom_call" | custom-call | tf_op jit(solution)/shard_map/pallas_call | solution.py:29
  79.7 3.0 %collective-permute-start.19 = (bf16[8,64,256]{2,1,0:T(8,128)(2,1)S(1)}, bf16[8,64,256]{2,1,0:T(8,128)(2,1)S(1)}, u32[]{:S(2)}, u32[]{:S(2)}) collective-permute-start(bf16[8,64,256]{2,1,0:T(8,128)(2,1)S(1)} %get-tuple-element.74), channel_id=1, source_target_pairs={{0,32},{1,225},{2,34},{3,227},{4,36},{5,229},{6,38},{7,231},{8,40}... | collective-permute-start | bytes 786440 | tf_op jit(solution)/shard_map/ppermute | solution.py:59
  82.6 2.0 %collective-permute-start.23 = (bf16[8,64,256]{2,1,0:T(8,128)(2,1)S(1)}, bf16[8,64,256]{2,1,0:T(8,128)(2,1)S(1)}, u32[]{:S(2)}, u32[]{:S(2)}) collective-permute-start(bf16[8,64,256]{2,1,0:T(8,128)(2,1)S(1)} %get-tuple-element.80), channel_id=1, source_target_pairs={{0,33},{1,224},{2,35},{3,226},{4,37},{5,228},{6,39},{7,230},{8,41}... | collective-permute-start | bytes 786440 | tf_op jit(solution)/shard_map/ppermute | solution.py:59
  84.9 2.6 %collective-permute-start.25 = (f32[64,384]{1,0:T(8,128)S(1)}, f32[64,384]{1,0:T(8,128)S(1)}, u32[]{:S(2)}, u32[]{:S(2)}) collective-permute-start(f32[64,384]{1,0:T(8,128)S(1)} %add_add_fusion), channel_id=1, source_target_pairs={{0,24},{1,25},{2,26},{3,27},{4,28},{5,29},{6,30},{7,31},{8,0},{9,1... | collective-permute-start | bytes 294920 | tf_op jit(solution)/shard_map/shrink_sum/ppermute | solution.py:59
  87.9 3.3 %shard_map.82 = f32[2,384,256]{2,1,0:T(8,128)S(1)} custom-call(s32[4]{0:T(128)S(1)} %pad_add_fusion.1.block_ref, f32[2,384,256]{2,1,0:T(8,128)S(1)} %copy-done.3, bf16[2,384,512]{2,1,0:T(8,128)(2,1)} %collective-permute-done.16.refs_1_, bf16[2,384,512]{2,1,0:T(8,128)(2,1)} %collective-permute-done.17.refs_2_, bf16[16,512,256]{2,1,0:T(8,128)(2,1)} %bitcast.10.refs_3_.refs_4_, ...), custom_call_target="tpu_custom_call" | custom-call | tf_op jit(solution)/shard_map/pallas_call | solution.py:29
  93.9 1.3 %collective-permute-done.27.other_ref = bf16[64,384]{1,0:T(8,128)(2,1)S(1)} collective-permute-done((bf16[64,384]{1,0:T(8,128)(2,1)S(1)}, bf16[64,384]{1,0:T(8,128)(2,1)S(1)}, u32[]{:S(2)}, u32[]{:S(2)}) %collective-permute-start.27) | collective-permute-done | bytes 49184 | tf_op jit(solution)/shard_map/shrink_sum/ppermute | solution.py:59
  (71 shorter events, 12.7 us)
Async XLA Ops:
  0.0 6.3 %collective-permute-start.1 = (bf16[24,64,256]{2,1,0:T(8,128)(2,1)}, bf16[24,64,256]{2,1,0:T(8,128)(2,1)S(1)}, u32[]{:S(2)}, u32[]{:S(2)}) collective-permute-start(bf16[24,64,256]{2,1,0:T(8,128)(2,1)} %refs_0_.1), channel_id=1, source_target_pairs={{0,1},{1,0},{2,3},{3,2},{4,5},{5,4},{6,7},{7,6},{8,9},{9,8},{10,11... | collective-permute-start | bytes 2359304 | tf_op jit(solution)/shard_map/ppermute | solution.py:59
  3.2 3.7 %collective-permute-start = (bf16[768,256]{1,0:T(8,128)(2,1)}, bf16[768,256]{1,0:T(8,128)(2,1)S(1)}, u32[]{:S(2)}, u32[]{:S(2)}) collective-permute-start(bf16[768,256]{1,0:T(8,128)(2,1)} %refs_2_.1), channel_id=1, source_target_pairs={{0,1},{1,0},{2,3},{3,2},{4,5},{5,4},{6,7},{7,6},{8,9},{9,8},{10,11... | collective-permute-start | bytes 1179656 | tf_op jit(solution)/shard_map/ppermute | solution.py:59
  4.0 3.8 %copy-start.8 = (bf16[24,64,256]{2,1,0:T(8,128)(2,1)S(1)}, bf16[24,64,256]{2,1,0:T(8,128)(2,1)}, u32[]{:S(2)}) copy-start(bf16[24,64,256]{2,1,0:T(8,128)(2,1)} %refs_1_.1) | copy-start | bytes 2359300
  7.2 37.6 %collective-permute-start.10 = (bf16[8192,256]{1,0:T(8,128)(2,1)}, bf16[8192,256]{1,0:T(8,128)(2,1)}, u32[]{:S(2)}, u32[]{:S(2)}) collective-permute-start(bf16[8192,256]{1,0:T(8,128)(2,1)} %param.8), channel_id=1, source_target_pairs={{0,1},{1,0},{2,3},{3,2},{4,5},{5,4},{6,7},{7,6},{8,9},{9,8},{10,11... | collective-permute-start | bytes 12582920 | tf_op jit(solution)/shard_map/ppermute | solution.py:59
  7.8 10.0 %collective-permute-start.4 = (bf16[24,64,256]{2,1,0:T(8,128)(2,1)S(1)}, bf16[24,64,256]{2,1,0:T(8,128)(2,1)S(1)}, u32[]{:S(2)}, u32[]{:S(2)}) collective-permute-start(bf16[24,64,256]{2,1,0:T(8,128)(2,1)S(1)} %copy-done.8), channel_id=1, source_target_pairs={{0,1},{1,0},{2,3},{3,2},{4,5},{5,4},{6,7},{7,6},{8,9},{9,8},{10,11... | collective-permute-start | bytes 2359304 | tf_op jit(solution)/shard_map/ppermute | solution.py:59
  7.9 9.9 %collective-permute-start.2 = (bf16[384,512]{1,0:T(8,128)(2,1)S(1)}, bf16[384,512]{1,0:T(8,128)(2,1)S(1)}, u32[]{:S(2)}, u32[]{:S(2)}) collective-permute-start(bf16[384,512]{1,0:T(8,128)(2,1)S(1)} %get-tuple-element.49), channel_id=1, source_target_pairs={{0,2},{1,9},{2,4},{3,11},{4,6},{5,13},{6,0},{7,15},{8,10},{9,17},{... | collective-permute-start | bytes 1179656 | tf_op jit(solution)/shard_map/ppermute | solution.py:59
  7.9 9.9 %collective-permute-start.3 = (bf16[384,512]{1,0:T(8,128)(2,1)S(1)}, bf16[384,512]{1,0:T(8,128)(2,1)S(1)}, u32[]{:S(2)}, u32[]{:S(2)}) collective-permute-start(bf16[384,512]{1,0:T(8,128)(2,1)S(1)} %get-tuple-element.49), channel_id=1, source_target_pairs={{0,6},{1,25},{2,0},{3,27},{4,2},{5,29},{6,4},{7,31},{8,14},{9,1},{... | collective-permute-start | bytes 1179656 | tf_op jit(solution)/shard_map/ppermute | solution.py:59
  10.6 7.2 %collective-permute-start.5 = (bf16[8,64,256]{2,1,0:T(8,128)(2,1)S(1)}, bf16[8,64,256]{2,1,0:T(8,128)(2,1)S(1)}, u32[]{:S(2)}, u32[]{:S(2)}) collective-permute-start(bf16[8,64,256]{2,1,0:T(8,128)(2,1)S(1)} %shard_map.74), channel_id=1, source_target_pairs={{0,32},{1,225},{2,34},{3,227},{4,36},{5,229},{6,38},{7,231},{8,40}... | collective-permute-start | bytes 786440 | tf_op jit(solution)/shard_map/ppermute | solution.py:59
  18.6 19.5 %collective-permute-start.9 = (bf16[24,64,256]{2,1,0:T(8,128)(2,1)S(1)}, bf16[24,64,256]{2,1,0:T(8,128)(2,1)S(1)}, u32[]{:S(2)}, u32[]{:S(2)}) collective-permute-start(bf16[24,64,256]{2,1,0:T(8,128)(2,1)S(1)} %shard_map.76), channel_id=1, source_target_pairs={{0,32},{1,225},{2,34},{3,227},{4,36},{5,229},{6,38},{7,231},{8,40}... | collective-permute-start | bytes 2359304 | tf_op jit(solution)/shard_map/ppermute | solution.py:59
  21.8 18.2 %collective-permute-start.6 = (bf16[2,384,512]{2,1,0:T(8,128)(2,1)S(1)}, bf16[2,384,512]{2,1,0:T(8,128)(2,1)}, u32[]{:S(2)}, u32[]{:S(2)}) collective-permute-start(bf16[2,384,512]{2,1,0:T(8,128)(2,1)S(1)} %pad_maximum_fusion.refs_0_), channel_id=1, source_target_pairs={{0,8},{1,3},{2,10},{3,5},{4,12},{5,7},{6,14},{7,1},{8,16},{9,11},{... | collective-permute-start | bytes 2359304 | tf_op jit(solution)/shard_map/ppermute | solution.py:59
  23.1 16.9 %collective-permute-start.7 = (bf16[2,384,512]{2,1,0:T(8,128)(2,1)S(1)}, bf16[2,384,512]{2,1,0:T(8,128)(2,1)S(1)}, u32[]{:S(2)}, u32[]{:S(2)}) collective-permute-start(bf16[2,384,512]{2,1,0:T(8,128)(2,1)S(1)} %pad_maximum_fusion.refs_0_), channel_id=1, source_target_pairs={{0,24},{1,7},{2,26},{3,1},{4,28},{5,3},{6,30},{7,5},{8,0},{9,15},{... | collective-permute-start | bytes 2359304 | tf_op jit(solution)/shard_map/ppermute | solution.py:59
  25.7 12.4 %collective-permute-start.8 = (bf16[384,512]{1,0:T(8,128)(2,1)S(1)}, bf16[384,512]{1,0:T(8,128)(2,1)S(1)}, u32[]{:S(2)}, u32[]{:S(2)}) collective-permute-start(bf16[384,512]{1,0:T(8,128)(2,1)S(1)} %collective-permute-done.2), channel_id=1, source_target_pairs={{0,2},{1,9},{2,4},{3,11},{4,6},{5,13},{6,0},{7,15},{8,10},{9,17},{... | collective-permute-start | bytes 1179656 | tf_op jit(solution)/shard_map/ppermute | solution.py:59
  40.0 14.3 %collective-permute-start.11 = (bf16[32,64,256]{2,1,0:T(8,128)(2,1)}, bf16[32,64,256]{2,1,0:T(8,128)(2,1)}, u32[]{:S(2)}, u32[]{:S(2)}) collective-permute-start(bf16[32,64,256]{2,1,0:T(8,128)(2,1)} %shard_map.77), channel_id=1, source_target_pairs={{0,32},{1,225},{2,34},{3,227},{4,36},{5,229},{6,38},{7,231},{8,40}... | collective-permute-start | bytes 3145736 | tf_op jit(solution)/shard_map/ppermute | solution.py:59
  42.0 16.1 %collective-permute-start.13 = (bf16[2,384,512]{2,1,0:T(8,128)(2,1)}, bf16[2,384,512]{2,1,0:T(8,128)(2,1)}, u32[]{:S(2)}, u32[]{:S(2)}) collective-permute-start(bf16[2,384,512]{2,1,0:T(8,128)(2,1)} %pad_maximum_fusion.1.refs_1_), channel_id=1, source_target_pairs={{0,8},{1,3},{2,10},{3,5},{4,12},{5,7},{6,14},{7,1},{8,16},{9,11},{... | collective-permute-start | bytes 2359304 | tf_op jit(solution)/shard_map/ppermute | solution.py:59
  42.0 16.1 %collective-permute-start.14 = (bf16[2,384,512]{2,1,0:T(8,128)(2,1)}, bf16[2,384,512]{2,1,0:T(8,128)(2,1)}, u32[]{:S(2)}, u32[]{:S(2)}) collective-permute-start(bf16[2,384,512]{2,1,0:T(8,128)(2,1)} %pad_maximum_fusion.1.refs_1_), channel_id=1, source_target_pairs={{0,24},{1,7},{2,26},{3,1},{4,28},{5,3},{6,30},{7,5},{8,0},{9,15},{... | collective-permute-start | bytes 2359304 | tf_op jit(solution)/shard_map/ppermute | solution.py:59
  56.7 10.3 %collective-permute-start.12 = (bf16[16,64,256]{2,1,0:T(8,128)(2,1)}, bf16[16,64,256]{2,1,0:T(8,128)(2,1)}, u32[]{:S(2)}, u32[]{:S(2)}) collective-permute-start(bf16[16,64,256]{2,1,0:T(8,128)(2,1)} %get-tuple-element.65), channel_id=1, source_target_pairs={{0,32},{1,225},{2,34},{3,227},{4,36},{5,229},{6,38},{7,231},{8,40}... | collective-permute-start | bytes 1572872 | tf_op jit(solution)/shard_map/ppermute | solution.py:59
  58.0 15.6 %collective-permute-start.16 = (bf16[2,384,512]{2,1,0:T(8,128)(2,1)}, bf16[2,384,512]{2,1,0:T(8,128)(2,1)}, u32[]{:S(2)}, u32[]{:S(2)}) collective-permute-start(bf16[2,384,512]{2,1,0:T(8,128)(2,1)} %collective-permute-done.6.refs_1_), channel_id=1, source_target_pairs={{0,8},{1,3},{2,10},{3,5},{4,12},{5,7},{6,14},{7,1},{8,16},{9,11},{... | collective-permute-start | bytes 2359304 | tf_op jit(solution)/shard_map/ppermute | solution.py:59
  58.0 15.6 %collective-permute-start.17 = (bf16[2,384,512]{2,1,0:T(8,128)(2,1)}, bf16[2,384,512]{2,1,0:T(8,128)(2,1)}, u32[]{:S(2)}, u32[]{:S(2)}) collective-permute-start(bf16[2,384,512]{2,1,0:T(8,128)(2,1)} %collective-permute-done.14.refs_3_), channel_id=1, source_target_pairs={{0,24},{1,7},{2,26},{3,1},{4,28},{5,3},{6,30},{7,5},{8,0},{9,15},{... | collective-permute-start | bytes 2359304 | tf_op jit(solution)/shard_map/ppermute | solution.py:59
  61.9 9.7 %copy-start.9 = (s32[768]{0:T(1024)S(1)}, s32[768]{0:T(1024)}, u32[]{:S(2)}) copy-start(s32[768]{0:T(1024)} %param.13) | copy-start | bytes 9220
  67.0 4.7 %collective-permute-start.15 = (bf16[16,64,256]{2,1,0:T(8,128)(2,1)}, bf16[16,64,256]{2,1,0:T(8,128)(2,1)}, u32[]{:S(2)}, u32[]{:S(2)}) collective-permute-start(bf16[16,64,256]{2,1,0:T(8,128)(2,1)} %collective-permute-done.12.here_ref), channel_id=1, source_target_pairs={{0,1},{1,0},{2,3},{3,2},{4,5},{5,4},{6,7},{7,6},{8,9},{9,8},{10,11... | collective-permute-start | bytes 1572872 | tf_op jit(solution)/shard_map/shrink/ppermute | solution.py:59
  69.8 8.6 %collective-permute-start.18 = (bf16[16,64,256]{2,1,0:T(8,128)(2,1)}, bf16[16,64,256]{2,1,0:T(8,128)(2,1)}, u32[]{:S(2)}, u32[]{:S(2)}) collective-permute-start(bf16[16,64,256]{2,1,0:T(8,128)(2,1)} %get-tuple-element.72), channel_id=1, source_target_pairs={{0,32},{1,225},{2,34},{3,227},{4,36},{5,229},{6,38},{7,231},{8,40}... | collective-permute-start | bytes 1572872 | tf_op jit(solution)/shard_map/ppermute | solution.py:59
  71.6 16.3 %copy-start.3 = (f32[2,384,256]{2,1,0:T(8,128)S(1)}, f32[2,384,256]{2,1,0:T(8,128)}, u32[]{:S(2)}) copy-start(f32[2,384,256]{2,1,0:T(8,128)} %copy-done.2) | copy-start | bytes 2359300
  73.6 11.0 %collective-permute-start.20 = (f32[64,384]{1,0:T(8,128)S(1)}, f32[64,384]{1,0:T(8,128)S(1)}, u32[]{:S(2)}, u32[]{:S(2)}) collective-permute-start(f32[64,384]{1,0:T(8,128)S(1)} %shrink.1), channel_id=1, source_target_pairs={{0,2},{1,3},{2,4},{3,5},{4,6},{5,7},{6,0},{7,1},{8,10},{9,11},{10,... | collective-permute-start | bytes 294920 | tf_op jit(solution)/shard_map/shrink_sum/ppermute | solution.py:59
  73.7 10.9 %collective-permute-start.21 = (f32[64,384]{1,0:T(8,128)S(1)}, f32[64,384]{1,0:T(8,128)S(1)}, u32[]{:S(2)}, u32[]{:S(2)}) collective-permute-start(f32[64,384]{1,0:T(8,128)S(1)} %shrink.1), channel_id=1, source_target_pairs={{0,6},{1,7},{2,0},{3,1},{4,2},{5,3},{6,4},{7,5},{8,14},{9,15},{10,... | collective-permute-start | bytes 294920 | tf_op jit(solution)/shard_map/shrink_sum/ppermute | solution.py:59
  76.4 8.3 %collective-permute-start.22 = (f32[64,384]{1,0:T(8,128)S(1)}, f32[64,384]{1,0:T(8,128)S(1)}, u32[]{:S(2)}, u32[]{:S(2)}) collective-permute-start(f32[64,384]{1,0:T(8,128)S(1)} %shrink.1), channel_id=1, source_target_pairs={{0,4},{1,5},{2,6},{3,7},{4,0},{5,1},{6,2},{7,3},{8,12},{9,13},{10,... | collective-permute-start | bytes 294920 | tf_op jit(solution)/shard_map/shrink_sum/ppermute | solution.py:59
  79.7 11.6 %collective-permute-start.19 = (bf16[8,64,256]{2,1,0:T(8,128)(2,1)S(1)}, bf16[8,64,256]{2,1,0:T(8,128)(2,1)S(1)}, u32[]{:S(2)}, u32[]{:S(2)}) collective-permute-start(bf16[8,64,256]{2,1,0:T(8,128)(2,1)S(1)} %get-tuple-element.74), channel_id=1, source_target_pairs={{0,32},{1,225},{2,34},{3,227},{4,36},{5,229},{6,38},{7,231},{8,40}... | collective-permute-start | bytes 786440 | tf_op jit(solution)/shard_map/ppermute | solution.py:59
  82.6 9.2 %collective-permute-start.23 = (bf16[8,64,256]{2,1,0:T(8,128)(2,1)S(1)}, bf16[8,64,256]{2,1,0:T(8,128)(2,1)S(1)}, u32[]{:S(2)}, u32[]{:S(2)}) collective-permute-start(bf16[8,64,256]{2,1,0:T(8,128)(2,1)S(1)} %get-tuple-element.80), channel_id=1, source_target_pairs={{0,33},{1,224},{2,35},{3,226},{4,37},{5,228},{6,39},{7,230},{8,41}... | collective-permute-start | bytes 786440 | tf_op jit(solution)/shard_map/ppermute | solution.py:59
  84.7 8.0 %collective-permute-start.24 = (f32[64,384]{1,0:T(8,128)S(1)}, f32[64,384]{1,0:T(8,128)S(1)}, u32[]{:S(2)}, u32[]{:S(2)}) collective-permute-start(f32[64,384]{1,0:T(8,128)S(1)} %add_add_fusion), channel_id=1, source_target_pairs={{0,8},{1,9},{2,10},{3,11},{4,12},{5,13},{6,14},{7,15},{8,16},{9,17... | collective-permute-start | bytes 294920 | tf_op jit(solution)/shard_map/shrink_sum/ppermute | solution.py:59
  84.9 7.9 %collective-permute-start.25 = (f32[64,384]{1,0:T(8,128)S(1)}, f32[64,384]{1,0:T(8,128)S(1)}, u32[]{:S(2)}, u32[]{:S(2)}) collective-permute-start(f32[64,384]{1,0:T(8,128)S(1)} %add_add_fusion), channel_id=1, source_target_pairs={{0,24},{1,25},{2,26},{3,27},{4,28},{5,29},{6,30},{7,31},{8,0},{9,1... | collective-permute-start | bytes 294920 | tf_op jit(solution)/shard_map/shrink_sum/ppermute | solution.py:59
  87.5 5.8 %collective-permute-start.26 = (f32[64,384]{1,0:T(8,128)S(1)}, f32[64,384]{1,0:T(8,128)S(1)}, u32[]{:S(2)}, u32[]{:S(2)}) collective-permute-start(f32[64,384]{1,0:T(8,128)S(1)} %add_add_fusion), channel_id=1, source_target_pairs={{0,16},{1,17},{2,18},{3,19},{4,20},{5,21},{6,22},{7,23},{8,24},{9,... | collective-permute-start | bytes 294920 | tf_op jit(solution)/shard_map/shrink_sum/ppermute | solution.py:59
  93.3 1.9 %collective-permute-start.28 = (f32[384,256]{1,0:T(8,128)S(1)}, f32[384,256]{1,0:T(8,128)S(1)}, u32[]{:S(2)}, u32[]{:S(2)}) collective-permute-start(f32[384,256]{1,0:T(8,128)S(1)} %get-tuple-element.84), channel_id=1, source_target_pairs={{0,1},{1,0},{2,3},{3,2},{4,5},{5,4},{6,7},{7,6},{8,9},{9,8},{10,11... | collective-permute-start | bytes 1179656 | tf_op jit(solution)/shard_map/base/ppermute | solution.py:59
  93.7 1.4 %collective-permute-start.27 = (bf16[64,384]{1,0:T(8,128)(2,1)S(1)}, bf16[64,384]{1,0:T(8,128)(2,1)S(1)}, u32[]{:S(2)}, u32[]{:S(2)}) collective-permute-start(bf16[64,384]{1,0:T(8,128)(2,1)S(1)} %multiply_convert_fusion.scaled_ref), channel_id=1, source_target_pairs={{0,1},{1,0},{2,3},{3,2},{4,5},{5,4},{6,7},{7,6},{8,9},{9,8},{10,11... | collective-permute-start | bytes 147464 | tf_op jit(solution)/shard_map/shrink_sum/ppermute | solution.py:59
  (7 other events, 7.1 us)

commit v4 on v3

--- a/solution.py
+++ b/solution.py
@@ -351,7 +351,7 @@
             scratch=[pltpu.VMEM((wanted, rank, 2 * feats), bf16), pltpu.VMEM((wanted * rank, rows // 2), f32)],
         )
     with jax.named_scope("shrink_sum"):
-        part = after(part, near_beyond, rest_beyond)
+        part = after(part, near_beyond)
         pieces = along_x(part, 1), along_x(part, -1), along_x(part, 2)
     up_to_same, up_to_cross = step(
         [
@@ -361,7 +361,7 @@
     )
     up_same, up_cross = along_z(up_to_same), along_z(up_to_cross, 1)
     with jax.named_scope("shrink_sum"):
-        pieces = after(pieces, up_to_same)
+        pieces = after(pieces, up_to_same, rest_beyond)
         part = part + pieces[0] + pieces[1] + pieces[2]
         pieces = along_y(part, 1), along_y(part, -1), along_y(part, 2)
     base = add_base(after(base, part), (near_beyond, near_at, 2), (rest_beyond, rest_at, 2))

time: 96.8 us -> 92.7 us (0.958)
  waiting for transfers between devices: 22.2 us -> 16.8 us
  starting transfers between devices: 39.7 us -> 41.1 us
    ppermute x29, waiting for transfers between devices: 22.2 us -> 16.8 us  [send(): return lax.ppermute(value, ('adapter', 'tensor'), pairs)]
    ppermute x29, starting transfers between devices: 39.7 us -> 41.1 us  [send(): return lax.ppermute(value, ('adapter', 'tensor'), pairs)]
  transfers between devices with their start and end apart: 29 -> 29, of which waited for: 8 -> 7; matrix products, arithmetic and copies ran while one was open for 3% -> 3% of each run, Pallas kernels for 24% -> 25%
where the time goes in v4:
time: 92.7 us; the launch traced here: 92.3 us
  starting transfers between devices  41.1 us (44%)
  Pallas kernels  23.4 us (25%)
  waiting for transfers between devices  16.8 us (18%)
  local copies, waits for them, and re-layouts  8.78 us (9%)
  other arithmetic  1.98 us (2%)
    ppermute x29, starting transfers between devices, send(): return lax.ppermute(value, ('adapter', 'tensor'), pairs)  41.1 us
    pallas_call x13, Pallas kernels, kernel_call(): pl.pallas_call(kernel, out_shape=out_shape, in_specs=specs, out_specs=jax...  23.4 us
    ppermute x29, waiting for transfers between devices, send(): return lax.ppermute(value, ('adapter', 'tensor'), pairs)  16.8 us
    unnamed x21, local copies, waits for them, and re-layouts  7.79 us
  transfers between devices with their start and end apart: 29, of which 7 were waited for; matrix products, arithmetic and copies ran while one was open for 3% of the time, Pallas kernels for 25%

profile of v4, /device:TPU:1, one launch (start us, length us, event | category | flops | bytes accessed | tf_op | source)
XLA Modules:
  0.0 92.3 jit_solution(8436984298492147571)
XLA Ops:
  0.0 3.2 %collective-permute-start.1 = (bf16[24,64,256]{2,1,0:T(8,128)(2,1)}, bf16[24,64,256]{2,1,0:T(8,128)(2,1)S(1)}, u32[]{:S(2)}, u32[]{:S(2)}) collective-permute-start(bf16[24,64,256]{2,1,0:T(8,128)(2,1)} %refs_0_.1), channel_id=1, source_target_pairs={{0,1},{1,0},{2,3},{3,2},{4,5},{5,4},{6,7},{7,6},{8,9},{9,8},{10,11... | collective-permute-start | bytes 2359304 | tf_op jit(solution)/shard_map/ppermute | solution.py:59
  4.0 1.6 %shard_map.73 = (bf16[24,64,256]{2,1,0:T(8,128)(2,1)S(1)}, bf16[24,64,256]{2,1,0:T(8,128)(2,1)S(1)}, bf16[768,256]{1,0:T(8,128)(2,1)S(1)}) custom-call(bf16[24,64,256]{2,1,0:T(8,128)(2,1)} %refs_0_.1, bf16[24,64,256]{2,1,0:T(8,128)(2,1)} %refs_1_.1, bf16[768,256]{1,0:T(8,128)(2,1)} %refs_2_.1), custom_call_target="tpu_custom_call" | custom-call | tf_op jit(solution)/shard_map/pallas_call | solution.py:29
  7.9 2.7 %collective-permute-start.3 = (bf16[384,512]{1,0:T(8,128)(2,1)S(1)}, bf16[384,512]{1,0:T(8,128)(2,1)S(1)}, u32[]{:S(2)}, u32[]{:S(2)}) collective-permute-start(bf16[384,512]{1,0:T(8,128)(2,1)S(1)} %get-tuple-element.49), channel_id=1, source_target_pairs={{0,6},{1,25},{2,0},{3,27},{4,2},{5,29},{6,4},{7,31},{8,14},{9,1},{... | collective-permute-start | bytes 1179656 | tf_op jit(solution)/shard_map/ppermute | solution.py:59
  10.6 3.9 %collective-permute-start.5 = (bf16[8,64,256]{2,1,0:T(8,128)(2,1)S(1)}, bf16[8,64,256]{2,1,0:T(8,128)(2,1)S(1)}, u32[]{:S(2)}, u32[]{:S(2)}) collective-permute-start(bf16[8,64,256]{2,1,0:T(8,128)(2,1)S(1)} %shard_map.74), channel_id=1, source_target_pairs={{0,32},{1,225},{2,34},{3,227},{4,36},{5,229},{6,38},{7,231},{8,40}... | collective-permute-start | bytes 786440 | tf_op jit(solution)/shard_map/ppermute | solution.py:59
  14.5 3.3 %collective-permute-done.5.refs_0_ = bf16[8,64,256]{2,1,0:T(8,128)(2,1)S(1)} collective-permute-done((bf16[8,64,256]{2,1,0:T(8,128)(2,1)S(1)}, bf16[8,64,256]{2,1,0:T(8,128)(2,1)S(1)}, u32[]{:S(2)}, u32[]{:S(2)}) %collective-permute-start.5) | collective-permute-done | bytes 262176 | tf_op jit(solution)/shard_map/ppermute | solution.py:59
  18.6 3.2 %collective-permute-start.9 = (bf16[24,64,256]{2,1,0:T(8,128)(2,1)S(1)}, bf16[24,64,256]{2,1,0:T(8,128)(2,1)S(1)}, u32[]{:S(2)}, u32[]{:S(2)}) collective-permute-start(bf16[24,64,256]{2,1,0:T(8,128)(2,1)S(1)} %shard_map.76), channel_id=1, source_target_pairs={{0,32},{1,225},{2,34},{3,227},{4,36},{5,229},{6,38},{7,231},{8,40}... | collective-permute-start | bytes 2359304 | tf_op jit(solution)/shard_map/ppermute | solution.py:59
  22.2 1.3 %collective-permute-start.6 = (bf16[2,384,512]{2,1,0:T(8,128)(2,1)S(1)}, bf16[2,384,512]{2,1,0:T(8,128)(2,1)}, u32[]{:S(2)}, u32[]{:S(2)}) collective-permute-start(bf16[2,384,512]{2,1,0:T(8,128)(2,1)S(1)} %pad_maximum_fusion.refs_0_), channel_id=1, source_target_pairs={{0,8},{1,3},{2,10},{3,5},{4,12},{5,7},{6,14},{7,1},{8,16},{9,11},{... | collective-permute-start | bytes 2359304 | tf_op jit(solution)/shard_map/ppermute | solution.py:59
  23.5 1.5 %collective-permute-start.7 = (bf16[2,384,512]{2,1,0:T(8,128)(2,1)S(1)}, bf16[2,384,512]{2,1,0:T(8,128)(2,1)S(1)}, u32[]{:S(2)}, u32[]{:S(2)}) collective-permute-start(bf16[2,384,512]{2,1,0:T(8,128)(2,1)S(1)} %pad_maximum_fusion.refs_0_), channel_id=1, source_target_pairs={{0,24},{1,7},{2,26},{3,1},{4,28},{5,3},{6,30},{7,5},{8,0},{9,15},{... | collective-permute-start | bytes 2359304 | tf_op jit(solution)/shard_map/ppermute | solution.py:59
  25.8 8.3 %collective-permute-done.8 = bf16[384,512]{1,0:T(8,128)(2,1)S(1)} collective-permute-done((bf16[384,512]{1,0:T(8,128)(2,1)S(1)}, bf16[384,512]{1,0:T(8,128)(2,1)S(1)}, u32[]{:S(2)}, u32[]{:S(2)}) %collective-permute-start.8) | collective-permute-done | bytes 393248 | tf_op jit(solution)/shard_map/ppermute | solution.py:59
  34.1 1.9 %shard_map.77 = bf16[32,64,256]{2,1,0:T(8,128)(2,1)} custom-call(s32[256]{0:T(256)S(1)} %pad_add_fusion.table_ref, bf16[24,64,256]{2,1,0:T(8,128)(2,1)S(1)} %collective-permute-done.9.refs_0_, bf16[24,64,256]{2,1,0:T(8,128)(2,1)S(1)} %get-tuple-element.47.refs_0_.refs_1_.mine_ref, bf16[24,64,256]{2,1,0:T(8,128)(2,1)S(1)} %collective-permute-done.1.refs_1_.refs_2_.sib_ref, ...), custom_call_target="tpu_custom_call" | custom-call | tf_op jit(solution)/shard_map/pallas_call | solution.py:29
  36.1 2.0 %collective-permute-done.6.refs_1_ = bf16[2,384,512]{2,1,0:T(8,128)(2,1)} collective-permute-done((bf16[2,384,512]{2,1,0:T(8,128)(2,1)S(1)}, bf16[2,384,512]{2,1,0:T(8,128)(2,1)}, u32[]{:S(2)}, u32[]{:S(2)}) %collective-permute-start.6) | collective-permute-done | bytes 786464 | tf_op jit(solution)/shard_map/ppermute | solution.py:59
  40.0 2.7 %collective-permute-start.14 = (bf16[2,384,512]{2,1,0:T(8,128)(2,1)}, bf16[2,384,512]{2,1,0:T(8,128)(2,1)}, u32[]{:S(2)}, u32[]{:S(2)}) collective-permute-start(bf16[2,384,512]{2,1,0:T(8,128)(2,1)} %pad_maximum_fusion.1.refs_1_), channel_id=1, source_target_pairs={{0,24},{1,7},{2,26},{3,1},{4,28},{5,3},{6,30},{7,5},{8,0},{9,15},{... | collective-permute-start | bytes 2359304 | tf_op jit(solution)/shard_map/ppermute | solution.py:59
  42.8 1.1 %copy-done.5 = bf16[2,384,512]{2,1,0:T(8,128)(2,1)S(1)} copy-done((bf16[2,384,512]{2,1,0:T(8,128)(2,1)S(1)}, bf16[2,384,512]{2,1,0:T(8,128)(2,1)}, u32[]{:S(2)}) %copy-start.5) | copy-done | bytes 786456
  45.0 4.2 %shard_map.78.refs_0_ = f32[2,384,256]{2,1,0:T(8,128)S(1)} custom-call(s32[6]{0:T(128)S(1)} %stack.81.block_ref, bf16[2,384,512]{2,1,0:T(8,128)(2,1)S(1)} %copy-done.5, bf16[2,384,512]{2,1,0:T(8,128)(2,1)} %collective-permute-done.6.refs_1_, bf16[2,384,512]{2,1,0:T(8,128)(2,1)S(1)} %copy-done.7, bf16[16,512,256]{2,1,0:T(8,128)(2,1)} %bitcast.10.refs_3_.refs_4_, ...), custom_call_target="tpu_custom_call" | custom-call | tf_op jit(solution)/shard_map/pallas_call | solution.py:29
  50.3 2.5 %shard_map.79 = (bf16[16,64,256]{2,1,0:T(8,128)(2,1)}, bf16[16,64,256]{2,1,0:T(8,128)(2,1)}) custom-call(s32[256]{0:T(256)S(1)} %pad_add_fusion.table_ref, bf16[32,64,256]{2,1,0:T(8,128)(2,1)} %collective-permute-done.11.refs_0_, bf16[24,64,256]{2,1,0:T(8,128)(2,1)S(1)} %get-tuple-element.47.refs_0_.refs_1_.mine_ref, ...), custom_call_target="tpu_custom_call" | custom-call | tf_op jit(solution)/shard_map/pallas_call | solution.py:29
  52.7 1.3 %collective-permute-start.12 = (bf16[16,64,256]{2,1,0:T(8,128)(2,1)}, bf16[16,64,256]{2,1,0:T(8,128)(2,1)}, u32[]{:S(2)}, u32[]{:S(2)}) collective-permute-start(bf16[16,64,256]{2,1,0:T(8,128)(2,1)} %get-tuple-element.65), channel_id=1, source_target_pairs={{0,32},{1,225},{2,34},{3,227},{4,36},{5,229},{6,38},{7,231},{8,40}... | collective-permute-start | bytes 1572872 | tf_op jit(solution)/shard_map/ppermute | solution.py:59
  54.0 1.2 %collective-permute-start.16 = (bf16[2,384,512]{2,1,0:T(8,128)(2,1)}, bf16[2,384,512]{2,1,0:T(8,128)(2,1)}, u32[]{:S(2)}, u32[]{:S(2)}) collective-permute-start(bf16[2,384,512]{2,1,0:T(8,128)(2,1)} %collective-permute-done.6.refs_1_), channel_id=1, source_target_pairs={{0,8},{1,3},{2,10},{3,5},{4,12},{5,7},{6,14},{7,1},{8,16},{9,11},{... | collective-permute-start | bytes 2359304 | tf_op jit(solution)/shard_map/ppermute | solution.py:59
  55.3 1.6 %collective-permute-start.22 = (bf16[2,384,512]{2,1,0:T(8,128)(2,1)}, bf16[2,384,512]{2,1,0:T(8,128)(2,1)}, u32[]{:S(2)}, u32[]{:S(2)}) collective-permute-start(bf16[2,384,512]{2,1,0:T(8,128)(2,1)} %collective-permute-done.14.refs_3_), channel_id=1, source_target_pairs={{0,24},{1,7},{2,26},{3,1},{4,28},{5,3},{6,30},{7,5},{8,0},{9,15},{... | collective-permute-start | bytes 2359304 | tf_op jit(solution)/shard_map/ppermute | solution.py:59
  58.1 4.1 %shard_map.80.refs_0_ = f32[2,384,256]{2,1,0:T(8,128)S(1)} custom-call(s32[6]{0:T(128)S(1)} %stack.94.block_ref, f32[2,384,256]{2,1,0:T(8,128)S(1)} %copy-done.1, bf16[2,384,512]{2,1,0:T(8,128)(2,1)} %pad_maximum_fusion.1.refs_1_, bf16[2,384,512]{2,1,0:T(8,128)(2,1)} %collective-permute-done.13.refs_2_, ...), custom_call_target="tpu_custom_call" | custom-call | tf_op jit(solution)/shard_map/pallas_call | solution.py:29
  63.2 2.3 %collective-permute-start.15 = (bf16[16,64,256]{2,1,0:T(8,128)(2,1)}, bf16[16,64,256]{2,1,0:T(8,128)(2,1)}, u32[]{:S(2)}, u32[]{:S(2)}) collective-permute-start(bf16[16,64,256]{2,1,0:T(8,128)(2,1)} %collective-permute-done.12.here_ref), channel_id=1, source_target_pairs={{0,1},{1,0},{2,3},{3,2},{4,5},{5,4},{6,7},{7,6},{8,9},{9,8},{10,11... | collective-permute-start | bytes 1572872 | tf_op jit(solution)/shard_map/shrink/ppermute | solution.py:59
  65.5 1.8 %collective-permute-start.17 = (bf16[16,64,256]{2,1,0:T(8,128)(2,1)}, bf16[16,64,256]{2,1,0:T(8,128)(2,1)}, u32[]{:S(2)}, u32[]{:S(2)}) collective-permute-start(bf16[16,64,256]{2,1,0:T(8,128)(2,1)} %get-tuple-element.72), channel_id=1, source_target_pairs={{0,32},{1,225},{2,34},{3,227},{4,36},{5,229},{6,38},{7,231},{8,40}... | collective-permute-start | bytes 1572872 | tf_op jit(solution)/shard_map/ppermute | solution.py:59
  67.4 1.9 %shrink.1 = f32[64,384]{1,0:T(8,128)S(1)} custom-call(s32[256]{0:T(256)S(1)} %pad_add_fusion.table_ref, bf16[16,64,256]{2,1,0:T(8,128)(2,1)} %collective-permute-done.12.here_ref, bf16[16,64,256]{2,1,0:T(8,128)(2,1)} %collective-permute-done.15.other_ref, bf16[24,64,256]{2,1,0:T(8,128)(2,1)S(1)} %get-tuple-element.47.refs_0_.refs_1_.mine_ref, ...), custom_call_target="tpu_custom_call" | custom-call | tf_op jit(solution)/shard_map/shrink/pallas_call | solution.py:29
  69.7 2.3 %collective-permute-start.20 = (f32[64,384]{1,0:T(8,128)S(1)}, f32[64,384]{1,0:T(8,128)S(1)}, u32[]{:S(2)}, u32[]{:S(2)}) collective-permute-start(f32[64,384]{1,0:T(8,128)S(1)} %shrink.1), channel_id=1, source_target_pairs={{0,6},{1,7},{2,0},{3,1},{4,2},{5,3},{6,4},{7,5},{8,14},{9,15},{10,... | collective-permute-start | bytes 294920 | tf_op jit(solution)/shard_map/shrink_sum/ppermute | solution.py:59
  72.6 1.6 %collective-permute-done.17.refs_0_ = bf16[16,64,256]{2,1,0:T(8,128)(2,1)} collective-permute-done((bf16[16,64,256]{2,1,0:T(8,128)(2,1)}, bf16[16,64,256]{2,1,0:T(8,128)(2,1)}, u32[]{:S(2)}, u32[]{:S(2)}) %collective-permute-start.17) | collective-permute-done | bytes 524320 | tf_op jit(solution)/shard_map/ppermute | solution.py:59
  74.1 1.2 %shard_map.81 = (bf16[8,64,256]{2,1,0:T(8,128)(2,1)S(1)}, bf16[8,64,256]{2,1,0:T(8,128)(2,1)S(1)}) custom-call(s32[256]{0:T(256)S(1)} %pad_add_fusion.table_ref, bf16[16,64,256]{2,1,0:T(8,128)(2,1)} %collective-permute-done.17.refs_0_, bf16[24,64,256]{2,1,0:T(8,128)(2,1)S(1)} %get-tuple-element.47.refs_0_.refs_1_.mine_ref, ...), custom_call_target="tpu_custom_call" | custom-call | tf_op jit(solution)/shard_map/pallas_call | solution.py:29
  75.3 3.0 %collective-permute-start.18 = (bf16[8,64,256]{2,1,0:T(8,128)(2,1)S(1)}, bf16[8,64,256]{2,1,0:T(8,128)(2,1)S(1)}, u32[]{:S(2)}, u32[]{:S(2)}) collective-permute-start(bf16[8,64,256]{2,1,0:T(8,128)(2,1)S(1)} %get-tuple-element.74), channel_id=1, source_target_pairs={{0,32},{1,225},{2,34},{3,227},{4,36},{5,229},{6,38},{7,231},{8,40}... | collective-permute-start | bytes 786440 | tf_op jit(solution)/shard_map/ppermute | solution.py:59
  78.3 2.0 %collective-permute-start.23 = (bf16[8,64,256]{2,1,0:T(8,128)(2,1)S(1)}, bf16[8,64,256]{2,1,0:T(8,128)(2,1)S(1)}, u32[]{:S(2)}, u32[]{:S(2)}) collective-permute-start(bf16[8,64,256]{2,1,0:T(8,128)(2,1)S(1)} %get-tuple-element.80), channel_id=1, source_target_pairs={{0,33},{1,224},{2,35},{3,226},{4,37},{5,228},{6,39},{7,230},{8,41}... | collective-permute-start | bytes 786440 | tf_op jit(solution)/shard_map/ppermute | solution.py:59
  80.4 1.4 %collective-permute-start.24 = (f32[64,384]{1,0:T(8,128)S(1)}, f32[64,384]{1,0:T(8,128)S(1)}, u32[]{:S(2)}, u32[]{:S(2)}) collective-permute-start(f32[64,384]{1,0:T(8,128)S(1)} %add_add_fusion), channel_id=1, source_target_pairs={{0,8},{1,9},{2,10},{3,11},{4,12},{5,13},{6,14},{7,15},{8,16},{9,17... | collective-permute-start | bytes 294920 | tf_op jit(solution)/shard_map/shrink_sum/ppermute | solution.py:59
  81.8 1.5 %collective-permute-start.25 = (f32[64,384]{1,0:T(8,128)S(1)}, f32[64,384]{1,0:T(8,128)S(1)}, u32[]{:S(2)}, u32[]{:S(2)}) collective-permute-start(f32[64,384]{1,0:T(8,128)S(1)} %add_add_fusion), channel_id=1, source_target_pairs={{0,24},{1,25},{2,26},{3,27},{4,28},{5,29},{6,30},{7,31},{8,0},{9,1... | collective-permute-start | bytes 294920 | tf_op jit(solution)/shard_map/shrink_sum/ppermute | solution.py:59
  83.3 1.6 %collective-permute-start.26 = (f32[64,384]{1,0:T(8,128)S(1)}, f32[64,384]{1,0:T(8,128)S(1)}, u32[]{:S(2)}, u32[]{:S(2)}) collective-permute-start(f32[64,384]{1,0:T(8,128)S(1)} %add_add_fusion), channel_id=1, source_target_pairs={{0,16},{1,17},{2,18},{3,19},{4,20},{5,21},{6,22},{7,23},{8,24},{9,... | collective-permute-start | bytes 294920 | tf_op jit(solution)/shard_map/shrink_sum/ppermute | solution.py:59
  84.9 3.3 %shard_map.82 = f32[2,384,256]{2,1,0:T(8,128)S(1)} custom-call(s32[4]{0:T(128)S(1)} %pad_add_fusion.1.block_ref, f32[2,384,256]{2,1,0:T(8,128)S(1)} %copy-done.3, bf16[2,384,512]{2,1,0:T(8,128)(2,1)} %collective-permute-done.16.refs_1_, bf16[2,384,512]{2,1,0:T(8,128)(2,1)} %collective-permute-done.22.refs_2_, bf16[16,512,256]{2,1,0:T(8,128)(2,1)} %bitcast.10.refs_3_.refs_4_, ...), custom_call_target="tpu_custom_call" | custom-call | tf_op jit(solution)/shard_map/pallas_call | solution.py:29
  89.8 1.3 %collective-permute-done.27.other_ref = bf16[64,384]{1,0:T(8,128)(2,1)S(1)} collective-permute-done((bf16[64,384]{1,0:T(8,128)(2,1)S(1)}, bf16[64,384]{1,0:T(8,128)(2,1)S(1)}, u32[]{:S(2)}, u32[]{:S(2)}) %collective-permute-start.27) | collective-permute-done | bytes 49184 | tf_op jit(solution)/shard_map/shrink_sum/ppermute | solution.py:59
  (71 shorter events, 15.4 us)
Async XLA Ops:
  0.0 6.3 %collective-permute-start.1 = (bf16[24,64,256]{2,1,0:T(8,128)(2,1)}, bf16[24,64,256]{2,1,0:T(8,128)(2,1)S(1)}, u32[]{:S(2)}, u32[]{:S(2)}) collective-permute-start(bf16[24,64,256]{2,1,0:T(8,128)(2,1)} %refs_0_.1), channel_id=1, source_target_pairs={{0,1},{1,0},{2,3},{3,2},{4,5},{5,4},{6,7},{7,6},{8,9},{9,8},{10,11... | collective-permute-start | bytes 2359304 | tf_op jit(solution)/shard_map/ppermute | solution.py:59
  3.2 3.7 %collective-permute-start = (bf16[768,256]{1,0:T(8,128)(2,1)}, bf16[768,256]{1,0:T(8,128)(2,1)S(1)}, u32[]{:S(2)}, u32[]{:S(2)}) collective-permute-start(bf16[768,256]{1,0:T(8,128)(2,1)} %refs_2_.1), channel_id=1, source_target_pairs={{0,1},{1,0},{2,3},{3,2},{4,5},{5,4},{6,7},{7,6},{8,9},{9,8},{10,11... | collective-permute-start | bytes 1179656 | tf_op jit(solution)/shard_map/ppermute | solution.py:59
  4.0 3.8 %copy-start.8 = (bf16[24,64,256]{2,1,0:T(8,128)(2,1)S(1)}, bf16[24,64,256]{2,1,0:T(8,128)(2,1)}, u32[]{:S(2)}) copy-start(bf16[24,64,256]{2,1,0:T(8,128)(2,1)} %refs_1_.1) | copy-start | bytes 2359300
  7.2 35.6 %collective-permute-start.10 = (bf16[8192,256]{1,0:T(8,128)(2,1)}, bf16[8192,256]{1,0:T(8,128)(2,1)}, u32[]{:S(2)}, u32[]{:S(2)}) collective-permute-start(bf16[8192,256]{1,0:T(8,128)(2,1)} %param.8), channel_id=1, source_target_pairs={{0,1},{1,0},{2,3},{3,2},{4,5},{5,4},{6,7},{7,6},{8,9},{9,8},{10,11... | collective-permute-start | bytes 12582920 | tf_op jit(solution)/shard_map/ppermute | solution.py:59
  7.8 10.0 %collective-permute-start.4 = (bf16[24,64,256]{2,1,0:T(8,128)(2,1)S(1)}, bf16[24,64,256]{2,1,0:T(8,128)(2,1)S(1)}, u32[]{:S(2)}, u32[]{:S(2)}) collective-permute-start(bf16[24,64,256]{2,1,0:T(8,128)(2,1)S(1)} %copy-done.8), channel_id=1, source_target_pairs={{0,1},{1,0},{2,3},{3,2},{4,5},{5,4},{6,7},{7,6},{8,9},{9,8},{10,11... | collective-permute-start | bytes 2359304 | tf_op jit(solution)/shard_map/ppermute | solution.py:59
  7.9 9.9 %collective-permute-start.2 = (bf16[384,512]{1,0:T(8,128)(2,1)S(1)}, bf16[384,512]{1,0:T(8,128)(2,1)S(1)}, u32[]{:S(2)}, u32[]{:S(2)}) collective-permute-start(bf16[384,512]{1,0:T(8,128)(2,1)S(1)} %get-tuple-element.49), channel_id=1, source_target_pairs={{0,2},{1,9},{2,4},{3,11},{4,6},{5,13},{6,0},{7,15},{8,10},{9,17},{... | collective-permute-start | bytes 1179656 | tf_op jit(solution)/shard_map/ppermute | solution.py:59
  7.9 9.9 %collective-permute-start.3 = (bf16[384,512]{1,0:T(8,128)(2,1)S(1)}, bf16[384,512]{1,0:T(8,128)(2,1)S(1)}, u32[]{:S(2)}, u32[]{:S(2)}) collective-permute-start(bf16[384,512]{1,0:T(8,128)(2,1)S(1)} %get-tuple-element.49), channel_id=1, source_target_pairs={{0,6},{1,25},{2,0},{3,27},{4,2},{5,29},{6,4},{7,31},{8,14},{9,1},{... | collective-permute-start | bytes 1179656 | tf_op jit(solution)/shard_map/ppermute | solution.py:59
  10.6 7.2 %collective-permute-start.5 = (bf16[8,64,256]{2,1,0:T(8,128)(2,1)S(1)}, bf16[8,64,256]{2,1,0:T(8,128)(2,1)S(1)}, u32[]{:S(2)}, u32[]{:S(2)}) collective-permute-start(bf16[8,64,256]{2,1,0:T(8,128)(2,1)S(1)} %shard_map.74), channel_id=1, source_target_pairs={{0,32},{1,225},{2,34},{3,227},{4,36},{5,229},{6,38},{7,231},{8,40}... | collective-permute-start | bytes 786440 | tf_op jit(solution)/shard_map/ppermute | solution.py:59
  18.6 15.6 %collective-permute-start.9 = (bf16[24,64,256]{2,1,0:T(8,128)(2,1)S(1)}, bf16[24,64,256]{2,1,0:T(8,128)(2,1)S(1)}, u32[]{:S(2)}, u32[]{:S(2)}) collective-permute-start(bf16[24,64,256]{2,1,0:T(8,128)(2,1)S(1)} %shard_map.76), channel_id=1, source_target_pairs={{0,32},{1,225},{2,34},{3,227},{4,36},{5,229},{6,38},{7,231},{8,40}... | collective-permute-start | bytes 2359304 | tf_op jit(solution)/shard_map/ppermute | solution.py:59
  21.8 12.4 %collective-permute-start.8 = (bf16[384,512]{1,0:T(8,128)(2,1)S(1)}, bf16[384,512]{1,0:T(8,128)(2,1)S(1)}, u32[]{:S(2)}, u32[]{:S(2)}) collective-permute-start(bf16[384,512]{1,0:T(8,128)(2,1)S(1)} %collective-permute-done.2), channel_id=1, source_target_pairs={{0,2},{1,9},{2,4},{3,11},{4,6},{5,13},{6,0},{7,15},{8,10},{9,17},{... | collective-permute-start | bytes 1179656 | tf_op jit(solution)/shard_map/ppermute | solution.py:59
  22.2 15.9 %collective-permute-start.6 = (bf16[2,384,512]{2,1,0:T(8,128)(2,1)S(1)}, bf16[2,384,512]{2,1,0:T(8,128)(2,1)}, u32[]{:S(2)}, u32[]{:S(2)}) collective-permute-start(bf16[2,384,512]{2,1,0:T(8,128)(2,1)S(1)} %pad_maximum_fusion.refs_0_), channel_id=1, source_target_pairs={{0,8},{1,3},{2,10},{3,5},{4,12},{5,7},{6,14},{7,1},{8,16},{9,11},{... | collective-permute-start | bytes 2359304 | tf_op jit(solution)/shard_map/ppermute | solution.py:59
  23.5 14.6 %collective-permute-start.7 = (bf16[2,384,512]{2,1,0:T(8,128)(2,1)S(1)}, bf16[2,384,512]{2,1,0:T(8,128)(2,1)S(1)}, u32[]{:S(2)}, u32[]{:S(2)}) collective-permute-start(bf16[2,384,512]{2,1,0:T(8,128)(2,1)S(1)} %pad_maximum_fusion.refs_0_), channel_id=1, source_target_pairs={{0,24},{1,7},{2,26},{3,1},{4,28},{5,3},{6,30},{7,5},{8,0},{9,15},{... | collective-permute-start | bytes 2359304 | tf_op jit(solution)/shard_map/ppermute | solution.py:59
  36.0 14.3 %collective-permute-start.11 = (bf16[32,64,256]{2,1,0:T(8,128)(2,1)}, bf16[32,64,256]{2,1,0:T(8,128)(2,1)}, u32[]{:S(2)}, u32[]{:S(2)}) collective-permute-start(bf16[32,64,256]{2,1,0:T(8,128)(2,1)} %shard_map.77), channel_id=1, source_target_pairs={{0,32},{1,225},{2,34},{3,227},{4,36},{5,229},{6,38},{7,231},{8,40}... | collective-permute-start | bytes 3145736 | tf_op jit(solution)/shard_map/ppermute | solution.py:59
  40.0 15.3 %collective-permute-start.13 = (bf16[2,384,512]{2,1,0:T(8,128)(2,1)}, bf16[2,384,512]{2,1,0:T(8,128)(2,1)}, u32[]{:S(2)}, u32[]{:S(2)}) collective-permute-start(bf16[2,384,512]{2,1,0:T(8,128)(2,1)} %pad_maximum_fusion.1.refs_1_), channel_id=1, source_target_pairs={{0,8},{1,3},{2,10},{3,5},{4,12},{5,7},{6,14},{7,1},{8,16},{9,11},{... | collective-permute-start | bytes 2359304 | tf_op jit(solution)/shard_map/ppermute | solution.py:59
  40.0 15.3 %collective-permute-start.14 = (bf16[2,384,512]{2,1,0:T(8,128)(2,1)}, bf16[2,384,512]{2,1,0:T(8,128)(2,1)}, u32[]{:S(2)}, u32[]{:S(2)}) collective-permute-start(bf16[2,384,512]{2,1,0:T(8,128)(2,1)} %pad_maximum_fusion.1.refs_1_), channel_id=1, source_target_pairs={{0,24},{1,7},{2,26},{3,1},{4,28},{5,3},{6,30},{7,5},{8,0},{9,15},{... | collective-permute-start | bytes 2359304 | tf_op jit(solution)/shard_map/ppermute | solution.py:59
  52.7 10.4 %collective-permute-start.12 = (bf16[16,64,256]{2,1,0:T(8,128)(2,1)}, bf16[16,64,256]{2,1,0:T(8,128)(2,1)}, u32[]{:S(2)}, u32[]{:S(2)}) collective-permute-start(bf16[16,64,256]{2,1,0:T(8,128)(2,1)} %get-tuple-element.65), channel_id=1, source_target_pairs={{0,32},{1,225},{2,34},{3,227},{4,36},{5,229},{6,38},{7,231},{8,40}... | collective-permute-start | bytes 1572872 | tf_op jit(solution)/shard_map/ppermute | solution.py:59
  54.0 15.2 %collective-permute-start.16 = (bf16[2,384,512]{2,1,0:T(8,128)(2,1)}, bf16[2,384,512]{2,1,0:T(8,128)(2,1)}, u32[]{:S(2)}, u32[]{:S(2)}) collective-permute-start(bf16[2,384,512]{2,1,0:T(8,128)(2,1)} %collective-permute-done.6.refs_1_), channel_id=1, source_target_pairs={{0,8},{1,3},{2,10},{3,5},{4,12},{5,7},{6,14},{7,1},{8,16},{9,11},{... | collective-permute-start | bytes 2359304 | tf_op jit(solution)/shard_map/ppermute | solution.py:59
  55.3 23.0 %collective-permute-start.22 = (bf16[2,384,512]{2,1,0:T(8,128)(2,1)}, bf16[2,384,512]{2,1,0:T(8,128)(2,1)}, u32[]{:S(2)}, u32[]{:S(2)}) collective-permute-start(bf16[2,384,512]{2,1,0:T(8,128)(2,1)} %collective-permute-done.14.refs_3_), channel_id=1, source_target_pairs={{0,24},{1,7},{2,26},{3,1},{4,28},{5,3},{6,30},{7,5},{8,0},{9,15},{... | collective-permute-start | bytes 2359304 | tf_op jit(solution)/shard_map/ppermute | solution.py:59
  58.1 9.1 %copy-start.9 = (s32[768]{0:T(1024)S(1)}, s32[768]{0:T(1024)}, u32[]{:S(2)}) copy-start(s32[768]{0:T(1024)} %param.13) | copy-start | bytes 9220
  63.2 4.2 %collective-permute-start.15 = (bf16[16,64,256]{2,1,0:T(8,128)(2,1)}, bf16[16,64,256]{2,1,0:T(8,128)(2,1)}, u32[]{:S(2)}, u32[]{:S(2)}) collective-permute-start(bf16[16,64,256]{2,1,0:T(8,128)(2,1)} %collective-permute-done.12.here_ref), channel_id=1, source_target_pairs={{0,1},{1,0},{2,3},{3,2},{4,5},{5,4},{6,7},{7,6},{8,9},{9,8},{10,11... | collective-permute-start | bytes 1572872 | tf_op jit(solution)/shard_map/shrink/ppermute | solution.py:59
  65.5 8.6 %collective-permute-start.17 = (bf16[16,64,256]{2,1,0:T(8,128)(2,1)}, bf16[16,64,256]{2,1,0:T(8,128)(2,1)}, u32[]{:S(2)}, u32[]{:S(2)}) collective-permute-start(bf16[16,64,256]{2,1,0:T(8,128)(2,1)} %get-tuple-element.72), channel_id=1, source_target_pairs={{0,32},{1,225},{2,34},{3,227},{4,36},{5,229},{6,38},{7,231},{8,40}... | collective-permute-start | bytes 1572872 | tf_op jit(solution)/shard_map/ppermute | solution.py:59
  67.3 17.6 %copy-start.3 = (f32[2,384,256]{2,1,0:T(8,128)S(1)}, f32[2,384,256]{2,1,0:T(8,128)}, u32[]{:S(2)}) copy-start(f32[2,384,256]{2,1,0:T(8,128)} %copy-done.2) | copy-start | bytes 2359300
  69.3 11.0 %collective-permute-start.19 = (f32[64,384]{1,0:T(8,128)S(1)}, f32[64,384]{1,0:T(8,128)S(1)}, u32[]{:S(2)}, u32[]{:S(2)}) collective-permute-start(f32[64,384]{1,0:T(8,128)S(1)} %shrink.1), channel_id=1, source_target_pairs={{0,2},{1,3},{2,4},{3,5},{4,6},{5,7},{6,0},{7,1},{8,10},{9,11},{10,... | collective-permute-start | bytes 294920 | tf_op jit(solution)/shard_map/shrink_sum/ppermute | solution.py:59
  69.7 10.6 %collective-permute-start.20 = (f32[64,384]{1,0:T(8,128)S(1)}, f32[64,384]{1,0:T(8,128)S(1)}, u32[]{:S(2)}, u32[]{:S(2)}) collective-permute-start(f32[64,384]{1,0:T(8,128)S(1)} %shrink.1), channel_id=1, source_target_pairs={{0,6},{1,7},{2,0},{3,1},{4,2},{5,3},{6,4},{7,5},{8,14},{9,15},{10,... | collective-permute-start | bytes 294920 | tf_op jit(solution)/shard_map/shrink_sum/ppermute | solution.py:59
  72.0 8.3 %collective-permute-start.21 = (f32[64,384]{1,0:T(8,128)S(1)}, f32[64,384]{1,0:T(8,128)S(1)}, u32[]{:S(2)}, u32[]{:S(2)}) collective-permute-start(f32[64,384]{1,0:T(8,128)S(1)} %shrink.1), channel_id=1, source_target_pairs={{0,4},{1,5},{2,6},{3,7},{4,0},{5,1},{6,2},{7,3},{8,12},{9,13},{10,... | collective-permute-start | bytes 294920 | tf_op jit(solution)/shard_map/shrink_sum/ppermute | solution.py:59
  75.3 12.9 %collective-permute-start.18 = (bf16[8,64,256]{2,1,0:T(8,128)(2,1)S(1)}, bf16[8,64,256]{2,1,0:T(8,128)(2,1)S(1)}, u32[]{:S(2)}, u32[]{:S(2)}) collective-permute-start(bf16[8,64,256]{2,1,0:T(8,128)(2,1)S(1)} %get-tuple-element.74), channel_id=1, source_target_pairs={{0,32},{1,225},{2,34},{3,227},{4,36},{5,229},{6,38},{7,231},{8,40}... | collective-permute-start | bytes 786440 | tf_op jit(solution)/shard_map/ppermute | solution.py:59
  78.3 9.9 %collective-permute-start.23 = (bf16[8,64,256]{2,1,0:T(8,128)(2,1)S(1)}, bf16[8,64,256]{2,1,0:T(8,128)(2,1)S(1)}, u32[]{:S(2)}, u32[]{:S(2)}) collective-permute-start(bf16[8,64,256]{2,1,0:T(8,128)(2,1)S(1)} %get-tuple-element.80), channel_id=1, source_target_pairs={{0,33},{1,224},{2,35},{3,226},{4,37},{5,228},{6,39},{7,230},{8,41}... | collective-permute-start | bytes 786440 | tf_op jit(solution)/shard_map/ppermute | solution.py:59
  80.4 8.8 %collective-permute-start.24 = (f32[64,384]{1,0:T(8,128)S(1)}, f32[64,384]{1,0:T(8,128)S(1)}, u32[]{:S(2)}, u32[]{:S(2)}) collective-permute-start(f32[64,384]{1,0:T(8,128)S(1)} %add_add_fusion), channel_id=1, source_target_pairs={{0,8},{1,9},{2,10},{3,11},{4,12},{5,13},{6,14},{7,15},{8,16},{9,17... | collective-permute-start | bytes 294920 | tf_op jit(solution)/shard_map/shrink_sum/ppermute | solution.py:59
  81.8 7.4 %collective-permute-start.25 = (f32[64,384]{1,0:T(8,128)S(1)}, f32[64,384]{1,0:T(8,128)S(1)}, u32[]{:S(2)}, u32[]{:S(2)}) collective-permute-start(f32[64,384]{1,0:T(8,128)S(1)} %add_add_fusion), channel_id=1, source_target_pairs={{0,24},{1,25},{2,26},{3,27},{4,28},{5,29},{6,30},{7,31},{8,0},{9,1... | collective-permute-start | bytes 294920 | tf_op jit(solution)/shard_map/shrink_sum/ppermute | solution.py:59
  83.3 5.9 %collective-permute-start.26 = (f32[64,384]{1,0:T(8,128)S(1)}, f32[64,384]{1,0:T(8,128)S(1)}, u32[]{:S(2)}, u32[]{:S(2)}) collective-permute-start(f32[64,384]{1,0:T(8,128)S(1)} %add_add_fusion), channel_id=1, source_target_pairs={{0,16},{1,17},{2,18},{3,19},{4,20},{5,21},{6,22},{7,23},{8,24},{9,... | collective-permute-start | bytes 294920 | tf_op jit(solution)/shard_map/shrink_sum/ppermute | solution.py:59
  89.2 1.9 %collective-permute-start.28 = (f32[384,256]{1,0:T(8,128)S(1)}, f32[384,256]{1,0:T(8,128)S(1)}, u32[]{:S(2)}, u32[]{:S(2)}) collective-permute-start(f32[384,256]{1,0:T(8,128)S(1)} %get-tuple-element.84), channel_id=1, source_target_pairs={{0,1},{1,0},{2,3},{3,2},{4,5},{5,4},{6,7},{7,6},{8,9},{9,8},{10,11... | collective-permute-start | bytes 1179656 | tf_op jit(solution)/shard_map/base/ppermute | solution.py:59
  89.3 1.8 %collective-permute-start.27 = (bf16[64,384]{1,0:T(8,128)(2,1)S(1)}, bf16[64,384]{1,0:T(8,128)(2,1)S(1)}, u32[]{:S(2)}, u32[]{:S(2)}) collective-permute-start(bf16[64,384]{1,0:T(8,128)(2,1)S(1)} %multiply_convert_fusion.scaled_ref), channel_id=1, source_target_pairs={{0,1},{1,0},{2,3},{3,2},{4,5},{5,4},{6,7},{7,6},{8,9},{9,8},{10,11... | collective-permute-start | bytes 147464 | tf_op jit(solution)/shard_map/shrink_sum/ppermute | solution.py:59
  (7 other events, 7.1 us)

commit v5 on v4

--- a/solution.py
+++ b/solution.py
@@ -119,7 +119,7 @@
             out[place + j] = jnp.where(here, panel, old)
             return carry
 
-        lax.fori_loop(0, width, slot, 0, unroll=4)
+        lax.fori_loop(0, width, slot, 0, unroll=True)
 
 
 def joined(table_ref, j, same_ref, cross_ref, store_ref):
@@ -158,7 +158,7 @@
             panels[j, :, side * feats : (side + 1) * feats] = jnp.where(behind == 0, store[at], came)
         return carry
 
-    lax.fori_loop(0, WANTED, one, 0, unroll=2)
+    lax.fori_loop(0, WANTED, one, 0, unroll=True)
     flat = panels[...].reshape(WANTED * rank, 2 * feats)
     parts[...] = jnp.dot(flat, turned_ref[...], preferred_element_type=f32)
     slot = slot_ref[:, pl.ds(pl.multiple_of(core * half, 128), half)]

time: 92.7 us -> 92.4 us (level)
  transfers between devices with their start and end apart: 29 -> 29, of which waited for: 7 -> 6; matrix products, arithmetic and copies ran while one was open for 3% -> 3% of each run, Pallas kernels for 25% -> 24%
where the time goes in v5:
time: 92.4 us; the launch traced here: 92 us
  starting transfers between devices  41.2 us (45%)
  Pallas kernels  22.9 us (25%)
  waiting for transfers between devices  16.8 us (18%)
  local copies, waits for them, and re-layouts  8.78 us (10%)
  other arithmetic  1.98 us (2%)
    ppermute x29, starting transfers between devices, send(): return lax.ppermute(value, ('adapter', 'tensor'), pairs)  41.2 us
    pallas_call x13, Pallas kernels, kernel_call(): pl.pallas_call(kernel, out_shape=out_shape, in_specs=specs, out_specs=jax...  22.9 us
    ppermute x29, waiting for transfers between devices, send(): return lax.ppermute(value, ('adapter', 'tensor'), pairs)  16.8 us
    unnamed x21, local copies, waits for them, and re-layouts  7.79 us
  transfers between devices with their start and end apart: 29, of which 6 were waited for; matrix products, arithmetic and copies ran while one was open for 3% of the time, Pallas kernels for 24%

profile of v5, /device:TPU:1, one launch (start us, length us, event | category | flops | bytes accessed | tf_op | source)
XLA Modules:
  0.0 92.0 jit_solution(14933369097953004129)
XLA Ops:
  0.0 3.2 %collective-permute-start.1 = (bf16[24,64,256]{2,1,0:T(8,128)(2,1)}, bf16[24,64,256]{2,1,0:T(8,128)(2,1)S(1)}, u32[]{:S(2)}, u32[]{:S(2)}) collective-permute-start(bf16[24,64,256]{2,1,0:T(8,128)(2,1)} %refs_0_.1), channel_id=1, source_target_pairs={{0,1},{1,0},{2,3},{3,2},{4,5},{5,4},{6,7},{7,6},{8,9},{9,8},{10,11... | collective-permute-start | bytes 2359304 | tf_op jit(solution)/shard_map/ppermute | solution.py:59
  4.0 1.6 %shard_map.73 = (bf16[24,64,256]{2,1,0:T(8,128)(2,1)S(1)}, bf16[24,64,256]{2,1,0:T(8,128)(2,1)S(1)}, bf16[768,256]{1,0:T(8,128)(2,1)S(1)}) custom-call(bf16[24,64,256]{2,1,0:T(8,128)(2,1)} %refs_0_.1, bf16[24,64,256]{2,1,0:T(8,128)(2,1)} %refs_1_.1, bf16[768,256]{1,0:T(8,128)(2,1)} %refs_2_.1), custom_call_target="tpu_custom_call" | custom-call | tf_op jit(solution)/shard_map/pallas_call | solution.py:29
  7.9 2.7 %collective-permute-start.3 = (bf16[384,512]{1,0:T(8,128)(2,1)S(1)}, bf16[384,512]{1,0:T(8,128)(2,1)S(1)}, u32[]{:S(2)}, u32[]{:S(2)}) collective-permute-start(bf16[384,512]{1,0:T(8,128)(2,1)S(1)} %get-tuple-element.49), channel_id=1, source_target_pairs={{0,6},{1,25},{2,0},{3,27},{4,2},{5,29},{6,4},{7,31},{8,14},{9,1},{... | collective-permute-start | bytes 1179656 | tf_op jit(solution)/shard_map/ppermute | solution.py:59
  10.6 3.9 %collective-permute-start.5 = (bf16[8,64,256]{2,1,0:T(8,128)(2,1)S(1)}, bf16[8,64,256]{2,1,0:T(8,128)(2,1)S(1)}, u32[]{:S(2)}, u32[]{:S(2)}) collective-permute-start(bf16[8,64,256]{2,1,0:T(8,128)(2,1)S(1)} %shard_map.74), channel_id=1, source_target_pairs={{0,32},{1,225},{2,34},{3,227},{4,36},{5,229},{6,38},{7,231},{8,40}... | collective-permute-start | bytes 786440 | tf_op jit(solution)/shard_map/ppermute | solution.py:59
  14.5 3.3 %collective-permute-done.5.refs_0_ = bf16[8,64,256]{2,1,0:T(8,128)(2,1)S(1)} collective-permute-done((bf16[8,64,256]{2,1,0:T(8,128)(2,1)S(1)}, bf16[8,64,256]{2,1,0:T(8,128)(2,1)S(1)}, u32[]{:S(2)}, u32[]{:S(2)}) %collective-permute-start.5) | collective-permute-done | bytes 262176 | tf_op jit(solution)/shard_map/ppermute | solution.py:59
  18.5 3.2 %collective-permute-start.9 = (bf16[24,64,256]{2,1,0:T(8,128)(2,1)S(1)}, bf16[24,64,256]{2,1,0:T(8,128)(2,1)S(1)}, u32[]{:S(2)}, u32[]{:S(2)}) collective-permute-start(bf16[24,64,256]{2,1,0:T(8,128)(2,1)S(1)} %shard_map.76), channel_id=1, source_target_pairs={{0,32},{1,225},{2,34},{3,227},{4,36},{5,229},{6,38},{7,231},{8,40}... | collective-permute-start | bytes 2359304 | tf_op jit(solution)/shard_map/ppermute | solution.py:59
  22.1 1.3 %collective-permute-start.6 = (bf16[2,384,512]{2,1,0:T(8,128)(2,1)S(1)}, bf16[2,384,512]{2,1,0:T(8,128)(2,1)}, u32[]{:S(2)}, u32[]{:S(2)}) collective-permute-start(bf16[2,384,512]{2,1,0:T(8,128)(2,1)S(1)} %pad_maximum_fusion.refs_0_), channel_id=1, source_target_pairs={{0,8},{1,3},{2,10},{3,5},{4,12},{5,7},{6,14},{7,1},{8,16},{9,11},{... | collective-permute-start | bytes 2359304 | tf_op jit(solution)/shard_map/ppermute | solution.py:59
  23.4 1.5 %collective-permute-start.7 = (bf16[2,384,512]{2,1,0:T(8,128)(2,1)S(1)}, bf16[2,384,512]{2,1,0:T(8,128)(2,1)S(1)}, u32[]{:S(2)}, u32[]{:S(2)}) collective-permute-start(bf16[2,384,512]{2,1,0:T(8,128)(2,1)S(1)} %pad_maximum_fusion.refs_0_), channel_id=1, source_target_pairs={{0,24},{1,7},{2,26},{3,1},{4,28},{5,3},{6,30},{7,5},{8,0},{9,15},{... | collective-permute-start | bytes 2359304 | tf_op jit(solution)/shard_map/ppermute | solution.py:59
  25.8 8.3 %collective-permute-done.8 = bf16[384,512]{1,0:T(8,128)(2,1)S(1)} collective-permute-done((bf16[384,512]{1,0:T(8,128)(2,1)S(1)}, bf16[384,512]{1,0:T(8,128)(2,1)S(1)}, u32[]{:S(2)}, u32[]{:S(2)}) %collective-permute-start.8) | collective-permute-done | bytes 393248 | tf_op jit(solution)/shard_map/ppermute | solution.py:59
  34.1 1.7 %shard_map.77 = bf16[32,64,256]{2,1,0:T(8,128)(2,1)} custom-call(s32[256]{0:T(256)S(1)} %pad_add_fusion.table_ref, bf16[24,64,256]{2,1,0:T(8,128)(2,1)S(1)} %collective-permute-done.9.refs_0_, bf16[24,64,256]{2,1,0:T(8,128)(2,1)S(1)} %get-tuple-element.47.refs_0_.refs_1_.mine_ref, bf16[24,64,256]{2,1,0:T(8,128)(2,1)S(1)} %collective-permute-done.1.refs_1_.refs_2_.sib_ref, ...), custom_call_target="tpu_custom_call" | custom-call | tf_op jit(solution)/shard_map/pallas_call | solution.py:29
  35.9 2.1 %collective-permute-done.6.refs_1_ = bf16[2,384,512]{2,1,0:T(8,128)(2,1)} collective-permute-done((bf16[2,384,512]{2,1,0:T(8,128)(2,1)S(1)}, bf16[2,384,512]{2,1,0:T(8,128)(2,1)}, u32[]{:S(2)}, u32[]{:S(2)}) %collective-permute-start.6) | collective-permute-done | bytes 786464 | tf_op jit(solution)/shard_map/ppermute | solution.py:59
  40.0 2.7 %collective-permute-start.14 = (bf16[2,384,512]{2,1,0:T(8,128)(2,1)}, bf16[2,384,512]{2,1,0:T(8,128)(2,1)}, u32[]{:S(2)}, u32[]{:S(2)}) collective-permute-start(bf16[2,384,512]{2,1,0:T(8,128)(2,1)} %pad_maximum_fusion.1.refs_1_), channel_id=1, source_target_pairs={{0,24},{1,7},{2,26},{3,1},{4,28},{5,3},{6,30},{7,5},{8,0},{9,15},{... | collective-permute-start | bytes 2359304 | tf_op jit(solution)/shard_map/ppermute | solution.py:59
  42.7 1.1 %copy-done.5 = bf16[2,384,512]{2,1,0:T(8,128)(2,1)S(1)} copy-done((bf16[2,384,512]{2,1,0:T(8,128)(2,1)S(1)}, bf16[2,384,512]{2,1,0:T(8,128)(2,1)}, u32[]{:S(2)}) %copy-start.5) | copy-done | bytes 786456
  45.0 4.2 %shard_map.78.refs_0_ = f32[2,384,256]{2,1,0:T(8,128)S(1)} custom-call(s32[6]{0:T(128)S(1)} %stack.81.block_ref, bf16[2,384,512]{2,1,0:T(8,128)(2,1)S(1)} %copy-done.5, bf16[2,384,512]{2,1,0:T(8,128)(2,1)} %collective-permute-done.6.refs_1_, bf16[2,384,512]{2,1,0:T(8,128)(2,1)S(1)} %copy-done.7, bf16[16,512,256]{2,1,0:T(8,128)(2,1)} %bitcast.10.refs_3_.refs_4_, ...), custom_call_target="tpu_custom_call" | custom-call | tf_op jit(solution)/shard_map/pallas_call | solution.py:29
  50.1 2.4 %shard_map.79 = (bf16[16,64,256]{2,1,0:T(8,128)(2,1)}, bf16[16,64,256]{2,1,0:T(8,128)(2,1)}) custom-call(s32[256]{0:T(256)S(1)} %pad_add_fusion.table_ref, bf16[32,64,256]{2,1,0:T(8,128)(2,1)} %collective-permute-done.11.refs_0_, bf16[24,64,256]{2,1,0:T(8,128)(2,1)S(1)} %get-tuple-element.47.refs_0_.refs_1_.mine_ref, ...), custom_call_target="tpu_custom_call" | custom-call | tf_op jit(solution)/shard_map/pallas_call | solution.py:29
  52.5 1.3 %collective-permute-start.12 = (bf16[16,64,256]{2,1,0:T(8,128)(2,1)}, bf16[16,64,256]{2,1,0:T(8,128)(2,1)}, u32[]{:S(2)}, u32[]{:S(2)}) collective-permute-start(bf16[16,64,256]{2,1,0:T(8,128)(2,1)} %get-tuple-element.65), channel_id=1, source_target_pairs={{0,32},{1,225},{2,34},{3,227},{4,36},{5,229},{6,38},{7,231},{8,40}... | collective-permute-start | bytes 1572872 | tf_op jit(solution)/shard_map/ppermute | solution.py:59
  53.8 1.2 %collective-permute-start.16 = (bf16[2,384,512]{2,1,0:T(8,128)(2,1)}, bf16[2,384,512]{2,1,0:T(8,128)(2,1)}, u32[]{:S(2)}, u32[]{:S(2)}) collective-permute-start(bf16[2,384,512]{2,1,0:T(8,128)(2,1)} %collective-permute-done.6.refs_1_), channel_id=1, source_target_pairs={{0,8},{1,3},{2,10},{3,5},{4,12},{5,7},{6,14},{7,1},{8,16},{9,11},{... | collective-permute-start | bytes 2359304 | tf_op jit(solution)/shard_map/ppermute | solution.py:59
  55.0 1.6 %collective-permute-start.22 = (bf16[2,384,512]{2,1,0:T(8,128)(2,1)}, bf16[2,384,512]{2,1,0:T(8,128)(2,1)}, u32[]{:S(2)}, u32[]{:S(2)}) collective-permute-start(bf16[2,384,512]{2,1,0:T(8,128)(2,1)} %collective-permute-done.14.refs_3_), channel_id=1, source_target_pairs={{0,24},{1,7},{2,26},{3,1},{4,28},{5,3},{6,30},{7,5},{8,0},{9,15},{... | collective-permute-start | bytes 2359304 | tf_op jit(solution)/shard_map/ppermute | solution.py:59
  57.9 4.1 %shard_map.80.refs_0_ = f32[2,384,256]{2,1,0:T(8,128)S(1)} custom-call(s32[6]{0:T(128)S(1)} %stack.94.block_ref, f32[2,384,256]{2,1,0:T(8,128)S(1)} %copy-done.1, bf16[2,384,512]{2,1,0:T(8,128)(2,1)} %pad_maximum_fusion.1.refs_1_, bf16[2,384,512]{2,1,0:T(8,128)(2,1)} %collective-permute-done.13.refs_2_, ...), custom_call_target="tpu_custom_call" | custom-call | tf_op jit(solution)/shard_map/pallas_call | solution.py:29
  62.9 2.3 %collective-permute-start.15 = (bf16[16,64,256]{2,1,0:T(8,128)(2,1)}, bf16[16,64,256]{2,1,0:T(8,128)(2,1)}, u32[]{:S(2)}, u32[]{:S(2)}) collective-permute-start(bf16[16,64,256]{2,1,0:T(8,128)(2,1)} %collective-permute-done.12.here_ref), channel_id=1, source_target_pairs={{0,1},{1,0},{2,3},{3,2},{4,5},{5,4},{6,7},{7,6},{8,9},{9,8},{10,11... | collective-permute-start | bytes 1572872 | tf_op jit(solution)/shard_map/shrink/ppermute | solution.py:59
  65.2 1.8 %collective-permute-start.17 = (bf16[16,64,256]{2,1,0:T(8,128)(2,1)}, bf16[16,64,256]{2,1,0:T(8,128)(2,1)}, u32[]{:S(2)}, u32[]{:S(2)}) collective-permute-start(bf16[16,64,256]{2,1,0:T(8,128)(2,1)} %get-tuple-element.72), channel_id=1, source_target_pairs={{0,32},{1,225},{2,34},{3,227},{4,36},{5,229},{6,38},{7,231},{8,40}... | collective-permute-start | bytes 1572872 | tf_op jit(solution)/shard_map/ppermute | solution.py:59
  67.1 1.7 %shrink.1 = f32[64,384]{1,0:T(8,128)S(1)} custom-call(s32[256]{0:T(256)S(1)} %pad_add_fusion.table_ref, bf16[16,64,256]{2,1,0:T(8,128)(2,1)} %collective-permute-done.12.here_ref, bf16[16,64,256]{2,1,0:T(8,128)(2,1)} %collective-permute-done.15.other_ref, bf16[24,64,256]{2,1,0:T(8,128)(2,1)S(1)} %get-tuple-element.47.refs_0_.refs_1_.mine_ref, ...), custom_call_target="tpu_custom_call" | custom-call | tf_op jit(solution)/shard_map/shrink/pallas_call | solution.py:29
  69.4 2.2 %collective-permute-start.20 = (f32[64,384]{1,0:T(8,128)S(1)}, f32[64,384]{1,0:T(8,128)S(1)}, u32[]{:S(2)}, u32[]{:S(2)}) collective-permute-start(f32[64,384]{1,0:T(8,128)S(1)} %shrink.1), channel_id=1, source_target_pairs={{0,6},{1,7},{2,0},{3,1},{4,2},{5,3},{6,4},{7,5},{8,14},{9,15},{10,... | collective-permute-start | bytes 294920 | tf_op jit(solution)/shard_map/shrink_sum/ppermute | solution.py:59
  72.2 1.6 %collective-permute-done.17.refs_0_ = bf16[16,64,256]{2,1,0:T(8,128)(2,1)} collective-permute-done((bf16[16,64,256]{2,1,0:T(8,128)(2,1)}, bf16[16,64,256]{2,1,0:T(8,128)(2,1)}, u32[]{:S(2)}, u32[]{:S(2)}) %collective-permute-start.17) | collective-permute-done | bytes 524320 | tf_op jit(solution)/shard_map/ppermute | solution.py:59
  73.9 1.1 %shard_map.81 = (bf16[8,64,256]{2,1,0:T(8,128)(2,1)S(1)}, bf16[8,64,256]{2,1,0:T(8,128)(2,1)S(1)}) custom-call(s32[256]{0:T(256)S(1)} %pad_add_fusion.table_ref, bf16[16,64,256]{2,1,0:T(8,128)(2,1)} %collective-permute-done.17.refs_0_, bf16[24,64,256]{2,1,0:T(8,128)(2,1)S(1)} %get-tuple-element.47.refs_0_.refs_1_.mine_ref, ...), custom_call_target="tpu_custom_call" | custom-call | tf_op jit(solution)/shard_map/pallas_call | solution.py:29
  75.0 2.9 %collective-permute-start.18 = (bf16[8,64,256]{2,1,0:T(8,128)(2,1)S(1)}, bf16[8,64,256]{2,1,0:T(8,128)(2,1)S(1)}, u32[]{:S(2)}, u32[]{:S(2)}) collective-permute-start(bf16[8,64,256]{2,1,0:T(8,128)(2,1)S(1)} %get-tuple-element.74), channel_id=1, source_target_pairs={{0,32},{1,225},{2,34},{3,227},{4,36},{5,229},{6,38},{7,231},{8,40}... | collective-permute-start | bytes 786440 | tf_op jit(solution)/shard_map/ppermute | solution.py:59
  77.9 2.1 %collective-permute-start.23 = (bf16[8,64,256]{2,1,0:T(8,128)(2,1)S(1)}, bf16[8,64,256]{2,1,0:T(8,128)(2,1)S(1)}, u32[]{:S(2)}, u32[]{:S(2)}) collective-permute-start(bf16[8,64,256]{2,1,0:T(8,128)(2,1)S(1)} %get-tuple-element.80), channel_id=1, source_target_pairs={{0,33},{1,224},{2,35},{3,226},{4,37},{5,228},{6,39},{7,230},{8,41}... | collective-permute-start | bytes 786440 | tf_op jit(solution)/shard_map/ppermute | solution.py:59
  80.1 1.4 %collective-permute-start.24 = (f32[64,384]{1,0:T(8,128)S(1)}, f32[64,384]{1,0:T(8,128)S(1)}, u32[]{:S(2)}, u32[]{:S(2)}) collective-permute-start(f32[64,384]{1,0:T(8,128)S(1)} %add_add_fusion), channel_id=1, source_target_pairs={{0,8},{1,9},{2,10},{3,11},{4,12},{5,13},{6,14},{7,15},{8,16},{9,17... | collective-permute-start | bytes 294920 | tf_op jit(solution)/shard_map/shrink_sum/ppermute | solution.py:59
  81.5 1.5 %collective-permute-start.25 = (f32[64,384]{1,0:T(8,128)S(1)}, f32[64,384]{1,0:T(8,128)S(1)}, u32[]{:S(2)}, u32[]{:S(2)}) collective-permute-start(f32[64,384]{1,0:T(8,128)S(1)} %add_add_fusion), channel_id=1, source_target_pairs={{0,24},{1,25},{2,26},{3,27},{4,28},{5,29},{6,30},{7,31},{8,0},{9,1... | collective-permute-start | bytes 294920 | tf_op jit(solution)/shard_map/shrink_sum/ppermute | solution.py:59
  83.0 1.6 %collective-permute-start.26 = (f32[64,384]{1,0:T(8,128)S(1)}, f32[64,384]{1,0:T(8,128)S(1)}, u32[]{:S(2)}, u32[]{:S(2)}) collective-permute-start(f32[64,384]{1,0:T(8,128)S(1)} %add_add_fusion), channel_id=1, source_target_pairs={{0,16},{1,17},{2,18},{3,19},{4,20},{5,21},{6,22},{7,23},{8,24},{9,... | collective-permute-start | bytes 294920 | tf_op jit(solution)/shard_map/shrink_sum/ppermute | solution.py:59
  84.5 3.3 %shard_map.82 = f32[2,384,256]{2,1,0:T(8,128)S(1)} custom-call(s32[4]{0:T(128)S(1)} %pad_add_fusion.1.block_ref, f32[2,384,256]{2,1,0:T(8,128)S(1)} %copy-done.3, bf16[2,384,512]{2,1,0:T(8,128)(2,1)} %collective-permute-done.16.refs_1_, bf16[2,384,512]{2,1,0:T(8,128)(2,1)} %collective-permute-done.22.refs_2_, bf16[16,512,256]{2,1,0:T(8,128)(2,1)} %bitcast.10.refs_3_.refs_4_, ...), custom_call_target="tpu_custom_call" | custom-call | tf_op jit(solution)/shard_map/pallas_call | solution.py:29
  89.5 1.3 %collective-permute-done.27.other_ref = bf16[64,384]{1,0:T(8,128)(2,1)S(1)} collective-permute-done((bf16[64,384]{1,0:T(8,128)(2,1)S(1)}, bf16[64,384]{1,0:T(8,128)(2,1)S(1)}, u32[]{:S(2)}, u32[]{:S(2)}) %collective-permute-start.27) | collective-permute-done | bytes 49184 | tf_op jit(solution)/shard_map/shrink_sum/ppermute | solution.py:59
  (71 shorter events, 15.5 us)
Async XLA Ops:
  0.0 6.3 %collective-permute-start.1 = (bf16[24,64,256]{2,1,0:T(8,128)(2,1)}, bf16[24,64,256]{2,1,0:T(8,128)(2,1)S(1)}, u32[]{:S(2)}, u32[]{:S(2)}) collective-permute-start(bf16[24,64,256]{2,1,0:T(8,128)(2,1)} %refs_0_.1), channel_id=1, source_target_pairs={{0,1},{1,0},{2,3},{3,2},{4,5},{5,4},{6,7},{7,6},{8,9},{9,8},{10,11... | collective-permute-start | bytes 2359304 | tf_op jit(solution)/shard_map/ppermute | solution.py:59
  3.2 3.7 %collective-permute-start = (bf16[768,256]{1,0:T(8,128)(2,1)}, bf16[768,256]{1,0:T(8,128)(2,1)S(1)}, u32[]{:S(2)}, u32[]{:S(2)}) collective-permute-start(bf16[768,256]{1,0:T(8,128)(2,1)} %refs_2_.1), channel_id=1, source_target_pairs={{0,1},{1,0},{2,3},{3,2},{4,5},{5,4},{6,7},{7,6},{8,9},{9,8},{10,11... | collective-permute-start | bytes 1179656 | tf_op jit(solution)/shard_map/ppermute | solution.py:59
  4.0 3.8 %copy-start.8 = (bf16[24,64,256]{2,1,0:T(8,128)(2,1)S(1)}, bf16[24,64,256]{2,1,0:T(8,128)(2,1)}, u32[]{:S(2)}) copy-start(bf16[24,64,256]{2,1,0:T(8,128)(2,1)} %refs_1_.1) | copy-start | bytes 2359300
  7.2 35.5 %collective-permute-start.10 = (bf16[8192,256]{1,0:T(8,128)(2,1)}, bf16[8192,256]{1,0:T(8,128)(2,1)}, u32[]{:S(2)}, u32[]{:S(2)}) collective-permute-start(bf16[8192,256]{1,0:T(8,128)(2,1)} %param.8), channel_id=1, source_target_pairs={{0,1},{1,0},{2,3},{3,2},{4,5},{5,4},{6,7},{7,6},{8,9},{9,8},{10,11... | collective-permute-start | bytes 12582920 | tf_op jit(solution)/shard_map/ppermute | solution.py:59
  7.8 10.0 %collective-permute-start.4 = (bf16[24,64,256]{2,1,0:T(8,128)(2,1)S(1)}, bf16[24,64,256]{2,1,0:T(8,128)(2,1)S(1)}, u32[]{:S(2)}, u32[]{:S(2)}) collective-permute-start(bf16[24,64,256]{2,1,0:T(8,128)(2,1)S(1)} %copy-done.8), channel_id=1, source_target_pairs={{0,1},{1,0},{2,3},{3,2},{4,5},{5,4},{6,7},{7,6},{8,9},{9,8},{10,11... | collective-permute-start | bytes 2359304 | tf_op jit(solution)/shard_map/ppermute | solution.py:59
  7.9 9.9 %collective-permute-start.2 = (bf16[384,512]{1,0:T(8,128)(2,1)S(1)}, bf16[384,512]{1,0:T(8,128)(2,1)S(1)}, u32[]{:S(2)}, u32[]{:S(2)}) collective-permute-start(bf16[384,512]{1,0:T(8,128)(2,1)S(1)} %get-tuple-element.49), channel_id=1, source_target_pairs={{0,2},{1,9},{2,4},{3,11},{4,6},{5,13},{6,0},{7,15},{8,10},{9,17},{... | collective-permute-start | bytes 1179656 | tf_op jit(solution)/shard_map/ppermute | solution.py:59
  7.9 9.9 %collective-permute-start.3 = (bf16[384,512]{1,0:T(8,128)(2,1)S(1)}, bf16[384,512]{1,0:T(8,128)(2,1)S(1)}, u32[]{:S(2)}, u32[]{:S(2)}) collective-permute-start(bf16[384,512]{1,0:T(8,128)(2,1)S(1)} %get-tuple-element.49), channel_id=1, source_target_pairs={{0,6},{1,25},{2,0},{3,27},{4,2},{5,29},{6,4},{7,31},{8,14},{9,1},{... | collective-permute-start | bytes 1179656 | tf_op jit(solution)/shard_map/ppermute | solution.py:59
  10.6 7.2 %collective-permute-start.5 = (bf16[8,64,256]{2,1,0:T(8,128)(2,1)S(1)}, bf16[8,64,256]{2,1,0:T(8,128)(2,1)S(1)}, u32[]{:S(2)}, u32[]{:S(2)}) collective-permute-start(bf16[8,64,256]{2,1,0:T(8,128)(2,1)S(1)} %shard_map.74), channel_id=1, source_target_pairs={{0,32},{1,225},{2,34},{3,227},{4,36},{5,229},{6,38},{7,231},{8,40}... | collective-permute-start | bytes 786440 | tf_op jit(solution)/shard_map/ppermute | solution.py:59
  18.5 15.6 %collective-permute-start.9 = (bf16[24,64,256]{2,1,0:T(8,128)(2,1)S(1)}, bf16[24,64,256]{2,1,0:T(8,128)(2,1)S(1)}, u32[]{:S(2)}, u32[]{:S(2)}) collective-permute-start(bf16[24,64,256]{2,1,0:T(8,128)(2,1)S(1)} %shard_map.76), channel_id=1, source_target_pairs={{0,32},{1,225},{2,34},{3,227},{4,36},{5,229},{6,38},{7,231},{8,40}... | collective-permute-start | bytes 2359304 | tf_op jit(solution)/shard_map/ppermute | solution.py:59
  21.7 12.4 %collective-permute-start.8 = (bf16[384,512]{1,0:T(8,128)(2,1)S(1)}, bf16[384,512]{1,0:T(8,128)(2,1)S(1)}, u32[]{:S(2)}, u32[]{:S(2)}) collective-permute-start(bf16[384,512]{1,0:T(8,128)(2,1)S(1)} %collective-permute-done.2), channel_id=1, source_target_pairs={{0,2},{1,9},{2,4},{3,11},{4,6},{5,13},{6,0},{7,15},{8,10},{9,17},{... | collective-permute-start | bytes 1179656 | tf_op jit(solution)/shard_map/ppermute | solution.py:59
  22.1 15.9 %collective-permute-start.6 = (bf16[2,384,512]{2,1,0:T(8,128)(2,1)S(1)}, bf16[2,384,512]{2,1,0:T(8,128)(2,1)}, u32[]{:S(2)}, u32[]{:S(2)}) collective-permute-start(bf16[2,384,512]{2,1,0:T(8,128)(2,1)S(1)} %pad_maximum_fusion.refs_0_), channel_id=1, source_target_pairs={{0,8},{1,3},{2,10},{3,5},{4,12},{5,7},{6,14},{7,1},{8,16},{9,11},{... | collective-permute-start | bytes 2359304 | tf_op jit(solution)/shard_map/ppermute | solution.py:59
  23.4 14.6 %collective-permute-start.7 = (bf16[2,384,512]{2,1,0:T(8,128)(2,1)S(1)}, bf16[2,384,512]{2,1,0:T(8,128)(2,1)S(1)}, u32[]{:S(2)}, u32[]{:S(2)}) collective-permute-start(bf16[2,384,512]{2,1,0:T(8,128)(2,1)S(1)} %pad_maximum_fusion.refs_0_), channel_id=1, source_target_pairs={{0,24},{1,7},{2,26},{3,1},{4,28},{5,3},{6,30},{7,5},{8,0},{9,15},{... | collective-permute-start | bytes 2359304 | tf_op jit(solution)/shard_map/ppermute | solution.py:59
  35.8 14.3 %collective-permute-start.11 = (bf16[32,64,256]{2,1,0:T(8,128)(2,1)}, bf16[32,64,256]{2,1,0:T(8,128)(2,1)}, u32[]{:S(2)}, u32[]{:S(2)}) collective-permute-start(bf16[32,64,256]{2,1,0:T(8,128)(2,1)} %shard_map.77), channel_id=1, source_target_pairs={{0,32},{1,225},{2,34},{3,227},{4,36},{5,229},{6,38},{7,231},{8,40}... | collective-permute-start | bytes 3145736 | tf_op jit(solution)/shard_map/ppermute | solution.py:59
  39.9 15.0 %collective-permute-start.13 = (bf16[2,384,512]{2,1,0:T(8,128)(2,1)}, bf16[2,384,512]{2,1,0:T(8,128)(2,1)}, u32[]{:S(2)}, u32[]{:S(2)}) collective-permute-start(bf16[2,384,512]{2,1,0:T(8,128)(2,1)} %pad_maximum_fusion.1.refs_1_), channel_id=1, source_target_pairs={{0,8},{1,3},{2,10},{3,5},{4,12},{5,7},{6,14},{7,1},{8,16},{9,11},{... | collective-permute-start | bytes 2359304 | tf_op jit(solution)/shard_map/ppermute | solution.py:59
  40.0 15.0 %collective-permute-start.14 = (bf16[2,384,512]{2,1,0:T(8,128)(2,1)}, bf16[2,384,512]{2,1,0:T(8,128)(2,1)}, u32[]{:S(2)}, u32[]{:S(2)}) collective-permute-start(bf16[2,384,512]{2,1,0:T(8,128)(2,1)} %pad_maximum_fusion.1.refs_1_), channel_id=1, source_target_pairs={{0,24},{1,7},{2,26},{3,1},{4,28},{5,3},{6,30},{7,5},{8,0},{9,15},{... | collective-permute-start | bytes 2359304 | tf_op jit(solution)/shard_map/ppermute | solution.py:59
  52.5 10.4 %collective-permute-start.12 = (bf16[16,64,256]{2,1,0:T(8,128)(2,1)}, bf16[16,64,256]{2,1,0:T(8,128)(2,1)}, u32[]{:S(2)}, u32[]{:S(2)}) collective-permute-start(bf16[16,64,256]{2,1,0:T(8,128)(2,1)} %get-tuple-element.65), channel_id=1, source_target_pairs={{0,32},{1,225},{2,34},{3,227},{4,36},{5,229},{6,38},{7,231},{8,40}... | collective-permute-start | bytes 1572872 | tf_op jit(solution)/shard_map/ppermute | solution.py:59
  53.8 15.1 %collective-permute-start.16 = (bf16[2,384,512]{2,1,0:T(8,128)(2,1)}, bf16[2,384,512]{2,1,0:T(8,128)(2,1)}, u32[]{:S(2)}, u32[]{:S(2)}) collective-permute-start(bf16[2,384,512]{2,1,0:T(8,128)(2,1)} %collective-permute-done.6.refs_1_), channel_id=1, source_target_pairs={{0,8},{1,3},{2,10},{3,5},{4,12},{5,7},{6,14},{7,1},{8,16},{9,11},{... | collective-permute-start | bytes 2359304 | tf_op jit(solution)/shard_map/ppermute | solution.py:59
  55.0 22.9 %collective-permute-start.22 = (bf16[2,384,512]{2,1,0:T(8,128)(2,1)}, bf16[2,384,512]{2,1,0:T(8,128)(2,1)}, u32[]{:S(2)}, u32[]{:S(2)}) collective-permute-start(bf16[2,384,512]{2,1,0:T(8,128)(2,1)} %collective-permute-done.14.refs_3_), channel_id=1, source_target_pairs={{0,24},{1,7},{2,26},{3,1},{4,28},{5,3},{6,30},{7,5},{8,0},{9,15},{... | collective-permute-start | bytes 2359304 | tf_op jit(solution)/shard_map/ppermute | solution.py:59
  57.9 9.1 %copy-start.9 = (s32[768]{0:T(1024)S(1)}, s32[768]{0:T(1024)}, u32[]{:S(2)}) copy-start(s32[768]{0:T(1024)} %param.13) | copy-start | bytes 9220
  62.9 4.2 %collective-permute-start.15 = (bf16[16,64,256]{2,1,0:T(8,128)(2,1)}, bf16[16,64,256]{2,1,0:T(8,128)(2,1)}, u32[]{:S(2)}, u32[]{:S(2)}) collective-permute-start(bf16[16,64,256]{2,1,0:T(8,128)(2,1)} %collective-permute-done.12.here_ref), channel_id=1, source_target_pairs={{0,1},{1,0},{2,3},{3,2},{4,5},{5,4},{6,7},{7,6},{8,9},{9,8},{10,11... | collective-permute-start | bytes 1572872 | tf_op jit(solution)/shard_map/shrink/ppermute | solution.py:59
  65.2 8.6 %collective-permute-start.17 = (bf16[16,64,256]{2,1,0:T(8,128)(2,1)}, bf16[16,64,256]{2,1,0:T(8,128)(2,1)}, u32[]{:S(2)}, u32[]{:S(2)}) collective-permute-start(bf16[16,64,256]{2,1,0:T(8,128)(2,1)} %get-tuple-element.72), channel_id=1, source_target_pairs={{0,32},{1,225},{2,34},{3,227},{4,36},{5,229},{6,38},{7,231},{8,40}... | collective-permute-start | bytes 1572872 | tf_op jit(solution)/shard_map/ppermute | solution.py:59
  67.0 17.5 %copy-start.3 = (f32[2,384,256]{2,1,0:T(8,128)S(1)}, f32[2,384,256]{2,1,0:T(8,128)}, u32[]{:S(2)}) copy-start(f32[2,384,256]{2,1,0:T(8,128)} %copy-done.2) | copy-start | bytes 2359300
  68.8 11.2 %collective-permute-start.19 = (f32[64,384]{1,0:T(8,128)S(1)}, f32[64,384]{1,0:T(8,128)S(1)}, u32[]{:S(2)}, u32[]{:S(2)}) collective-permute-start(f32[64,384]{1,0:T(8,128)S(1)} %shrink.1), channel_id=1, source_target_pairs={{0,2},{1,3},{2,4},{3,5},{4,6},{5,7},{6,0},{7,1},{8,10},{9,11},{10,... | collective-permute-start | bytes 294920 | tf_op jit(solution)/shard_map/shrink_sum/ppermute | solution.py:59
  69.4 10.6 %collective-permute-start.20 = (f32[64,384]{1,0:T(8,128)S(1)}, f32[64,384]{1,0:T(8,128)S(1)}, u32[]{:S(2)}, u32[]{:S(2)}) collective-permute-start(f32[64,384]{1,0:T(8,128)S(1)} %shrink.1), channel_id=1, source_target_pairs={{0,6},{1,7},{2,0},{3,1},{4,2},{5,3},{6,4},{7,5},{8,14},{9,15},{10,... | collective-permute-start | bytes 294920 | tf_op jit(solution)/shard_map/shrink_sum/ppermute | solution.py:59
  71.6 8.4 %collective-permute-start.21 = (f32[64,384]{1,0:T(8,128)S(1)}, f32[64,384]{1,0:T(8,128)S(1)}, u32[]{:S(2)}, u32[]{:S(2)}) collective-permute-start(f32[64,384]{1,0:T(8,128)S(1)} %shrink.1), channel_id=1, source_target_pairs={{0,4},{1,5},{2,6},{3,7},{4,0},{5,1},{6,2},{7,3},{8,12},{9,13},{10,... | collective-permute-start | bytes 294920 | tf_op jit(solution)/shard_map/shrink_sum/ppermute | solution.py:59
  75.0 12.9 %collective-permute-start.18 = (bf16[8,64,256]{2,1,0:T(8,128)(2,1)S(1)}, bf16[8,64,256]{2,1,0:T(8,128)(2,1)S(1)}, u32[]{:S(2)}, u32[]{:S(2)}) collective-permute-start(bf16[8,64,256]{2,1,0:T(8,128)(2,1)S(1)} %get-tuple-element.74), channel_id=1, source_target_pairs={{0,32},{1,225},{2,34},{3,227},{4,36},{5,229},{6,38},{7,231},{8,40}... | collective-permute-start | bytes 786440 | tf_op jit(solution)/shard_map/ppermute | solution.py:59
  77.9 10.0 %collective-permute-start.23 = (bf16[8,64,256]{2,1,0:T(8,128)(2,1)S(1)}, bf16[8,64,256]{2,1,0:T(8,128)(2,1)S(1)}, u32[]{:S(2)}, u32[]{:S(2)}) collective-permute-start(bf16[8,64,256]{2,1,0:T(8,128)(2,1)S(1)} %get-tuple-element.80), channel_id=1, source_target_pairs={{0,33},{1,224},{2,35},{3,226},{4,37},{5,228},{6,39},{7,230},{8,41}... | collective-permute-start | bytes 786440 | tf_op jit(solution)/shard_map/ppermute | solution.py:59
  80.1 8.8 %collective-permute-start.24 = (f32[64,384]{1,0:T(8,128)S(1)}, f32[64,384]{1,0:T(8,128)S(1)}, u32[]{:S(2)}, u32[]{:S(2)}) collective-permute-start(f32[64,384]{1,0:T(8,128)S(1)} %add_add_fusion), channel_id=1, source_target_pairs={{0,8},{1,9},{2,10},{3,11},{4,12},{5,13},{6,14},{7,15},{8,16},{9,17... | collective-permute-start | bytes 294920 | tf_op jit(solution)/shard_map/shrink_sum/ppermute | solution.py:59
  81.5 7.4 %collective-permute-start.25 = (f32[64,384]{1,0:T(8,128)S(1)}, f32[64,384]{1,0:T(8,128)S(1)}, u32[]{:S(2)}, u32[]{:S(2)}) collective-permute-start(f32[64,384]{1,0:T(8,128)S(1)} %add_add_fusion), channel_id=1, source_target_pairs={{0,24},{1,25},{2,26},{3,27},{4,28},{5,29},{6,30},{7,31},{8,0},{9,1... | collective-permute-start | bytes 294920 | tf_op jit(solution)/shard_map/shrink_sum/ppermute | solution.py:59
  83.0 5.9 %collective-permute-start.26 = (f32[64,384]{1,0:T(8,128)S(1)}, f32[64,384]{1,0:T(8,128)S(1)}, u32[]{:S(2)}, u32[]{:S(2)}) collective-permute-start(f32[64,384]{1,0:T(8,128)S(1)} %add_add_fusion), channel_id=1, source_target_pairs={{0,16},{1,17},{2,18},{3,19},{4,20},{5,21},{6,22},{7,23},{8,24},{9,... | collective-permute-start | bytes 294920 | tf_op jit(solution)/shard_map/shrink_sum/ppermute | solution.py:59
  88.9 1.9 %collective-permute-start.28 = (f32[384,256]{1,0:T(8,128)S(1)}, f32[384,256]{1,0:T(8,128)S(1)}, u32[]{:S(2)}, u32[]{:S(2)}) collective-permute-start(f32[384,256]{1,0:T(8,128)S(1)} %get-tuple-element.84), channel_id=1, source_target_pairs={{0,1},{1,0},{2,3},{3,2},{4,5},{5,4},{6,7},{7,6},{8,9},{9,8},{10,11... | collective-permute-start | bytes 1179656 | tf_op jit(solution)/shard_map/base/ppermute | solution.py:59
  89.0 1.8 %collective-permute-start.27 = (bf16[64,384]{1,0:T(8,128)(2,1)S(1)}, bf16[64,384]{1,0:T(8,128)(2,1)S(1)}, u32[]{:S(2)}, u32[]{:S(2)}) collective-permute-start(bf16[64,384]{1,0:T(8,128)(2,1)S(1)} %multiply_convert_fusion.scaled_ref), channel_id=1, source_target_pairs={{0,1},{1,0},{2,3},{3,2},{4,5},{5,4},{6,7},{7,6},{8,9},{9,8},{10,11... | collective-permute-start | bytes 147464 | tf_op jit(solution)/shard_map/shrink_sum/ppermute | solution.py:59
  (7 other events, 7.1 us)

commit v6 on v5

--- a/solution.py
+++ b/solution.py
@@ -200,11 +200,12 @@
     lax.fori_loop(0, len(pieces), piece, 0)
 
 
-def expand_kernel(panels_ref, scaled_ref, other_ref, slot_ref, here_ref, there_ref, out_ref):
+def expand_kernel(panels_ref, scaled_ref, other_ref, slot_ref, here_ref, there_ref, out_ref, halves, sems):
     core = lax.rem(lax.axis_index("tensor"), 2)
     wanted, rank, columns = panels_ref.shape
     half = scaled_ref.shape[1]
     panel = panels_ref[...].reshape(wanted * rank, columns)
+    stores = []
     for part in range(2):
         mine = core == part
         scaled = jnp.where(mine, scaled_ref[...], other_ref[...])
@@ -214,7 +215,11 @@
             [jnp.where(slot == j, scaled, jnp.zeros_like(scaled)) for j in range(wanted)], axis=0
         )
         total = base + lax.dot_general(delta, panel, (((0,), (0,)), ((), ())), preferred_element_type=f32)
-        out_ref[part * half : (part + 1) * half, :] = total.astype(out_ref.dtype)
+        halves[part] = total.astype(halves.dtype)
+        stores.append(pltpu.make_async_copy(halves.at[part], out_ref.at[pl.ds(part * half, half)], sems.at[part]))
+        stores[part].start()
+    for store in stores:
+        store.wait()
 
 
 def own_kernel(hidden_ref, got_ref, out_ref, turned_ref):
@@ -378,10 +383,15 @@
         base_there = to_sibling(after(base[1], scaled))
 
     with jax.named_scope("expand"):
-        return kernel_call(
-            expand_kernel, jax.ShapeDtypeStruct((rows, columns), bf16),
-            up_here, scaled, scaled_other, slot_row, base_here, base_there,
-        )
+        inputs = up_here, scaled, scaled_other, slot_row, base_here, base_there
+        return pl.pallas_call(
+            expand_kernel,
+            out_shape=jax.ShapeDtypeStruct((rows, columns), bf16),
+            in_specs=[VMEM] * len(inputs),
+            out_specs=ANY,
+            scratch_shapes=[pltpu.VMEM((2, rows // 2, columns), bf16), pltpu.SemaphoreType.DMA((2,))],
+            compiler_params=pltpu.CompilerParams(vmem_limit_bytes=16 << 20),
+        )(*inputs)
 
 
 def solution(mesh):

time: 92.4 us -> 92.5 us (level)
    pallas_call x0 -> x1, Pallas kernels: none -> 1.17 us  [per_device(): pl.pallas_call(expand_kernel, out_shape=jax.ShapeDtypeStruct((rows, colum...]
    unnamed x21 -> x20, local copies, waits for them, and re-layouts: 7.79 us -> 7.04 us
    pallas_call x13 -> x12, Pallas kernels: 22.9 us -> 22.5 us  [kernel_call(): pl.pallas_call(kernel, out_shape=out_shape, in_specs=specs, out_specs=jax...]
where the time goes in v6:
time: 92.5 us; the launch traced here: 92.1 us
  starting transfers between devices  41.2 us (45%)
  Pallas kernels  23.7 us (26%)
  waiting for transfers between devices  16.8 us (18%)
  local copies, waits for them, and re-layouts  8.03 us (9%)
  other arithmetic  1.98 us (2%)
    ppermute x29, starting transfers between devices, send(): return lax.ppermute(value, ('adapter', 'tensor'), pairs)  41.2 us
    pallas_call x12, Pallas kernels, kernel_call(): pl.pallas_call(kernel, out_shape=out_shape, in_specs=specs, out_specs=jax...  22.5 us
    ppermute x29, waiting for transfers between devices, send(): return lax.ppermute(value, ('adapter', 'tensor'), pairs)  16.8 us
    unnamed x20, local copies, waits for them, and re-layouts  7.04 us
  transfers between devices with their start and end apart: 29, of which 6 were waited for; matrix products, arithmetic and copies ran while one was open for 3% of the time, Pallas kernels for 24%

profile of v6, /device:TPU:1, one launch (start us, length us, event | category | flops | bytes accessed | tf_op | source)
XLA Modules:
  0.0 92.1 jit_solution(8418706183315854977)
XLA Ops:
  0.0 3.2 %collective-permute-start.1 = (bf16[24,64,256]{2,1,0:T(8,128)(2,1)}, bf16[24,64,256]{2,1,0:T(8,128)(2,1)S(1)}, u32[]{:S(2)}, u32[]{:S(2)}) collective-permute-start(bf16[24,64,256]{2,1,0:T(8,128)(2,1)} %refs_0_.1), channel_id=1, source_target_pairs={{0,1},{1,0},{2,3},{3,2},{4,5},{5,4},{6,7},{7,6},{8,9},{9,8},{10,11... | collective-permute-start | bytes 2359304 | tf_op jit(solution)/shard_map/ppermute | solution.py:59
  4.0 1.6 %shard_map.73 = (bf16[24,64,256]{2,1,0:T(8,128)(2,1)S(1)}, bf16[24,64,256]{2,1,0:T(8,128)(2,1)S(1)}, bf16[768,256]{1,0:T(8,128)(2,1)S(1)}) custom-call(bf16[24,64,256]{2,1,0:T(8,128)(2,1)} %refs_0_.1, bf16[24,64,256]{2,1,0:T(8,128)(2,1)} %refs_1_.1, bf16[768,256]{1,0:T(8,128)(2,1)} %refs_2_.1), custom_call_target="tpu_custom_call" | custom-call | tf_op jit(solution)/shard_map/pallas_call | solution.py:29
  7.9 2.7 %collective-permute-start.3 = (bf16[384,512]{1,0:T(8,128)(2,1)S(1)}, bf16[384,512]{1,0:T(8,128)(2,1)S(1)}, u32[]{:S(2)}, u32[]{:S(2)}) collective-permute-start(bf16[384,512]{1,0:T(8,128)(2,1)S(1)} %get-tuple-element.49), channel_id=1, source_target_pairs={{0,6},{1,25},{2,0},{3,27},{4,2},{5,29},{6,4},{7,31},{8,14},{9,1},{... | collective-permute-start | bytes 1179656 | tf_op jit(solution)/shard_map/ppermute | solution.py:59
  10.6 3.9 %collective-permute-start.5 = (bf16[8,64,256]{2,1,0:T(8,128)(2,1)S(1)}, bf16[8,64,256]{2,1,0:T(8,128)(2,1)S(1)}, u32[]{:S(2)}, u32[]{:S(2)}) collective-permute-start(bf16[8,64,256]{2,1,0:T(8,128)(2,1)S(1)} %shard_map.74), channel_id=1, source_target_pairs={{0,32},{1,225},{2,34},{3,227},{4,36},{5,229},{6,38},{7,231},{8,40}... | collective-permute-start | bytes 786440 | tf_op jit(solution)/shard_map/ppermute | solution.py:59
  14.5 3.3 %collective-permute-done.5.refs_0_ = bf16[8,64,256]{2,1,0:T(8,128)(2,1)S(1)} collective-permute-done((bf16[8,64,256]{2,1,0:T(8,128)(2,1)S(1)}, bf16[8,64,256]{2,1,0:T(8,128)(2,1)S(1)}, u32[]{:S(2)}, u32[]{:S(2)}) %collective-permute-start.5) | collective-permute-done | bytes 262176 | tf_op jit(solution)/shard_map/ppermute | solution.py:59
  18.5 3.2 %collective-permute-start.9 = (bf16[24,64,256]{2,1,0:T(8,128)(2,1)S(1)}, bf16[24,64,256]{2,1,0:T(8,128)(2,1)S(1)}, u32[]{:S(2)}, u32[]{:S(2)}) collective-permute-start(bf16[24,64,256]{2,1,0:T(8,128)(2,1)S(1)} %shard_map.76), channel_id=1, source_target_pairs={{0,32},{1,225},{2,34},{3,227},{4,36},{5,229},{6,38},{7,231},{8,40}... | collective-permute-start | bytes 2359304 | tf_op jit(solution)/shard_map/ppermute | solution.py:59
  22.1 1.3 %collective-permute-start.6 = (bf16[2,384,512]{2,1,0:T(8,128)(2,1)S(1)}, bf16[2,384,512]{2,1,0:T(8,128)(2,1)}, u32[]{:S(2)}, u32[]{:S(2)}) collective-permute-start(bf16[2,384,512]{2,1,0:T(8,128)(2,1)S(1)} %pad_maximum_fusion.refs_0_), channel_id=1, source_target_pairs={{0,8},{1,3},{2,10},{3,5},{4,12},{5,7},{6,14},{7,1},{8,16},{9,11},{... | collective-permute-start | bytes 2359304 | tf_op jit(solution)/shard_map/ppermute | solution.py:59
  23.4 1.5 %collective-permute-start.7 = (bf16[2,384,512]{2,1,0:T(8,128)(2,1)S(1)}, bf16[2,384,512]{2,1,0:T(8,128)(2,1)S(1)}, u32[]{:S(2)}, u32[]{:S(2)}) collective-permute-start(bf16[2,384,512]{2,1,0:T(8,128)(2,1)S(1)} %pad_maximum_fusion.refs_0_), channel_id=1, source_target_pairs={{0,24},{1,7},{2,26},{3,1},{4,28},{5,3},{6,30},{7,5},{8,0},{9,15},{... | collective-permute-start | bytes 2359304 | tf_op jit(solution)/shard_map/ppermute | solution.py:59
  25.8 8.3 %collective-permute-done.8 = bf16[384,512]{1,0:T(8,128)(2,1)S(1)} collective-permute-done((bf16[384,512]{1,0:T(8,128)(2,1)S(1)}, bf16[384,512]{1,0:T(8,128)(2,1)S(1)}, u32[]{:S(2)}, u32[]{:S(2)}) %collective-permute-start.8) | collective-permute-done | bytes 393248 | tf_op jit(solution)/shard_map/ppermute | solution.py:59
  34.1 1.7 %shard_map.77 = bf16[32,64,256]{2,1,0:T(8,128)(2,1)} custom-call(s32[256]{0:T(256)S(1)} %pad_add_fusion.table_ref, bf16[24,64,256]{2,1,0:T(8,128)(2,1)S(1)} %collective-permute-done.9.refs_0_, bf16[24,64,256]{2,1,0:T(8,128)(2,1)S(1)} %get-tuple-element.47.refs_0_.refs_1_.mine_ref, bf16[24,64,256]{2,1,0:T(8,128)(2,1)S(1)} %collective-permute-done.1.refs_1_.refs_2_.sib_ref, ...), custom_call_target="tpu_custom_call" | custom-call | tf_op jit(solution)/shard_map/pallas_call | solution.py:29
  35.9 2.1 %collective-permute-done.6.refs_1_ = bf16[2,384,512]{2,1,0:T(8,128)(2,1)} collective-permute-done((bf16[2,384,512]{2,1,0:T(8,128)(2,1)S(1)}, bf16[2,384,512]{2,1,0:T(8,128)(2,1)}, u32[]{:S(2)}, u32[]{:S(2)}) %collective-permute-start.6) | collective-permute-done | bytes 786464 | tf_op jit(solution)/shard_map/ppermute | solution.py:59
  40.0 2.7 %collective-permute-start.14 = (bf16[2,384,512]{2,1,0:T(8,128)(2,1)}, bf16[2,384,512]{2,1,0:T(8,128)(2,1)}, u32[]{:S(2)}, u32[]{:S(2)}) collective-permute-start(bf16[2,384,512]{2,1,0:T(8,128)(2,1)} %pad_maximum_fusion.1.refs_1_), channel_id=1, source_target_pairs={{0,24},{1,7},{2,26},{3,1},{4,28},{5,3},{6,30},{7,5},{8,0},{9,15},{... | collective-permute-start | bytes 2359304 | tf_op jit(solution)/shard_map/ppermute | solution.py:59
  45.0 4.2 %shard_map.78.refs_0_ = f32[2,384,256]{2,1,0:T(8,128)S(1)} custom-call(s32[6]{0:T(128)S(1)} %stack.81.block_ref, bf16[2,384,512]{2,1,0:T(8,128)(2,1)S(1)} %copy-done.5, bf16[2,384,512]{2,1,0:T(8,128)(2,1)} %collective-permute-done.6.refs_1_, bf16[2,384,512]{2,1,0:T(8,128)(2,1)S(1)} %copy-done.7, bf16[16,512,256]{2,1,0:T(8,128)(2,1)} %bitcast.10.refs_3_.refs_4_, ...), custom_call_target="tpu_custom_call" | custom-call | tf_op jit(solution)/shard_map/pallas_call | solution.py:29
  50.1 2.4 %shard_map.79 = (bf16[16,64,256]{2,1,0:T(8,128)(2,1)}, bf16[16,64,256]{2,1,0:T(8,128)(2,1)}) custom-call(s32[256]{0:T(256)S(1)} %pad_add_fusion.table_ref, bf16[32,64,256]{2,1,0:T(8,128)(2,1)} %collective-permute-done.11.refs_0_, bf16[24,64,256]{2,1,0:T(8,128)(2,1)S(1)} %get-tuple-element.47.refs_0_.refs_1_.mine_ref, ...), custom_call_target="tpu_custom_call" | custom-call | tf_op jit(solution)/shard_map/pallas_call | solution.py:29
  52.5 1.3 %collective-permute-start.12 = (bf16[16,64,256]{2,1,0:T(8,128)(2,1)}, bf16[16,64,256]{2,1,0:T(8,128)(2,1)}, u32[]{:S(2)}, u32[]{:S(2)}) collective-permute-start(bf16[16,64,256]{2,1,0:T(8,128)(2,1)} %get-tuple-element.65), channel_id=1, source_target_pairs={{0,32},{1,225},{2,34},{3,227},{4,36},{5,229},{6,38},{7,231},{8,40}... | collective-permute-start | bytes 1572872 | tf_op jit(solution)/shard_map/ppermute | solution.py:59
  53.8 1.2 %collective-permute-start.16 = (bf16[2,384,512]{2,1,0:T(8,128)(2,1)}, bf16[2,384,512]{2,1,0:T(8,128)(2,1)}, u32[]{:S(2)}, u32[]{:S(2)}) collective-permute-start(bf16[2,384,512]{2,1,0:T(8,128)(2,1)} %collective-permute-done.6.refs_1_), channel_id=1, source_target_pairs={{0,8},{1,3},{2,10},{3,5},{4,12},{5,7},{6,14},{7,1},{8,16},{9,11},{... | collective-permute-start | bytes 2359304 | tf_op jit(solution)/shard_map/ppermute | solution.py:59
  55.0 1.6 %collective-permute-start.22 = (bf16[2,384,512]{2,1,0:T(8,128)(2,1)}, bf16[2,384,512]{2,1,0:T(8,128)(2,1)}, u32[]{:S(2)}, u32[]{:S(2)}) collective-permute-start(bf16[2,384,512]{2,1,0:T(8,128)(2,1)} %collective-permute-done.14.refs_3_), channel_id=1, source_target_pairs={{0,24},{1,7},{2,26},{3,1},{4,28},{5,3},{6,30},{7,5},{8,0},{9,15},{... | collective-permute-start | bytes 2359304 | tf_op jit(solution)/shard_map/ppermute | solution.py:59
  57.9 4.1 %shard_map.80.refs_0_ = f32[2,384,256]{2,1,0:T(8,128)S(1)} custom-call(s32[6]{0:T(128)S(1)} %stack.94.block_ref, f32[2,384,256]{2,1,0:T(8,128)S(1)} %copy-done.1, bf16[2,384,512]{2,1,0:T(8,128)(2,1)} %pad_maximum_fusion.1.refs_1_, bf16[2,384,512]{2,1,0:T(8,128)(2,1)} %collective-permute-done.13.refs_2_, ...), custom_call_target="tpu_custom_call" | custom-call | tf_op jit(solution)/shard_map/pallas_call | solution.py:29
  62.9 2.3 %collective-permute-start.15 = (bf16[16,64,256]{2,1,0:T(8,128)(2,1)}, bf16[16,64,256]{2,1,0:T(8,128)(2,1)}, u32[]{:S(2)}, u32[]{:S(2)}) collective-permute-start(bf16[16,64,256]{2,1,0:T(8,128)(2,1)} %collective-permute-done.12.here_ref), channel_id=1, source_target_pairs={{0,1},{1,0},{2,3},{3,2},{4,5},{5,4},{6,7},{7,6},{8,9},{9,8},{10,11... | collective-permute-start | bytes 1572872 | tf_op jit(solution)/shard_map/shrink/ppermute | solution.py:59
  65.2 1.8 %collective-permute-start.17 = (bf16[16,64,256]{2,1,0:T(8,128)(2,1)}, bf16[16,64,256]{2,1,0:T(8,128)(2,1)}, u32[]{:S(2)}, u32[]{:S(2)}) collective-permute-start(bf16[16,64,256]{2,1,0:T(8,128)(2,1)} %get-tuple-element.72), channel_id=1, source_target_pairs={{0,32},{1,225},{2,34},{3,227},{4,36},{5,229},{6,38},{7,231},{8,40}... | collective-permute-start | bytes 1572872 | tf_op jit(solution)/shard_map/ppermute | solution.py:59
  67.1 1.7 %shrink.1 = f32[64,384]{1,0:T(8,128)S(1)} custom-call(s32[256]{0:T(256)S(1)} %pad_add_fusion.table_ref, bf16[16,64,256]{2,1,0:T(8,128)(2,1)} %collective-permute-done.12.here_ref, bf16[16,64,256]{2,1,0:T(8,128)(2,1)} %collective-permute-done.15.other_ref, bf16[24,64,256]{2,1,0:T(8,128)(2,1)S(1)} %get-tuple-element.47.refs_0_.refs_1_.mine_ref, ...), custom_call_target="tpu_custom_call" | custom-call | tf_op jit(solution)/shard_map/shrink/pallas_call | solution.py:29
  69.4 2.2 %collective-permute-start.20 = (f32[64,384]{1,0:T(8,128)S(1)}, f32[64,384]{1,0:T(8,128)S(1)}, u32[]{:S(2)}, u32[]{:S(2)}) collective-permute-start(f32[64,384]{1,0:T(8,128)S(1)} %shrink.1), channel_id=1, source_target_pairs={{0,6},{1,7},{2,0},{3,1},{4,2},{5,3},{6,4},{7,5},{8,14},{9,15},{10,... | collective-permute-start | bytes 294920 | tf_op jit(solution)/shard_map/shrink_sum/ppermute | solution.py:59
  72.2 1.6 %collective-permute-done.17.refs_0_ = bf16[16,64,256]{2,1,0:T(8,128)(2,1)} collective-permute-done((bf16[16,64,256]{2,1,0:T(8,128)(2,1)}, bf16[16,64,256]{2,1,0:T(8,128)(2,1)}, u32[]{:S(2)}, u32[]{:S(2)}) %collective-permute-start.17) | collective-permute-done | bytes 524320 | tf_op jit(solution)/shard_map/ppermute | solution.py:59
  73.9 1.1 %shard_map.81 = (bf16[8,64,256]{2,1,0:T(8,128)(2,1)S(1)}, bf16[8,64,256]{2,1,0:T(8,128)(2,1)S(1)}) custom-call(s32[256]{0:T(256)S(1)} %pad_add_fusion.table_ref, bf16[16,64,256]{2,1,0:T(8,128)(2,1)} %collective-permute-done.17.refs_0_, bf16[24,64,256]{2,1,0:T(8,128)(2,1)S(1)} %get-tuple-element.47.refs_0_.refs_1_.mine_ref, ...), custom_call_target="tpu_custom_call" | custom-call | tf_op jit(solution)/shard_map/pallas_call | solution.py:29
  75.0 2.9 %collective-permute-start.18 = (bf16[8,64,256]{2,1,0:T(8,128)(2,1)S(1)}, bf16[8,64,256]{2,1,0:T(8,128)(2,1)S(1)}, u32[]{:S(2)}, u32[]{:S(2)}) collective-permute-start(bf16[8,64,256]{2,1,0:T(8,128)(2,1)S(1)} %get-tuple-element.74), channel_id=1, source_target_pairs={{0,32},{1,225},{2,34},{3,227},{4,36},{5,229},{6,38},{7,231},{8,40}... | collective-permute-start | bytes 786440 | tf_op jit(solution)/shard_map/ppermute | solution.py:59
  77.9 2.1 %collective-permute-start.23 = (bf16[8,64,256]{2,1,0:T(8,128)(2,1)S(1)}, bf16[8,64,256]{2,1,0:T(8,128)(2,1)S(1)}, u32[]{:S(2)}, u32[]{:S(2)}) collective-permute-start(bf16[8,64,256]{2,1,0:T(8,128)(2,1)S(1)} %get-tuple-element.80), channel_id=1, source_target_pairs={{0,33},{1,224},{2,35},{3,226},{4,37},{5,228},{6,39},{7,230},{8,41}... | collective-permute-start | bytes 786440 | tf_op jit(solution)/shard_map/ppermute | solution.py:59
  80.1 1.4 %collective-permute-start.24 = (f32[64,384]{1,0:T(8,128)S(1)}, f32[64,384]{1,0:T(8,128)S(1)}, u32[]{:S(2)}, u32[]{:S(2)}) collective-permute-start(f32[64,384]{1,0:T(8,128)S(1)} %add_add_fusion), channel_id=1, source_target_pairs={{0,8},{1,9},{2,10},{3,11},{4,12},{5,13},{6,14},{7,15},{8,16},{9,17... | collective-permute-start | bytes 294920 | tf_op jit(solution)/shard_map/shrink_sum/ppermute | solution.py:59
  81.5 1.5 %collective-permute-start.25 = (f32[64,384]{1,0:T(8,128)S(1)}, f32[64,384]{1,0:T(8,128)S(1)}, u32[]{:S(2)}, u32[]{:S(2)}) collective-permute-start(f32[64,384]{1,0:T(8,128)S(1)} %add_add_fusion), channel_id=1, source_target_pairs={{0,24},{1,25},{2,26},{3,27},{4,28},{5,29},{6,30},{7,31},{8,0},{9,1... | collective-permute-start | bytes 294920 | tf_op jit(solution)/shard_map/shrink_sum/ppermute | solution.py:59
  83.0 1.6 %collective-permute-start.26 = (f32[64,384]{1,0:T(8,128)S(1)}, f32[64,384]{1,0:T(8,128)S(1)}, u32[]{:S(2)}, u32[]{:S(2)}) collective-permute-start(f32[64,384]{1,0:T(8,128)S(1)} %add_add_fusion), channel_id=1, source_target_pairs={{0,16},{1,17},{2,18},{3,19},{4,20},{5,21},{6,22},{7,23},{8,24},{9,... | collective-permute-start | bytes 294920 | tf_op jit(solution)/shard_map/shrink_sum/ppermute | solution.py:59
  84.5 3.3 %shard_map.82 = f32[2,384,256]{2,1,0:T(8,128)S(1)} custom-call(s32[4]{0:T(128)S(1)} %pad_add_fusion.1.block_ref, f32[2,384,256]{2,1,0:T(8,128)S(1)} %copy-done.3, bf16[2,384,512]{2,1,0:T(8,128)(2,1)} %collective-permute-done.16.refs_1_, bf16[2,384,512]{2,1,0:T(8,128)(2,1)} %collective-permute-done.22.refs_2_, bf16[16,512,256]{2,1,0:T(8,128)(2,1)} %bitcast.10.refs_3_.refs_4_, ...), custom_call_target="tpu_custom_call" | custom-call | tf_op jit(solution)/shard_map/pallas_call | solution.py:29
  89.5 1.3 %collective-permute-done.27.other_ref = bf16[64,384]{1,0:T(8,128)(2,1)S(1)} collective-permute-done((bf16[64,384]{1,0:T(8,128)(2,1)S(1)}, bf16[64,384]{1,0:T(8,128)(2,1)S(1)}, u32[]{:S(2)}, u32[]{:S(2)}) %collective-permute-start.27) | collective-permute-done | bytes 49184 | tf_op jit(solution)/shard_map/shrink_sum/ppermute | solution.py:59
  90.8 1.2 %expand.1 = bf16[768,256]{1,0:T(8,128)(2,1)} custom-call(bf16[8,64,256]{2,1,0:T(8,128)(2,1)S(1)} %shard_map.83.panels_ref, bf16[64,384]{1,0:T(8,128)(2,1)S(1)} %multiply_convert_fusion.scaled_ref, bf16[64,384]{1,0:T(8,128)(2,1)S(1)} %collective-permute-done.27.other_ref, s32[1,768]{1,0:T(1,128)S(1)} %reshape.19.slot_ref, ...), custom_call_target="tpu_custom_call" | custom-call | tf_op jit(solution)/shard_map/expand/pallas_call | solution.py:387
  (70 shorter events, 15.4 us)
Async XLA Ops:
  0.0 6.3 %collective-permute-start.1 = (bf16[24,64,256]{2,1,0:T(8,128)(2,1)}, bf16[24,64,256]{2,1,0:T(8,128)(2,1)S(1)}, u32[]{:S(2)}, u32[]{:S(2)}) collective-permute-start(bf16[24,64,256]{2,1,0:T(8,128)(2,1)} %refs_0_.1), channel_id=1, source_target_pairs={{0,1},{1,0},{2,3},{3,2},{4,5},{5,4},{6,7},{7,6},{8,9},{9,8},{10,11... | collective-permute-start | bytes 2359304 | tf_op jit(solution)/shard_map/ppermute | solution.py:59
  3.2 3.7 %collective-permute-start = (bf16[768,256]{1,0:T(8,128)(2,1)}, bf16[768,256]{1,0:T(8,128)(2,1)S(1)}, u32[]{:S(2)}, u32[]{:S(2)}) collective-permute-start(bf16[768,256]{1,0:T(8,128)(2,1)} %refs_2_.1), channel_id=1, source_target_pairs={{0,1},{1,0},{2,3},{3,2},{4,5},{5,4},{6,7},{7,6},{8,9},{9,8},{10,11... | collective-permute-start | bytes 1179656 | tf_op jit(solution)/shard_map/ppermute | solution.py:59
  4.0 3.8 %copy-start.8 = (bf16[24,64,256]{2,1,0:T(8,128)(2,1)S(1)}, bf16[24,64,256]{2,1,0:T(8,128)(2,1)}, u32[]{:S(2)}) copy-start(bf16[24,64,256]{2,1,0:T(8,128)(2,1)} %refs_1_.1) | copy-start | bytes 2359300
  7.2 35.5 %collective-permute-start.10 = (bf16[8192,256]{1,0:T(8,128)(2,1)}, bf16[8192,256]{1,0:T(8,128)(2,1)}, u32[]{:S(2)}, u32[]{:S(2)}) collective-permute-start(bf16[8192,256]{1,0:T(8,128)(2,1)} %param.8), channel_id=1, source_target_pairs={{0,1},{1,0},{2,3},{3,2},{4,5},{5,4},{6,7},{7,6},{8,9},{9,8},{10,11... | collective-permute-start | bytes 12582920 | tf_op jit(solution)/shard_map/ppermute | solution.py:59
  7.8 10.0 %collective-permute-start.4 = (bf16[24,64,256]{2,1,0:T(8,128)(2,1)S(1)}, bf16[24,64,256]{2,1,0:T(8,128)(2,1)S(1)}, u32[]{:S(2)}, u32[]{:S(2)}) collective-permute-start(bf16[24,64,256]{2,1,0:T(8,128)(2,1)S(1)} %copy-done.8), channel_id=1, source_target_pairs={{0,1},{1,0},{2,3},{3,2},{4,5},{5,4},{6,7},{7,6},{8,9},{9,8},{10,11... | collective-permute-start | bytes 2359304 | tf_op jit(solution)/shard_map/ppermute | solution.py:59
  7.9 9.9 %collective-permute-start.2 = (bf16[384,512]{1,0:T(8,128)(2,1)S(1)}, bf16[384,512]{1,0:T(8,128)(2,1)S(1)}, u32[]{:S(2)}, u32[]{:S(2)}) collective-permute-start(bf16[384,512]{1,0:T(8,128)(2,1)S(1)} %get-tuple-element.49), channel_id=1, source_target_pairs={{0,2},{1,9},{2,4},{3,11},{4,6},{5,13},{6,0},{7,15},{8,10},{9,17},{... | collective-permute-start | bytes 1179656 | tf_op jit(solution)/shard_map/ppermute | solution.py:59
  7.9 9.9 %collective-permute-start.3 = (bf16[384,512]{1,0:T(8,128)(2,1)S(1)}, bf16[384,512]{1,0:T(8,128)(2,1)S(1)}, u32[]{:S(2)}, u32[]{:S(2)}) collective-permute-start(bf16[384,512]{1,0:T(8,128)(2,1)S(1)} %get-tuple-element.49), channel_id=1, source_target_pairs={{0,6},{1,25},{2,0},{3,27},{4,2},{5,29},{6,4},{7,31},{8,14},{9,1},{... | collective-permute-start | bytes 1179656 | tf_op jit(solution)/shard_map/ppermute | solution.py:59
  10.6 7.2 %collective-permute-start.5 = (bf16[8,64,256]{2,1,0:T(8,128)(2,1)S(1)}, bf16[8,64,256]{2,1,0:T(8,128)(2,1)S(1)}, u32[]{:S(2)}, u32[]{:S(2)}) collective-permute-start(bf16[8,64,256]{2,1,0:T(8,128)(2,1)S(1)} %shard_map.74), channel_id=1, source_target_pairs={{0,32},{1,225},{2,34},{3,227},{4,36},{5,229},{6,38},{7,231},{8,40}... | collective-permute-start | bytes 786440 | tf_op jit(solution)/shard_map/ppermute | solution.py:59
  18.5 15.6 %collective-permute-start.9 = (bf16[24,64,256]{2,1,0:T(8,128)(2,1)S(1)}, bf16[24,64,256]{2,1,0:T(8,128)(2,1)S(1)}, u32[]{:S(2)}, u32[]{:S(2)}) collective-permute-start(bf16[24,64,256]{2,1,0:T(8,128)(2,1)S(1)} %shard_map.76), channel_id=1, source_target_pairs={{0,32},{1,225},{2,34},{3,227},{4,36},{5,229},{6,38},{7,231},{8,40}... | collective-permute-start | bytes 2359304 | tf_op jit(solution)/shard_map/ppermute | solution.py:59
  21.7 12.4 %collective-permute-start.8 = (bf16[384,512]{1,0:T(8,128)(2,1)S(1)}, bf16[384,512]{1,0:T(8,128)(2,1)S(1)}, u32[]{:S(2)}, u32[]{:S(2)}) collective-permute-start(bf16[384,512]{1,0:T(8,128)(2,1)S(1)} %collective-permute-done.2), channel_id=1, source_target_pairs={{0,2},{1,9},{2,4},{3,11},{4,6},{5,13},{6,0},{7,15},{8,10},{9,17},{... | collective-permute-start | bytes 1179656 | tf_op jit(solution)/shard_map/ppermute | solution.py:59
  22.1 15.9 %collective-permute-start.6 = (bf16[2,384,512]{2,1,0:T(8,128)(2,1)S(1)}, bf16[2,384,512]{2,1,0:T(8,128)(2,1)}, u32[]{:S(2)}, u32[]{:S(2)}) collective-permute-start(bf16[2,384,512]{2,1,0:T(8,128)(2,1)S(1)} %pad_maximum_fusion.refs_0_), channel_id=1, source_target_pairs={{0,8},{1,3},{2,10},{3,5},{4,12},{5,7},{6,14},{7,1},{8,16},{9,11},{... | collective-permute-start | bytes 2359304 | tf_op jit(solution)/shard_map/ppermute | solution.py:59
  23.4 14.6 %collective-permute-start.7 = (bf16[2,384,512]{2,1,0:T(8,128)(2,1)S(1)}, bf16[2,384,512]{2,1,0:T(8,128)(2,1)S(1)}, u32[]{:S(2)}, u32[]{:S(2)}) collective-permute-start(bf16[2,384,512]{2,1,0:T(8,128)(2,1)S(1)} %pad_maximum_fusion.refs_0_), channel_id=1, source_target_pairs={{0,24},{1,7},{2,26},{3,1},{4,28},{5,3},{6,30},{7,5},{8,0},{9,15},{... | collective-permute-start | bytes 2359304 | tf_op jit(solution)/shard_map/ppermute | solution.py:59
  35.8 14.3 %collective-permute-start.11 = (bf16[32,64,256]{2,1,0:T(8,128)(2,1)}, bf16[32,64,256]{2,1,0:T(8,128)(2,1)}, u32[]{:S(2)}, u32[]{:S(2)}) collective-permute-start(bf16[32,64,256]{2,1,0:T(8,128)(2,1)} %shard_map.77), channel_id=1, source_target_pairs={{0,32},{1,225},{2,34},{3,227},{4,36},{5,229},{6,38},{7,231},{8,40}... | collective-permute-start | bytes 3145736 | tf_op jit(solution)/shard_map/ppermute | solution.py:59
  39.9 15.0 %collective-permute-start.13 = (bf16[2,384,512]{2,1,0:T(8,128)(2,1)}, bf16[2,384,512]{2,1,0:T(8,128)(2,1)}, u32[]{:S(2)}, u32[]{:S(2)}) collective-permute-start(bf16[2,384,512]{2,1,0:T(8,128)(2,1)} %pad_maximum_fusion.1.refs_1_), channel_id=1, source_target_pairs={{0,8},{1,3},{2,10},{3,5},{4,12},{5,7},{6,14},{7,1},{8,16},{9,11},{... | collective-permute-start | bytes 2359304 | tf_op jit(solution)/shard_map/ppermute | solution.py:59
  40.0 15.0 %collective-permute-start.14 = (bf16[2,384,512]{2,1,0:T(8,128)(2,1)}, bf16[2,384,512]{2,1,0:T(8,128)(2,1)}, u32[]{:S(2)}, u32[]{:S(2)}) collective-permute-start(bf16[2,384,512]{2,1,0:T(8,128)(2,1)} %pad_maximum_fusion.1.refs_1_), channel_id=1, source_target_pairs={{0,24},{1,7},{2,26},{3,1},{4,28},{5,3},{6,30},{7,5},{8,0},{9,15},{... | collective-permute-start | bytes 2359304 | tf_op jit(solution)/shard_map/ppermute | solution.py:59
  52.5 10.4 %collective-permute-start.12 = (bf16[16,64,256]{2,1,0:T(8,128)(2,1)}, bf16[16,64,256]{2,1,0:T(8,128)(2,1)}, u32[]{:S(2)}, u32[]{:S(2)}) collective-permute-start(bf16[16,64,256]{2,1,0:T(8,128)(2,1)} %get-tuple-element.65), channel_id=1, source_target_pairs={{0,32},{1,225},{2,34},{3,227},{4,36},{5,229},{6,38},{7,231},{8,40}... | collective-permute-start | bytes 1572872 | tf_op jit(solution)/shard_map/ppermute | solution.py:59
  53.8 15.1 %collective-permute-start.16 = (bf16[2,384,512]{2,1,0:T(8,128)(2,1)}, bf16[2,384,512]{2,1,0:T(8,128)(2,1)}, u32[]{:S(2)}, u32[]{:S(2)}) collective-permute-start(bf16[2,384,512]{2,1,0:T(8,128)(2,1)} %collective-permute-done.6.refs_1_), channel_id=1, source_target_pairs={{0,8},{1,3},{2,10},{3,5},{4,12},{5,7},{6,14},{7,1},{8,16},{9,11},{... | collective-permute-start | bytes 2359304 | tf_op jit(solution)/shard_map/ppermute | solution.py:59
  55.0 22.9 %collective-permute-start.22 = (bf16[2,384,512]{2,1,0:T(8,128)(2,1)}, bf16[2,384,512]{2,1,0:T(8,128)(2,1)}, u32[]{:S(2)}, u32[]{:S(2)}) collective-permute-start(bf16[2,384,512]{2,1,0:T(8,128)(2,1)} %collective-permute-done.14.refs_3_), channel_id=1, source_target_pairs={{0,24},{1,7},{2,26},{3,1},{4,28},{5,3},{6,30},{7,5},{8,0},{9,15},{... | collective-permute-start | bytes 2359304 | tf_op jit(solution)/shard_map/ppermute | solution.py:59
  57.9 9.1 %copy-start.9 = (s32[768]{0:T(1024)S(1)}, s32[768]{0:T(1024)}, u32[]{:S(2)}) copy-start(s32[768]{0:T(1024)} %param.13) | copy-start | bytes 9220
  62.9 4.2 %collective-permute-start.15 = (bf16[16,64,256]{2,1,0:T(8,128)(2,1)}, bf16[16,64,256]{2,1,0:T(8,128)(2,1)}, u32[]{:S(2)}, u32[]{:S(2)}) collective-permute-start(bf16[16,64,256]{2,1,0:T(8,128)(2,1)} %collective-permute-done.12.here_ref), channel_id=1, source_target_pairs={{0,1},{1,0},{2,3},{3,2},{4,5},{5,4},{6,7},{7,6},{8,9},{9,8},{10,11... | collective-permute-start | bytes 1572872 | tf_op jit(solution)/shard_map/shrink/ppermute | solution.py:59
  65.2 8.6 %collective-permute-start.17 = (bf16[16,64,256]{2,1,0:T(8,128)(2,1)}, bf16[16,64,256]{2,1,0:T(8,128)(2,1)}, u32[]{:S(2)}, u32[]{:S(2)}) collective-permute-start(bf16[16,64,256]{2,1,0:T(8,128)(2,1)} %get-tuple-element.72), channel_id=1, source_target_pairs={{0,32},{1,225},{2,34},{3,227},{4,36},{5,229},{6,38},{7,231},{8,40}... | collective-permute-start | bytes 1572872 | tf_op jit(solution)/shard_map/ppermute | solution.py:59
  67.0 17.5 %copy-start.3 = (f32[2,384,256]{2,1,0:T(8,128)S(1)}, f32[2,384,256]{2,1,0:T(8,128)}, u32[]{:S(2)}) copy-start(f32[2,384,256]{2,1,0:T(8,128)} %copy-done.2) | copy-start | bytes 2359300
  68.8 11.2 %collective-permute-start.19 = (f32[64,384]{1,0:T(8,128)S(1)}, f32[64,384]{1,0:T(8,128)S(1)}, u32[]{:S(2)}, u32[]{:S(2)}) collective-permute-start(f32[64,384]{1,0:T(8,128)S(1)} %shrink.1), channel_id=1, source_target_pairs={{0,2},{1,3},{2,4},{3,5},{4,6},{5,7},{6,0},{7,1},{8,10},{9,11},{10,... | collective-permute-start | bytes 294920 | tf_op jit(solution)/shard_map/shrink_sum/ppermute | solution.py:59
  69.4 10.6 %collective-permute-start.20 = (f32[64,384]{1,0:T(8,128)S(1)}, f32[64,384]{1,0:T(8,128)S(1)}, u32[]{:S(2)}, u32[]{:S(2)}) collective-permute-start(f32[64,384]{1,0:T(8,128)S(1)} %shrink.1), channel_id=1, source_target_pairs={{0,6},{1,7},{2,0},{3,1},{4,2},{5,3},{6,4},{7,5},{8,14},{9,15},{10,... | collective-permute-start | bytes 294920 | tf_op jit(solution)/shard_map/shrink_sum/ppermute | solution.py:59
  71.6 8.4 %collective-permute-start.21 = (f32[64,384]{1,0:T(8,128)S(1)}, f32[64,384]{1,0:T(8,128)S(1)}, u32[]{:S(2)}, u32[]{:S(2)}) collective-permute-start(f32[64,384]{1,0:T(8,128)S(1)} %shrink.1), channel_id=1, source_target_pairs={{0,4},{1,5},{2,6},{3,7},{4,0},{5,1},{6,2},{7,3},{8,12},{9,13},{10,... | collective-permute-start | bytes 294920 | tf_op jit(solution)/shard_map/shrink_sum/ppermute | solution.py:59
  75.0 12.9 %collective-permute-start.18 = (bf16[8,64,256]{2,1,0:T(8,128)(2,1)S(1)}, bf16[8,64,256]{2,1,0:T(8,128)(2,1)S(1)}, u32[]{:S(2)}, u32[]{:S(2)}) collective-permute-start(bf16[8,64,256]{2,1,0:T(8,128)(2,1)S(1)} %get-tuple-element.74), channel_id=1, source_target_pairs={{0,32},{1,225},{2,34},{3,227},{4,36},{5,229},{6,38},{7,231},{8,40}... | collective-permute-start | bytes 786440 | tf_op jit(solution)/shard_map/ppermute | solution.py:59
  77.9 10.0 %collective-permute-start.23 = (bf16[8,64,256]{2,1,0:T(8,128)(2,1)S(1)}, bf16[8,64,256]{2,1,0:T(8,128)(2,1)S(1)}, u32[]{:S(2)}, u32[]{:S(2)}) collective-permute-start(bf16[8,64,256]{2,1,0:T(8,128)(2,1)S(1)} %get-tuple-element.80), channel_id=1, source_target_pairs={{0,33},{1,224},{2,35},{3,226},{4,37},{5,228},{6,39},{7,230},{8,41}... | collective-permute-start | bytes 786440 | tf_op jit(solution)/shard_map/ppermute | solution.py:59
  80.1 8.8 %collective-permute-start.24 = (f32[64,384]{1,0:T(8,128)S(1)}, f32[64,384]{1,0:T(8,128)S(1)}, u32[]{:S(2)}, u32[]{:S(2)}) collective-permute-start(f32[64,384]{1,0:T(8,128)S(1)} %add_add_fusion), channel_id=1, source_target_pairs={{0,8},{1,9},{2,10},{3,11},{4,12},{5,13},{6,14},{7,15},{8,16},{9,17... | collective-permute-start | bytes 294920 | tf_op jit(solution)/shard_map/shrink_sum/ppermute | solution.py:59
  81.5 7.4 %collective-permute-start.25 = (f32[64,384]{1,0:T(8,128)S(1)}, f32[64,384]{1,0:T(8,128)S(1)}, u32[]{:S(2)}, u32[]{:S(2)}) collective-permute-start(f32[64,384]{1,0:T(8,128)S(1)} %add_add_fusion), channel_id=1, source_target_pairs={{0,24},{1,25},{2,26},{3,27},{4,28},{5,29},{6,30},{7,31},{8,0},{9,1... | collective-permute-start | bytes 294920 | tf_op jit(solution)/shard_map/shrink_sum/ppermute | solution.py:59
  83.0 5.9 %collective-permute-start.26 = (f32[64,384]{1,0:T(8,128)S(1)}, f32[64,384]{1,0:T(8,128)S(1)}, u32[]{:S(2)}, u32[]{:S(2)}) collective-permute-start(f32[64,384]{1,0:T(8,128)S(1)} %add_add_fusion), channel_id=1, source_target_pairs={{0,16},{1,17},{2,18},{3,19},{4,20},{5,21},{6,22},{7,23},{8,24},{9,... | collective-permute-start | bytes 294920 | tf_op jit(solution)/shard_map/shrink_sum/ppermute | solution.py:59
  88.9 1.9 %collective-permute-start.28 = (f32[384,256]{1,0:T(8,128)S(1)}, f32[384,256]{1,0:T(8,128)S(1)}, u32[]{:S(2)}, u32[]{:S(2)}) collective-permute-start(f32[384,256]{1,0:T(8,128)S(1)} %get-tuple-element.84), channel_id=1, source_target_pairs={{0,1},{1,0},{2,3},{3,2},{4,5},{5,4},{6,7},{7,6},{8,9},{9,8},{10,11... | collective-permute-start | bytes 1179656 | tf_op jit(solution)/shard_map/base/ppermute | solution.py:59
  89.0 1.8 %collective-permute-start.27 = (bf16[64,384]{1,0:T(8,128)(2,1)S(1)}, bf16[64,384]{1,0:T(8,128)(2,1)S(1)}, u32[]{:S(2)}, u32[]{:S(2)}) collective-permute-start(bf16[64,384]{1,0:T(8,128)(2,1)S(1)} %multiply_convert_fusion.scaled_ref), channel_id=1, source_target_pairs={{0,1},{1,0},{2,3},{3,2},{4,5},{5,4},{6,7},{7,6},{8,9},{9,8},{10,11... | collective-permute-start | bytes 147464 | tf_op jit(solution)/shard_map/shrink_sum/ppermute | solution.py:59
  (7 other events, 7.1 us)
